TPU v7x, 512 devices: a whole 4x8x8 slice. The times are simulated.
512 devices in a mesh: seq: 64 (over x, y, core), section: 8 (over z).
Axes of the slice: x: 4, y: 8, z: 8, core: 2. Of those that a mesh axis runs over, the one named last changes fastest.
Arguments:
- encoded: bfloat16 [8, 4096, 1408], P(None, 'seq'), may hold values from -6 to 6
- conv_weight: bfloat16 [8, 4224, 1408], P('section', 'seq'), may hold values from -0.09375 to 0.09375
- section_gain: float32 [8, 1408], P('section'), may hold values from 0.4 to 1.6
- head_gain: float32 [1408], replicated, may hold values from 0.4 to 1.6
- head_weight: bfloat16 [1408, 1408], P('seq'), may hold values from -0.15625 to 0.15625
- pair_donor: int32 [8, 64, 64], P('section', 'seq'), may hold values from 0 to 63
- pair_acceptor: int32 [8, 64, 64], P('section', 'seq'), may hold values from 0 to 63
- pair_count: int32 [8, 64, 4], P('section', 'seq'), may hold values from 0 to 16, as said below
- pair_cotangent: float32 [8, 64, 64], P('section', 'seq'), may hold values from -48 to 48
Outputs:
- stash: bfloat16 [8, 8, 4096, 1408], P('section', None, 'seq')
- junction_grad: float32 [8, 4096, 1408], P('section', 'seq')
Inputs may be any that keep to these rules, and one draw needn't show every extreme that they name: pair_count[m, i, o] is 0 where i + o >= 64; in every micro-batch some slab holds exactly 16 live slots for some reach o >= 1.
All inputs are finite; a program needn't handle non-finite values.
Results may differ from a plain program's by a relative error of at most 0.013.
Values may be sent and summed in bfloat16 or wider, within the bound.
No kernel may reach another device: no remote copies, remote signals or barrier semaphores. Data moves between devices by JAX's collectives and lax.ppermute only.
A program may use at most 128 MiB of HBM per device.

v0:
```python
import jax
import jax.numpy as jnp
from jax import lax
from jax.sharding import PartitionSpec as P


def padded(cells, sides, width):
    for axis, dim in sides:
        count = lax.axis_size(axis)
        ends = count - 1
        head = lax.slice_in_dim(cells, 0, width, axis=dim)
        tail = lax.slice_in_dim(cells, cells.shape[dim] - width, cells.shape[dim], axis=dim)
        cells = jnp.concatenate(
            [
                lax.ppermute(tail, axis, [(i, (i + 1) % count) for i in range(ends)]),
                cells,
                lax.ppermute(head, axis, [((i + 1) % count, i) for i in range(ends)]),
            ],
            axis=dim,
        )
    return cells


def from_behind(shard, axis, by):
    size = lax.axis_size(axis)
    pairs = [(i, i + by) for i in range(size) if 0 <= i + by < size]
    return lax.ppermute(shard, axis, pairs)


def broadcast(block, axis, holder):
    block = jnp.where(lax.axis_index(axis) == holder, block, jnp.zeros_like(block))
    return lax.psum(block, axis)


def rms_scaled(values, gains):
    return values * lax.rsqrt(jnp.mean(values * values, axis=-1, keepdims=True) + 1e-06) * gains


def on_device(
    encoded,
    conv_weight,
    section_gain,
    head_gain,
    head_weight,
    pair_donor,
    pair_acceptor,
    pair_count,
    pair_cotangent,
):
    micro_count, slab_rows, channels = encoded.shape
    sections = lax.axis_size("section")
    section_pos = lax.axis_index("section")
    dilation = slab_rows // 2
    weights = lax.all_gather(conv_weight[0], "seq", axis=0, tiled=True)
    head_full = lax.all_gather(head_weight, "seq", axis=0, tiled=True)
    gains = section_gain[0]

    def tick_step(tick_now, carry):
        incoming, stashed = carry
        micro_idx = tick_now - section_pos
        active = (micro_idx >= 0) & (micro_idx < micro_count)
        picked = jnp.clip(micro_idx, 0, micro_count - 1)
        fresh = lax.dynamic_index_in_dim(encoded, picked, 0, keepdims=False)
        entering = jnp.where(section_pos == 0, fresh, incoming)
        normed = rms_scaled(entering.astype(jnp.float32), gains).astype(jnp.bfloat16)
        padded_input = padded(normed, (("seq", 0),), dilation)

        def compute():
            kernel_tap_rows = jnp.concatenate(
                [
                    padded_input[:slab_rows],
                    padded_input[dilation : dilation + slab_rows],
                    padded_input[2 * dilation : 2 * dilation + slab_rows],
                ],
                axis=1,
            )
            mixed = jnp.dot(kernel_tap_rows, weights, preferred_element_type=jnp.float32)
            return (entering.astype(jnp.float32) + jax.nn.gelu(mixed)).astype(jnp.bfloat16)

        def resting():
            return jnp.zeros_like(entering)

        result = lax.cond(active, compute, resting)
        previous = lax.dynamic_index_in_dim(stashed, picked, 0, keepdims=False)
        stashed = lax.dynamic_update_index_in_dim(
            stashed, jnp.where(active, result, previous), picked, 0
        )
        passed = from_behind(result, "section", 1)
        return (passed, stashed)

    start = (jnp.zeros((slab_rows, channels), jnp.bfloat16), jnp.zeros_like(encoded))
    handed, stashed = lax.fori_loop(0, micro_count + sections - 1, tick_step, start)
    final_all = broadcast(stashed, "section", sections - 1)
    skip_all = broadcast(stashed, "section", 0)
    final_rows = lax.dynamic_index_in_dim(final_all, section_pos, 0, keepdims=False)
    skip_rows = lax.dynamic_index_in_dim(skip_all, section_pos, 0, keepdims=False)
    embed = rms_scaled(
        final_rows.astype(jnp.float32) + skip_rows.astype(jnp.float32), head_gain
    ).astype(jnp.bfloat16)
    queries = jnp.dot(embed, head_full, preferred_element_type=jnp.float32).astype(jnp.bfloat16)
    scale = channels ** (-0.5)
    reach_count = pair_count.shape[2]
    capacity = pair_donor.shape[2] // reach_count
    donors = pair_donor[0, 0]
    acceptors = pair_acceptor[0, 0]
    counts = pair_count[0, 0]
    cotangents = pair_cotangent[0, 0]
    slot = jnp.arange(reach_count * capacity, dtype=jnp.int32)
    valid = slot % capacity < jnp.repeat(counts, capacity)
    weighted = jnp.where(valid, cotangents, jnp.zeros_like(cotangents))[:, None]
    sent = (weighted * jnp.take(queries, donors, axis=0).astype(jnp.float32) * scale).astype(
        jnp.bfloat16
    )
    answers = jnp.take(embed, acceptors, axis=0)
    received = [sent[:capacity]]
    returned = [answers[:capacity]]
    for reach_idx in range(1, reach_count):
        lower = reach_idx * capacity
        received.append(from_behind(sent[lower : lower + capacity], "seq", reach_idx))
        returned.append(from_behind(answers[lower : lower + capacity], "seq", -reach_idx))
    received = jnp.concatenate(received, axis=0)
    returned = jnp.concatenate(returned, axis=0)
    position_index = jnp.arange(slab_rows, dtype=jnp.int32)
    accept_hot = (position_index[:, None] == acceptors[None, :]).astype(jnp.bfloat16)
    from_acc = jnp.dot(accept_hot, received, preferred_element_type=jnp.float32)
    donor_onehot = (position_index[:, None] == donors[None, :]).astype(jnp.float32)
    query_grad = jnp.dot(
        donor_onehot,
        weighted * returned.astype(jnp.float32) * scale,
        precision=lax.Precision.HIGHEST,
    )
    grad_rows = (
        lax.dot_general(
            query_grad.astype(jnp.bfloat16),
            head_full,
            (((1,), (1,)), ((), ())),
            preferred_element_type=jnp.float32,
        )
        + from_acc
    )
    return (stashed[None], grad_rows[None])


def solution(mesh):
    placed = (
        P(None, "seq", None),
        P("section", "seq", None),
        P("section", None),
        P(),
        P("seq", None),
        P("section", "seq", None),
        P("section", "seq", None),
        P("section", "seq", None),
        P("section", "seq", None),
    )
    return jax.shard_map(
        on_device,
        mesh=mesh,
        in_specs=placed,
        out_specs=(P("section", None, "seq", None), P("section", "seq", None)),
        check_vma=False,
    )
```

profile of v0, /device:TPU:1, one launch (start us, length us, event | category | flops | bytes accessed | tf_op | source)
XLA Modules:
  0.0 659.9 jit_solution(15055641141476861329)
XLA Ops:
  10.0 130.7 %all-gather.5.cloned.1.call-done = bf16[1,4224,1408]{2,0,1:T(2,128)(2,1)} async-done(((bf16[1,66,1408]{2,0,1:T(2,128)(2,1)}), bf16[1,4224,1408]{2,0,1:T(2,128)(2,1)}) %all-gather.5.cloned.1.call-update) | async-done | bytes 11894800 | tf_op jit(solution)/shard_map/all_gather | solution.py:54
  140.7 16.2 %copy.15 = bf16[1,4224,1408]{2,1,0:T(8,128)(2,1)} copy(bf16[1,4224,1408]{2,0,1:T(2,128)(2,1)} %all-gather.5.cloned.1.call-done) | data formatting | bytes 23789568
  157.6 339.0 %while.16 = (s32[]{:T(128)}, bf16[64,1408]{1,0:T(8,128)(2,1)S(1)}, bf16[8,64,1408]{2,1,0:T(8,128)(2,1)S(1)}, s32[]{:T(128)}, pred[]{:T(512)}, /*index=5*/bf16[8,...) while((s32[]{:T(128)}, bf16[64,1408]{1,0:T(8,128)(2,1)S(1)}, ...), condition=%wide.region_4.5_spmd, body=%wide.region_0.4_spmd.sunk | while | flops 765771840 | bytes 17860460 | solution.py:92
  166.1 6.5 conditional.2
  166.1 6.4 fusion.18
  179.9 4.6 collective-permute-start.1
  186.0 6.5 conditional.2
  186.1 6.4 fusion.18
  202.2 5.2 collective-permute-start.1
  209.4 6.6 conditional.2
  209.5 6.5 fusion.18
  225.3 7.2 %collective-permute-start.1 = (bf16[32,1408]{1,0:T(8,128)(2,1)S(1)}, bf16[32,1408]{1,0:T(8,128)(2,1)S(1)}, u32[]{:S(2)}, u32[]{:S(2)}) collective-permute-start(bf16[32,1408]{1,0:T(8,128)(2,1)S(1)} %get-tuple-element.273), channel_id=1, source_target_pairs={{0,8},{8,16},{16,24},{24,32},{32,40},{40,48},{48,56},{56,64},{64,7... | collective-permute-start | bytes 270344 | tf_op jit(solution)/shard_map/while/body/eval_jaxpr/ppermute | solution.py:15
  234.0 6.5 conditional.2
  234.1 6.4 fusion.18
  240.5 4.1 collective-permute-start.2
  250.2 6.9 %collective-permute-start.1 = (bf16[32,1408]{1,0:T(8,128)(2,1)S(1)}, bf16[32,1408]{1,0:T(8,128)(2,1)S(1)}, u32[]{:S(2)}, u32[]{:S(2)}) collective-permute-start(bf16[32,1408]{1,0:T(8,128)(2,1)S(1)} %get-tuple-element.273), channel_id=1, source_target_pairs={{0,8},{8,16},{16,24},{24,32},{32,40},{40,48},{48,56},{56,64},{64,7... | collective-permute-start | bytes 270344 | tf_op jit(solution)/shard_map/while/body/eval_jaxpr/ppermute | solution.py:15
  258.8 6.5 conditional.2
  258.8 6.4 fusion.18
  265.2 4.1 collective-permute-start.2
  275.0 6.5 collective-permute-start.1
  283.0 6.5 conditional.2
  283.1 6.4 fusion.18
  289.5 4.1 collective-permute-start.2
  299.2 6.4 collective-permute-start.1
  307.2 6.5 conditional.2
  307.2 6.4 fusion.18
  313.6 4.1 collective-permute-start.2
  323.4 6.4 collective-permute-start.1
  331.3 6.5 conditional.2
  331.4 6.4 fusion.18
  337.8 4.1 collective-permute-start.2
  347.5 6.4 collective-permute-start.1
  355.5 10.5 %collective-permute-start.2 = (bf16[64,1408]{1,0:T(8,128)(2,1)S(1)}, bf16[64,1408]{1,0:T(8,128)(2,1)S(1)}, u32[]{:S(2)}, u32[]{:S(2)}) collective-permute-start(bf16[64,1408]{1,0:T(8,128)(2,1)S(1)} %get-tuple-element.315), channel_id=1, source_target_pairs={{0,1},{1,2},{2,3},{3,4},{4,5},{5,6},{6,7},{8,9},{9,10},{10,11},{11... | collective-permute-start | bytes 540680 | tf_op jit(solution)/shard_map/while/body/eval_jaxpr/ppermute | solution.py:27
  371.7 6.4 collective-permute-start.1
  379.7 4.1 collective-permute-start.2
  389.4 6.4 collective-permute-start.1
  397.4 8.3 %collective-permute-start.2 = (bf16[64,1408]{1,0:T(8,128)(2,1)S(1)}, bf16[64,1408]{1,0:T(8,128)(2,1)S(1)}, u32[]{:S(2)}, u32[]{:S(2)}) collective-permute-start(bf16[64,1408]{1,0:T(8,128)(2,1)S(1)} %get-tuple-element.315), channel_id=1, source_target_pairs={{0,1},{1,2},{2,3},{3,4},{4,5},{5,6},{6,7},{8,9},{9,10},{10,11},{11... | collective-permute-start | bytes 540680 | tf_op jit(solution)/shard_map/while/body/eval_jaxpr/ppermute | solution.py:27
  411.3 6.4 collective-permute-start.1
  419.3 5.2 collective-permute-start.2
  430.1 6.4 collective-permute-start.1
  438.1 11.7 %collective-permute-start.2 = (bf16[64,1408]{1,0:T(8,128)(2,1)S(1)}, bf16[64,1408]{1,0:T(8,128)(2,1)S(1)}, u32[]{:S(2)}, u32[]{:S(2)}) collective-permute-start(bf16[64,1408]{1,0:T(8,128)(2,1)S(1)} %get-tuple-element.315), channel_id=1, source_target_pairs={{0,1},{1,2},{2,3},{3,4},{4,5},{5,6},{6,7},{8,9},{9,10},{10,11},{11... | collective-permute-start | bytes 540680 | tf_op jit(solution)/shard_map/while/body/eval_jaxpr/ppermute | solution.py:27
  455.5 6.4 collective-permute-start.1
  463.5 5.3 collective-permute-start.2
  474.4 6.4 collective-permute-start.1
  482.4 11.7 %collective-permute-start.2 = (bf16[64,1408]{1,0:T(8,128)(2,1)S(1)}, bf16[64,1408]{1,0:T(8,128)(2,1)S(1)}, u32[]{:S(2)}, u32[]{:S(2)}) collective-permute-start(bf16[64,1408]{1,0:T(8,128)(2,1)S(1)} %get-tuple-element.315), channel_id=1, source_target_pairs={{0,1},{1,2},{2,3},{3,4},{4,5},{5,6},{6,7},{8,9},{9,10},{10,11},{11... | collective-permute-start | bytes 540680 | tf_op jit(solution)/shard_map/while/body/eval_jaxpr/ppermute | solution.py:27
  499.6 6.2 reshape.77
  505.8 117.6 %all-reduce.3.cloned.1.call-done = (bf16[8,64,1408]{2,1,0:T(8,128)(2,1)}, bf16[8,64,1408]{2,1,0:T(8,128)(2,1)}) async-done(((bf16[8,64,1408]{2,1,0:T(8,128)(2,1)}, bf16[8,64,1408]{2,1,0:T(8,128)(2,1)}), (bf16[8,64,1408]{2,1,0:T(8,128)(2,1)}, bf16[8,64,1408]{2,1,0:T(8,128)(2,1)})) %all-reduce.3.cloned.1.call-update) | async-done | bytes 2883600 | tf_op jit(solution)/shard_map/psum | solution.py:32
  640.5 4.3 collective-permute-start.7
  (263 shorter events, 153.2 us)
Async XLA Ops:
  7.2 133.6 %all-gather.5.cloned.1.call-start = ((), (), s32[]{:S(2)}) async-start(), calls=%async_computation | async-start | bytes 24161280 | tf_op jit(solution)/shard_map/all_gather | solution.py:54
  9.2 490.4 %all-gather.7.cloned.1.call-start = ((), (), s32[]{:S(2)}) async-start(), calls=%async_computation.1 | async-start | bytes 4392960 | tf_op jit(solution)/shard_map/all_gather | solution.py:55
  9.9 613.4 %all-reduce.3.cloned.1.call-start = ((), (), s32[]{:S(2)}) async-start(), calls=%async_computation.2 | async-start | bytes 5767168 | tf_op jit(solution)/shard_map/psum | solution.py:32
  178.0 6.8 %collective-permute-start = (bf16[32,1408]{1,0:T(8,128)(2,1)S(1)}, bf16[32,1408]{1,0:T(8,128)(2,1)S(1)}, u32[]{:S(2)}, u32[]{:S(2)}) collective-permute-start(bf16[32,1408]{1,0:T(8,128)(2,1)S(1)} %get-tuple-element.272), channel_id=1, source_target_pairs={{8,0},{16,8},{24,16},{32,24},{40,32},{48,40},{56,48},{64,56},{72,6... | collective-permute-start | bytes 270344 | tf_op jit(solution)/shard_map/while/body/eval_jaxpr/ppermute | solution.py:17
  200.3 8.8 %collective-permute-start = (bf16[32,1408]{1,0:T(8,128)(2,1)S(1)}, bf16[32,1408]{1,0:T(8,128)(2,1)S(1)}, u32[]{:S(2)}, u32[]{:S(2)}) collective-permute-start(bf16[32,1408]{1,0:T(8,128)(2,1)S(1)} %get-tuple-element.272), channel_id=1, source_target_pairs={{8,0},{16,8},{24,16},{32,24},{40,32},{48,40},{56,48},{64,56},{72,6... | collective-permute-start | bytes 270344 | tf_op jit(solution)/shard_map/while/body/eval_jaxpr/ppermute | solution.py:17
  202.2 7.2 %collective-permute-start.1 = (bf16[32,1408]{1,0:T(8,128)(2,1)S(1)}, bf16[32,1408]{1,0:T(8,128)(2,1)S(1)}, u32[]{:S(2)}, u32[]{:S(2)}) collective-permute-start(bf16[32,1408]{1,0:T(8,128)(2,1)S(1)} %get-tuple-element.273), channel_id=1, source_target_pairs={{0,8},{8,16},{16,24},{24,32},{32,40},{40,48},{48,56},{56,64},{64,7... | collective-permute-start | bytes 270344 | tf_op jit(solution)/shard_map/while/body/eval_jaxpr/ppermute | solution.py:15
  223.4 9.4 %collective-permute-start = (bf16[32,1408]{1,0:T(8,128)(2,1)S(1)}, bf16[32,1408]{1,0:T(8,128)(2,1)S(1)}, u32[]{:S(2)}, u32[]{:S(2)}) collective-permute-start(bf16[32,1408]{1,0:T(8,128)(2,1)S(1)} %get-tuple-element.272), channel_id=1, source_target_pairs={{8,0},{16,8},{24,16},{32,24},{40,32},{48,40},{56,48},{64,56},{72,6... | collective-permute-start | bytes 270344 | tf_op jit(solution)/shard_map/while/body/eval_jaxpr/ppermute | solution.py:17
  225.3 8.7 %collective-permute-start.1 = (bf16[32,1408]{1,0:T(8,128)(2,1)S(1)}, bf16[32,1408]{1,0:T(8,128)(2,1)S(1)}, u32[]{:S(2)}, u32[]{:S(2)}) collective-permute-start(bf16[32,1408]{1,0:T(8,128)(2,1)S(1)} %get-tuple-element.273), channel_id=1, source_target_pairs={{0,8},{8,16},{16,24},{24,32},{32,40},{40,48},{48,56},{56,64},{64,7... | collective-permute-start | bytes 270344 | tf_op jit(solution)/shard_map/while/body/eval_jaxpr/ppermute | solution.py:15
  240.5 6.5 collective-permute-start.2
  248.3 9.1 %collective-permute-start = (bf16[32,1408]{1,0:T(8,128)(2,1)S(1)}, bf16[32,1408]{1,0:T(8,128)(2,1)S(1)}, u32[]{:S(2)}, u32[]{:S(2)}) collective-permute-start(bf16[32,1408]{1,0:T(8,128)(2,1)S(1)} %get-tuple-element.272), channel_id=1, source_target_pairs={{8,0},{16,8},{24,16},{32,24},{40,32},{48,40},{56,48},{64,56},{72,6... | collective-permute-start | bytes 270344 | tf_op jit(solution)/shard_map/while/body/eval_jaxpr/ppermute | solution.py:17
  250.2 8.5 %collective-permute-start.1 = (bf16[32,1408]{1,0:T(8,128)(2,1)S(1)}, bf16[32,1408]{1,0:T(8,128)(2,1)S(1)}, u32[]{:S(2)}, u32[]{:S(2)}) collective-permute-start(bf16[32,1408]{1,0:T(8,128)(2,1)S(1)} %get-tuple-element.273), channel_id=1, source_target_pairs={{0,8},{8,16},{16,24},{24,32},{32,40},{40,48},{48,56},{56,64},{64,7... | collective-permute-start | bytes 270344 | tf_op jit(solution)/shard_map/while/body/eval_jaxpr/ppermute | solution.py:15
  265.2 6.5 collective-permute-start.2
  273.0 8.7 %collective-permute-start = (bf16[32,1408]{1,0:T(8,128)(2,1)S(1)}, bf16[32,1408]{1,0:T(8,128)(2,1)S(1)}, u32[]{:S(2)}, u32[]{:S(2)}) collective-permute-start(bf16[32,1408]{1,0:T(8,128)(2,1)S(1)} %get-tuple-element.272), channel_id=1, source_target_pairs={{8,0},{16,8},{24,16},{32,24},{40,32},{48,40},{56,48},{64,56},{72,6... | collective-permute-start | bytes 270344 | tf_op jit(solution)/shard_map/while/body/eval_jaxpr/ppermute | solution.py:17
  275.0 8.0 %collective-permute-start.1 = (bf16[32,1408]{1,0:T(8,128)(2,1)S(1)}, bf16[32,1408]{1,0:T(8,128)(2,1)S(1)}, u32[]{:S(2)}, u32[]{:S(2)}) collective-permute-start(bf16[32,1408]{1,0:T(8,128)(2,1)S(1)} %get-tuple-element.273), channel_id=1, source_target_pairs={{0,8},{8,16},{16,24},{24,32},{32,40},{40,48},{48,56},{56,64},{64,7... | collective-permute-start | bytes 270344 | tf_op jit(solution)/shard_map/while/body/eval_jaxpr/ppermute | solution.py:15
  289.5 6.5 collective-permute-start.2
  297.3 8.6 %collective-permute-start = (bf16[32,1408]{1,0:T(8,128)(2,1)S(1)}, bf16[32,1408]{1,0:T(8,128)(2,1)S(1)}, u32[]{:S(2)}, u32[]{:S(2)}) collective-permute-start(bf16[32,1408]{1,0:T(8,128)(2,1)S(1)} %get-tuple-element.272), channel_id=1, source_target_pairs={{8,0},{16,8},{24,16},{32,24},{40,32},{48,40},{56,48},{64,56},{72,6... | collective-permute-start | bytes 270344 | tf_op jit(solution)/shard_map/while/body/eval_jaxpr/ppermute | solution.py:17
  299.2 7.9 %collective-permute-start.1 = (bf16[32,1408]{1,0:T(8,128)(2,1)S(1)}, bf16[32,1408]{1,0:T(8,128)(2,1)S(1)}, u32[]{:S(2)}, u32[]{:S(2)}) collective-permute-start(bf16[32,1408]{1,0:T(8,128)(2,1)S(1)} %get-tuple-element.273), channel_id=1, source_target_pairs={{0,8},{8,16},{16,24},{24,32},{32,40},{40,48},{48,56},{56,64},{64,7... | collective-permute-start | bytes 270344 | tf_op jit(solution)/shard_map/while/body/eval_jaxpr/ppermute | solution.py:15
  313.6 6.5 collective-permute-start.2
  321.4 8.6 %collective-permute-start = (bf16[32,1408]{1,0:T(8,128)(2,1)S(1)}, bf16[32,1408]{1,0:T(8,128)(2,1)S(1)}, u32[]{:S(2)}, u32[]{:S(2)}) collective-permute-start(bf16[32,1408]{1,0:T(8,128)(2,1)S(1)} %get-tuple-element.272), channel_id=1, source_target_pairs={{8,0},{16,8},{24,16},{32,24},{40,32},{48,40},{56,48},{64,56},{72,6... | collective-permute-start | bytes 270344 | tf_op jit(solution)/shard_map/while/body/eval_jaxpr/ppermute | solution.py:17
  323.4 7.9 %collective-permute-start.1 = (bf16[32,1408]{1,0:T(8,128)(2,1)S(1)}, bf16[32,1408]{1,0:T(8,128)(2,1)S(1)}, u32[]{:S(2)}, u32[]{:S(2)}) collective-permute-start(bf16[32,1408]{1,0:T(8,128)(2,1)S(1)} %get-tuple-element.273), channel_id=1, source_target_pairs={{0,8},{8,16},{16,24},{24,32},{32,40},{40,48},{48,56},{56,64},{64,7... | collective-permute-start | bytes 270344 | tf_op jit(solution)/shard_map/while/body/eval_jaxpr/ppermute | solution.py:15
  337.8 6.5 collective-permute-start.2
  345.6 8.6 %collective-permute-start = (bf16[32,1408]{1,0:T(8,128)(2,1)S(1)}, bf16[32,1408]{1,0:T(8,128)(2,1)S(1)}, u32[]{:S(2)}, u32[]{:S(2)}) collective-permute-start(bf16[32,1408]{1,0:T(8,128)(2,1)S(1)} %get-tuple-element.272), channel_id=1, source_target_pairs={{8,0},{16,8},{24,16},{32,24},{40,32},{48,40},{56,48},{64,56},{72,6... | collective-permute-start | bytes 270344 | tf_op jit(solution)/shard_map/while/body/eval_jaxpr/ppermute | solution.py:17
  347.5 7.9 %collective-permute-start.1 = (bf16[32,1408]{1,0:T(8,128)(2,1)S(1)}, bf16[32,1408]{1,0:T(8,128)(2,1)S(1)}, u32[]{:S(2)}, u32[]{:S(2)}) collective-permute-start(bf16[32,1408]{1,0:T(8,128)(2,1)S(1)} %get-tuple-element.273), channel_id=1, source_target_pairs={{0,8},{8,16},{16,24},{24,32},{32,40},{40,48},{48,56},{56,64},{64,7... | collective-permute-start | bytes 270344 | tf_op jit(solution)/shard_map/while/body/eval_jaxpr/ppermute | solution.py:15
  355.5 13.0 %collective-permute-start.2 = (bf16[64,1408]{1,0:T(8,128)(2,1)S(1)}, bf16[64,1408]{1,0:T(8,128)(2,1)S(1)}, u32[]{:S(2)}, u32[]{:S(2)}) collective-permute-start(bf16[64,1408]{1,0:T(8,128)(2,1)S(1)} %get-tuple-element.315), channel_id=1, source_target_pairs={{0,1},{1,2},{2,3},{3,4},{4,5},{5,6},{6,7},{8,9},{9,10},{10,11},{11... | collective-permute-start | bytes 540680 | tf_op jit(solution)/shard_map/while/body/eval_jaxpr/ppermute | solution.py:27
  369.7 8.6 %collective-permute-start = (bf16[32,1408]{1,0:T(8,128)(2,1)S(1)}, bf16[32,1408]{1,0:T(8,128)(2,1)S(1)}, u32[]{:S(2)}, u32[]{:S(2)}) collective-permute-start(bf16[32,1408]{1,0:T(8,128)(2,1)S(1)} %get-tuple-element.272), channel_id=1, source_target_pairs={{8,0},{16,8},{24,16},{32,24},{40,32},{48,40},{56,48},{64,56},{72,6... | collective-permute-start | bytes 270344 | tf_op jit(solution)/shard_map/while/body/eval_jaxpr/ppermute | solution.py:17
  371.7 7.9 %collective-permute-start.1 = (bf16[32,1408]{1,0:T(8,128)(2,1)S(1)}, bf16[32,1408]{1,0:T(8,128)(2,1)S(1)}, u32[]{:S(2)}, u32[]{:S(2)}) collective-permute-start(bf16[32,1408]{1,0:T(8,128)(2,1)S(1)} %get-tuple-element.273), channel_id=1, source_target_pairs={{0,8},{8,16},{16,24},{24,32},{32,40},{40,48},{48,56},{56,64},{64,7... | collective-permute-start | bytes 270344 | tf_op jit(solution)/shard_map/while/body/eval_jaxpr/ppermute | solution.py:15
  379.7 6.5 collective-permute-start.2
  387.5 8.6 %collective-permute-start = (bf16[32,1408]{1,0:T(8,128)(2,1)S(1)}, bf16[32,1408]{1,0:T(8,128)(2,1)S(1)}, u32[]{:S(2)}, u32[]{:S(2)}) collective-permute-start(bf16[32,1408]{1,0:T(8,128)(2,1)S(1)} %get-tuple-element.272), channel_id=1, source_target_pairs={{8,0},{16,8},{24,16},{32,24},{40,32},{48,40},{56,48},{64,56},{72,6... | collective-permute-start | bytes 270344 | tf_op jit(solution)/shard_map/while/body/eval_jaxpr/ppermute | solution.py:17
  389.4 7.9 %collective-permute-start.1 = (bf16[32,1408]{1,0:T(8,128)(2,1)S(1)}, bf16[32,1408]{1,0:T(8,128)(2,1)S(1)}, u32[]{:S(2)}, u32[]{:S(2)}) collective-permute-start(bf16[32,1408]{1,0:T(8,128)(2,1)S(1)} %get-tuple-element.273), channel_id=1, source_target_pairs={{0,8},{8,16},{16,24},{24,32},{32,40},{40,48},{48,56},{56,64},{64,7... | collective-permute-start | bytes 270344 | tf_op jit(solution)/shard_map/while/body/eval_jaxpr/ppermute | solution.py:15
  397.4 10.8 %collective-permute-start.2 = (bf16[64,1408]{1,0:T(8,128)(2,1)S(1)}, bf16[64,1408]{1,0:T(8,128)(2,1)S(1)}, u32[]{:S(2)}, u32[]{:S(2)}) collective-permute-start(bf16[64,1408]{1,0:T(8,128)(2,1)S(1)} %get-tuple-element.315), channel_id=1, source_target_pairs={{0,1},{1,2},{2,3},{3,4},{4,5},{5,6},{6,7},{8,9},{9,10},{10,11},{11... | collective-permute-start | bytes 540680 | tf_op jit(solution)/shard_map/while/body/eval_jaxpr/ppermute | solution.py:27
  409.4 8.6 %collective-permute-start = (bf16[32,1408]{1,0:T(8,128)(2,1)S(1)}, bf16[32,1408]{1,0:T(8,128)(2,1)S(1)}, u32[]{:S(2)}, u32[]{:S(2)}) collective-permute-start(bf16[32,1408]{1,0:T(8,128)(2,1)S(1)} %get-tuple-element.272), channel_id=1, source_target_pairs={{8,0},{16,8},{24,16},{32,24},{40,32},{48,40},{56,48},{64,56},{72,6... | collective-permute-start | bytes 270344 | tf_op jit(solution)/shard_map/while/body/eval_jaxpr/ppermute | solution.py:17
  411.3 7.9 %collective-permute-start.1 = (bf16[32,1408]{1,0:T(8,128)(2,1)S(1)}, bf16[32,1408]{1,0:T(8,128)(2,1)S(1)}, u32[]{:S(2)}, u32[]{:S(2)}) collective-permute-start(bf16[32,1408]{1,0:T(8,128)(2,1)S(1)} %get-tuple-element.273), channel_id=1, source_target_pairs={{0,8},{8,16},{16,24},{24,32},{32,40},{40,48},{48,56},{56,64},{64,7... | collective-permute-start | bytes 270344 | tf_op jit(solution)/shard_map/while/body/eval_jaxpr/ppermute | solution.py:15
  419.3 7.6 %collective-permute-start.2 = (bf16[64,1408]{1,0:T(8,128)(2,1)S(1)}, bf16[64,1408]{1,0:T(8,128)(2,1)S(1)}, u32[]{:S(2)}, u32[]{:S(2)}) collective-permute-start(bf16[64,1408]{1,0:T(8,128)(2,1)S(1)} %get-tuple-element.315), channel_id=1, source_target_pairs={{0,1},{1,2},{2,3},{3,4},{4,5},{5,6},{6,7},{8,9},{9,10},{10,11},{11... | collective-permute-start | bytes 540680 | tf_op jit(solution)/shard_map/while/body/eval_jaxpr/ppermute | solution.py:27
  428.2 8.6 %collective-permute-start = (bf16[32,1408]{1,0:T(8,128)(2,1)S(1)}, bf16[32,1408]{1,0:T(8,128)(2,1)S(1)}, u32[]{:S(2)}, u32[]{:S(2)}) collective-permute-start(bf16[32,1408]{1,0:T(8,128)(2,1)S(1)} %get-tuple-element.272), channel_id=1, source_target_pairs={{8,0},{16,8},{24,16},{32,24},{40,32},{48,40},{56,48},{64,56},{72,6... | collective-permute-start | bytes 270344 | tf_op jit(solution)/shard_map/while/body/eval_jaxpr/ppermute | solution.py:17
  430.1 7.9 %collective-permute-start.1 = (bf16[32,1408]{1,0:T(8,128)(2,1)S(1)}, bf16[32,1408]{1,0:T(8,128)(2,1)S(1)}, u32[]{:S(2)}, u32[]{:S(2)}) collective-permute-start(bf16[32,1408]{1,0:T(8,128)(2,1)S(1)} %get-tuple-element.273), channel_id=1, source_target_pairs={{0,8},{8,16},{16,24},{24,32},{32,40},{40,48},{48,56},{56,64},{64,7... | collective-permute-start | bytes 270344 | tf_op jit(solution)/shard_map/while/body/eval_jaxpr/ppermute | solution.py:15
  438.1 14.2 %collective-permute-start.2 = (bf16[64,1408]{1,0:T(8,128)(2,1)S(1)}, bf16[64,1408]{1,0:T(8,128)(2,1)S(1)}, u32[]{:S(2)}, u32[]{:S(2)}) collective-permute-start(bf16[64,1408]{1,0:T(8,128)(2,1)S(1)} %get-tuple-element.315), channel_id=1, source_target_pairs={{0,1},{1,2},{2,3},{3,4},{4,5},{5,6},{6,7},{8,9},{9,10},{10,11},{11... | collective-permute-start | bytes 540680 | tf_op jit(solution)/shard_map/while/body/eval_jaxpr/ppermute | solution.py:27
  453.5 8.6 %collective-permute-start = (bf16[32,1408]{1,0:T(8,128)(2,1)S(1)}, bf16[32,1408]{1,0:T(8,128)(2,1)S(1)}, u32[]{:S(2)}, u32[]{:S(2)}) collective-permute-start(bf16[32,1408]{1,0:T(8,128)(2,1)S(1)} %get-tuple-element.272), channel_id=1, source_target_pairs={{8,0},{16,8},{24,16},{32,24},{40,32},{48,40},{56,48},{64,56},{72,6... | collective-permute-start | bytes 270344 | tf_op jit(solution)/shard_map/while/body/eval_jaxpr/ppermute | solution.py:17
  455.5 7.9 %collective-permute-start.1 = (bf16[32,1408]{1,0:T(8,128)(2,1)S(1)}, bf16[32,1408]{1,0:T(8,128)(2,1)S(1)}, u32[]{:S(2)}, u32[]{:S(2)}) collective-permute-start(bf16[32,1408]{1,0:T(8,128)(2,1)S(1)} %get-tuple-element.273), channel_id=1, source_target_pairs={{0,8},{8,16},{16,24},{24,32},{32,40},{40,48},{48,56},{56,64},{64,7... | collective-permute-start | bytes 270344 | tf_op jit(solution)/shard_map/while/body/eval_jaxpr/ppermute | solution.py:15
  463.5 7.7 %collective-permute-start.2 = (bf16[64,1408]{1,0:T(8,128)(2,1)S(1)}, bf16[64,1408]{1,0:T(8,128)(2,1)S(1)}, u32[]{:S(2)}, u32[]{:S(2)}) collective-permute-start(bf16[64,1408]{1,0:T(8,128)(2,1)S(1)} %get-tuple-element.315), channel_id=1, source_target_pairs={{0,1},{1,2},{2,3},{3,4},{4,5},{5,6},{6,7},{8,9},{9,10},{10,11},{11... | collective-permute-start | bytes 540680 | tf_op jit(solution)/shard_map/while/body/eval_jaxpr/ppermute | solution.py:27
  472.5 8.6 %collective-permute-start = (bf16[32,1408]{1,0:T(8,128)(2,1)S(1)}, bf16[32,1408]{1,0:T(8,128)(2,1)S(1)}, u32[]{:S(2)}, u32[]{:S(2)}) collective-permute-start(bf16[32,1408]{1,0:T(8,128)(2,1)S(1)} %get-tuple-element.272), channel_id=1, source_target_pairs={{8,0},{16,8},{24,16},{32,24},{40,32},{48,40},{56,48},{64,56},{72,6... | collective-permute-start | bytes 270344 | tf_op jit(solution)/shard_map/while/body/eval_jaxpr/ppermute | solution.py:17
  474.4 7.9 %collective-permute-start.1 = (bf16[32,1408]{1,0:T(8,128)(2,1)S(1)}, bf16[32,1408]{1,0:T(8,128)(2,1)S(1)}, u32[]{:S(2)}, u32[]{:S(2)}) collective-permute-start(bf16[32,1408]{1,0:T(8,128)(2,1)S(1)} %get-tuple-element.273), channel_id=1, source_target_pairs={{0,8},{8,16},{16,24},{24,32},{32,40},{40,48},{48,56},{56,64},{64,7... | collective-permute-start | bytes 270344 | tf_op jit(solution)/shard_map/while/body/eval_jaxpr/ppermute | solution.py:15
  482.4 14.2 %collective-permute-start.2 = (bf16[64,1408]{1,0:T(8,128)(2,1)S(1)}, bf16[64,1408]{1,0:T(8,128)(2,1)S(1)}, u32[]{:S(2)}, u32[]{:S(2)}) collective-permute-start(bf16[64,1408]{1,0:T(8,128)(2,1)S(1)} %get-tuple-element.315), channel_id=1, source_target_pairs={{0,1},{1,2},{2,3},{3,4},{4,5},{5,6},{6,7},{8,9},{9,10},{10,11},{11... | collective-permute-start | bytes 540680 | tf_op jit(solution)/shard_map/while/body/eval_jaxpr/ppermute | solution.py:27
  626.5 18.3 %collective-permute-start.3 = (bf16[16,1408]{1,0:T(8,128)(2,1)S(1)}, bf16[16,1408]{1,0:T(8,128)(2,1)S(1)}, u32[]{:S(2)}, u32[]{:S(2)}) collective-permute-start(bf16[16,1408]{1,0:T(8,128)(2,1)S(1)} %get-tuple-element.214), channel_id=1, source_target_pairs={{8,0},{16,8},{24,16},{32,24},{40,32},{48,40},{56,48},{64,56},{72,6... | collective-permute-start | bytes 135176 | tf_op jit(solution)/shard_map/ppermute | solution.py:27
  630.5 18.0 %collective-permute-start.4 = (bf16[16,1408]{1,0:T(8,128)(2,1)S(1)}, bf16[16,1408]{1,0:T(8,128)(2,1)S(1)}, u32[]{:S(2)}, u32[]{:S(2)}) collective-permute-start(bf16[16,1408]{1,0:T(8,128)(2,1)S(1)} %get-tuple-element.213), channel_id=1, source_target_pairs={{16,0},{24,8},{32,16},{40,24},{48,32},{56,40},{64,48},{72,56},{80,... | collective-permute-start | bytes 135176 | tf_op jit(solution)/shard_map/ppermute | solution.py:27
  631.9 16.7 %collective-permute-start.5 = (bf16[16,1408]{1,0:T(8,128)(2,1)S(1)}, bf16[16,1408]{1,0:T(8,128)(2,1)S(1)}, u32[]{:S(2)}, u32[]{:S(2)}) collective-permute-start(bf16[16,1408]{1,0:T(8,128)(2,1)S(1)} %get-tuple-element.212), channel_id=1, source_target_pairs={{24,0},{32,8},{40,16},{48,24},{56,32},{64,40},{72,48},{80,56},{88,... | collective-permute-start | bytes 135176 | tf_op jit(solution)/shard_map/ppermute | solution.py:27
  636.9 15.6 %collective-permute-start.6 = (bf16[16,1408]{1,0:T(8,128)(2,1)S(1)}, bf16[16,1408]{1,0:T(8,128)(2,1)S(1)}, u32[]{:S(2)}, u32[]{:S(2)}) collective-permute-start(bf16[16,1408]{1,0:T(8,128)(2,1)S(1)} %get-tuple-element.210), channel_id=1, source_target_pairs={{0,8},{8,16},{16,24},{24,32},{32,40},{40,48},{48,56},{56,64},{64,7... | collective-permute-start | bytes 135176 | tf_op jit(solution)/shard_map/ppermute | solution.py:27
  640.5 11.9 %collective-permute-start.7 = (bf16[16,1408]{1,0:T(8,128)(2,1)S(1)}, bf16[16,1408]{1,0:T(8,128)(2,1)S(1)}, u32[]{:S(2)}, u32[]{:S(2)}) collective-permute-start(bf16[16,1408]{1,0:T(8,128)(2,1)S(1)} %get-tuple-element.209), channel_id=1, source_target_pairs={{0,16},{8,24},{16,32},{24,40},{32,48},{40,56},{48,64},{56,72},{64,... | collective-permute-start | bytes 135176 | tf_op jit(solution)/shard_map/ppermute | solution.py:27
  644.8 7.6 %collective-permute-start.8 = (bf16[16,1408]{1,0:T(8,128)(2,1)S(1)}, bf16[16,1408]{1,0:T(8,128)(2,1)S(1)}, u32[]{:S(2)}, u32[]{:S(2)}) collective-permute-start(bf16[16,1408]{1,0:T(8,128)(2,1)S(1)} %get-tuple-element.208), channel_id=1, source_target_pairs={{0,24},{8,32},{16,40},{24,48},{32,56},{40,64},{48,72},{56,80},{64,... | collective-permute-start | bytes 135176 | tf_op jit(solution)/shard_map/ppermute | solution.py:27
  (13 other events, 165.2 us)
Sparse Core Ops, SparseCore 0:
  11.8 128.8 all-gather.4
  144.0 81.9 all-gather.6
  498.8 124.5 all-reduce.2
where the time goes:
time: 665 us; the launch traced here: 660 us
  waiting for transfers between devices  308 us (46%)
  starting transfers between devices  225 us (34%)
  matrix products  58.9 us (9%)
  local copies, waits for them, and re-layouts  28.3 us (4%)
  other arithmetic  24.3 us (4%)
  between operations  14 us (2%)
    all_gather x1, waiting for transfers between devices, on_device(): weights = lax.all_gather(conv_weight[0], 'seq', axis=0, tiled=True)  131 us
    psum x1, waiting for transfers between devices, broadcast(): return lax.psum(block, axis)  118 us
    ppermute x21, starting transfers between devices, from_behind(): return lax.ppermute(shard, axis, pairs)  105 us
    ppermute x15, starting transfers between devices, padded(): lax.ppermute(tail, axis, [(i, (i + 1) % count) for i in range(ends)])  91 us
    dot_general x8, matrix products, compute(): jnp.dot(kernel_tap_rows, weights, preferred_element_type=jnp.float32)  51.3 us
    ppermute x21, waiting for transfers between devices, from_behind(): return lax.ppermute(shard, axis, pairs)  35.6 us
    ppermute x15, starting transfers between devices, padded(): lax.ppermute(head, axis, [((i + 1) % count, i) for i in range(ends)])  29 us
    unnamed x17, local copies, waits for them, and re-layouts  25.6 us
  transfers between devices with their start and end apart: 54, of which 47 were waited for; matrix products, arithmetic and copies ran while one was open for 16% of the time, Pallas kernels for 0%

commit v1 on v0

v1 whole, which is shorter than its diff:
```python
import functools

import jax
import jax.numpy as jnp
from jax import lax
from jax.experimental import pallas as pl
from jax.experimental.pallas import tpu as pltpu
from jax.sharding import PartitionSpec as P


def from_behind(shard, axis, by):
    size = lax.axis_size(axis)
    pairs = [(i, i + by) for i in range(size) if 0 <= i + by < size]
    return lax.ppermute(shard, axis, pairs)


def rms_scaled(values, gains):
    return values * lax.rsqrt(jnp.mean(values * values, axis=-1, keepdims=True) + 1e-06) * gains


def core_swap(shard):
    return lax.ppermute(shard, "seq", [(i, i ^ 1) for i in range(lax.axis_size("seq"))])


def in_core_order(first_core, mine, other, axis):
    return jnp.where(
        first_core,
        jnp.concatenate([mine, other], axis=axis),
        jnp.concatenate([other, mine], axis=axis),
    )


def gathered_columns(shard, fetched):
    count = lax.axis_size("seq")
    columns = shard.shape[1]
    first_core = lax.axis_index("seq") % 2 == 0
    left, right = shard[:, :fetched], shard[:, columns - fetched :]
    arrived = core_swap(jnp.where(first_core, right, left))
    rows = in_core_order(first_core, jnp.where(first_core, left, right), arrived, 0)
    same_core = [list(range(core, count, 2)) for core in range(2)]
    return lax.all_gather(rows, "seq", axis_index_groups=same_core, axis=0, tiled=True)


def place_kernel(core_ref, mine_ref, other_ref, weights_ref, sems):
    fetched = mine_ref.shape[1]
    shared = 2 * fetched - weights_ref.shape[1]

    def place(left_ref, right_ref):
        copies = [
            pltpu.make_async_copy(left_ref, weights_ref.at[:, :fetched], sems.at[0]),
            pltpu.make_async_copy(right_ref.at[:, shared:], weights_ref.at[:, fetched:], sems.at[1]),
        ]
        for copy in copies:
            copy.start()
        for copy in copies:
            copy.wait()

    @pl.when(core_ref[0] == 0)
    def _():
        place(mine_ref, other_ref)

    @pl.when(core_ref[0] != 0)
    def _():
        place(other_ref, mine_ref)


def placed_weights(core, mine, other, columns):
    rows = mine.shape[0]
    return pl.pallas_call(
        place_kernel,
        out_shape=pltpu.VMEM((rows, columns), mine.dtype),
        in_specs=[
            pl.BlockSpec(memory_space=pltpu.SMEM),
            pl.BlockSpec(memory_space=pl.ANY),
            pl.BlockSpec(memory_space=pl.ANY),
        ],
        out_specs=pl.BlockSpec(memory_space=pltpu.VMEM),
        scratch_shapes=[pltpu.SemaphoreType.DMA((2,))],
        compiler_params=pltpu.CompilerParams(vmem_limit_bytes=16 << 20),
        cost_estimate=pl.CostEstimate(flops=0, bytes_accessed=2 * rows * columns * 2, transcendentals=0),
    )(core, mine, other)


def block_kernel(
    wide_columns, flags_ref, weights_ref, gain_ref, incoming_ref, fresh_ref, result_ref, own_ref, taps_ref, acts_ref
):
    rows, channels = incoming_ref.shape
    kept_rows = own_ref.shape[0]
    padded_rows = taps_ref.shape[0]
    fresh, low_half, forward = (flags_ref[i] != 0 for i in range(3))
    acts = jnp.where(fresh, fresh_ref[...].astype(jnp.float32), incoming_ref[...].astype(jnp.float32))
    acts_ref[...] = acts
    normed = rms_scaled(acts, gain_ref[...])
    normed = jnp.concatenate([normed, jnp.zeros((padded_rows - rows, channels), jnp.float32)], axis=0)
    taps_ref[:, :channels] = pltpu.roll(normed, 1, 0).astype(jnp.bfloat16)
    taps_ref[:, channels : 2 * channels] = normed.astype(jnp.bfloat16)
    taps_ref[:, 2 * channels :] = pltpu.roll(normed, padded_rows - 1, 0).astype(jnp.bfloat16)

    def columns(at):
        mixed = jnp.dot(taps_ref[...], weights_ref[:, at], preferred_element_type=jnp.float32)
        result = acts_ref[:, at] + jax.nn.gelu(mixed[:rows])
        own = jnp.where(low_half, result[:kept_rows], result[rows - kept_rows :])
        own_ref[:, at] = own.astype(jnp.bfloat16)
        sent = jnp.where(forward, incoming_ref[:, at].astype(jnp.float32), result)
        result_ref[:, at] = sent.astype(jnp.bfloat16)

    whole = channels // wide_columns

    def step(i, _):
        columns(pl.ds(pl.multiple_of(i * wide_columns, wide_columns), wide_columns))
        return 0

    lax.fori_loop(0, whole, step, 0)
    if channels > whole * wide_columns:
        columns(pl.ds(whole * wide_columns, channels - whole * wide_columns))


def block(flags, weights, gains, incoming, fresh, kept_rows):
    rows, channels = incoming.shape
    padded_rows = -(-rows // 16) * 16
    vmem = pl.BlockSpec(memory_space=pltpu.VMEM)
    return pl.pallas_call(
        functools.partial(block_kernel, 256),
        out_shape=(
            jax.ShapeDtypeStruct((rows, channels), jnp.bfloat16),
            jax.ShapeDtypeStruct((kept_rows, channels), jnp.bfloat16),
        ),
        in_specs=[pl.BlockSpec(memory_space=pltpu.SMEM)] + [vmem] * 4,
        out_specs=(vmem, vmem),
        scratch_shapes=[
            pltpu.VMEM((padded_rows, weights.shape[0]), jnp.bfloat16),
            pltpu.VMEM((rows, channels), jnp.float32),
        ],
        compiler_params=pltpu.CompilerParams(vmem_limit_bytes=20 << 20),
        cost_estimate=pl.CostEstimate(
            flops=2 * rows * weights.shape[0] * channels,
            bytes_accessed=4 * rows * channels * 2,
            transcendentals=rows * channels,
        ),
    )(flags, pltpu.with_memory_space_constraint(weights, pltpu.VMEM), gains, incoming, fresh)


def on_device(
    encoded,
    conv_weight,
    section_gain,
    head_gain,
    head_weight,
    pair_donor,
    pair_acceptor,
    pair_count,
    pair_cotangent,
):
    micro_count, slab_rows, channels = encoded.shape
    sections = lax.axis_size("section")
    last = sections - 1
    section_pos = lax.axis_index("section")
    slabs = lax.axis_size("seq")
    dilation = slab_rows // 2
    half = slabs // 2
    spare = sections
    low_half = lax.axis_index("seq") < half
    halves = [list(range(half)), list(range(half, slabs))]

    fetched = -(-channels // 256) * 128
    weight_part = gathered_columns(conv_weight[0], fetched)
    def to_chains(rows):
        blocks = rows.reshape(2, dilation, channels)
        chains = lax.all_to_all(blocks, "seq", 1, 0, axis_index_groups=halves)
        return chains.reshape(slab_rows, channels)

    def to_slabs(chains):
        lead = chains.shape[:-2]
        blocks = chains.reshape(*lead, half, 2, channels)
        at = len(lead)
        rows = lax.all_to_all(blocks, "seq", at, at + 1, axis_index_groups=halves)
        return rows.reshape(*lead, slab_rows, channels)

    def own_rows(wide):
        return jnp.where(low_half, wide[..., :slab_rows, :], wide[..., spare:, :])

    mine = lax.dynamic_index_in_dim(encoded, section_pos, 0, keepdims=False)
    chains = to_chains(mine)
    edge = lax.ppermute(
        jnp.where(low_half, chains[slab_rows - spare :], chains[:spare]),
        "seq",
        [(i, (i + half) % slabs) for i in range(slabs)],
    )
    wide = jnp.where(
        low_half,
        jnp.concatenate([chains, edge], axis=0),
        jnp.concatenate([edge, chains], axis=0),
    )
    order = list(range(last - 1, -1, -1)) + [last]
    fresh = [wide if m == 0 else lax.ppermute(wide, "section", [(m, 0)]) for m in order]
    weight_part, *fresh = lax.optimization_barrier((weight_part, *fresh))
    core = (lax.axis_index("seq") % 2).astype(jnp.int32)
    weights = placed_weights(core[None], weight_part, core_swap(weight_part), channels)
    head_weight, weight_part = lax.optimization_barrier((head_weight, weight_part))
    head_parts = lax.all_gather(head_weight, "seq")

    ticks = micro_count + last
    def gathered_outputs(owns, first, count):
        held = jnp.stack(owns[first : first + count + last])
        return lax.dynamic_slice_in_dim(held, section_pos, count, 0)

    early = micro_count // 2
    results, owns, landing = [], [], []
    skip_input = 0.0
    incoming = jnp.zeros_like(wide)
    for tick in range(ticks):
        rank = tick - section_pos
        flags = jnp.stack(
            [
                (section_pos == 0) & (tick < micro_count),
                low_half,
                rank >= micro_count,
            ]
        ).astype(jnp.int32)
        result, own = block(
            flags, weights, section_gain, incoming, fresh[tick] if tick < micro_count else incoming, slab_rows
        )
        results.append(result)
        owns.append(own)
        if tick == ticks - 1:
            final = jnp.where(section_pos == last, result, incoming)
            break
        if tick >= micro_count - 1:
            home = tick - micro_count + 1 or last
            skip, result = lax.optimization_barrier((results[order.index(home)], result))
            landing.append(lax.ppermute(skip, "section", [(0, home)]))
        incoming = lax.ppermute(
            result, "section", [(i, (i + 1) % sections) for i in range(sections)]
        )
        if len(landing) > 1:
            landed, incoming = lax.optimization_barrier((landing.pop(0), incoming))
            skip_input = skip_input + landed.astype(jnp.float32)
        if tick == early - 1 + last:
            early_rows = to_slabs(gathered_outputs(owns, 0, early))
        if tick == early + 1 + last:
            head_parts, early_rows, incoming = lax.optimization_barrier((head_parts, early_rows, incoming))
            head_full = head_parts.reshape(channels, channels)
        if tick == ticks - 2:
            late_rows = to_slabs(gathered_outputs(owns, early, last - early))
    for landed in landing:
        skip_input = skip_input + landed.astype(jnp.float32)
    skip_input = skip_input + jnp.where(section_pos == 0, results[order.index(0)], 0).astype(jnp.float32)
    head_input = final.astype(jnp.float32) + skip_input
    embed = own_rows(rms_scaled(head_input, head_gain).astype(jnp.bfloat16))
    newest = functools.reduce(
        lambda total, s: jnp.where(section_pos == s, owns[last + s], total), range(1, sections), owns[last]
    )
    embed, late_rows = lax.optimization_barrier((embed, late_rows))
    embed, newest_rows = to_slabs(jnp.stack([embed, newest]))
    entered = jnp.concatenate([early_rows, late_rows, newest_rows[None]], axis=0)
    stashed = jnp.stack([entered[order.index(m)] for m in range(micro_count)])

    scale = channels ** (-0.5)
    reach_count = pair_count.shape[2]
    capacity = pair_donor.shape[2] // reach_count
    donors = pair_donor[0, 0]
    acceptors = pair_acceptor[0, 0]
    counts = pair_count[0, 0]
    cotangents = pair_cotangent[0, 0]
    answers = jnp.take(embed, acceptors, axis=0)
    returned = [answers[:capacity]]
    for reach_idx in range(1, reach_count):
        lower = reach_idx * capacity
        returned.append(from_behind(answers[lower : lower + capacity], "seq", -reach_idx))
    queries = jnp.dot(embed, head_full, preferred_element_type=jnp.float32).astype(jnp.bfloat16)
    slot = jnp.arange(reach_count * capacity, dtype=jnp.int32)
    valid = slot % capacity < jnp.repeat(counts, capacity)
    weighted = jnp.where(valid, cotangents, jnp.zeros_like(cotangents))[:, None]
    sent = (weighted * jnp.take(queries, donors, axis=0).astype(jnp.float32) * scale).astype(
        jnp.bfloat16
    )
    received = [sent[:capacity]]
    for reach_idx in range(1, reach_count):
        lower = reach_idx * capacity
        received.append(from_behind(sent[lower : lower + capacity], "seq", reach_idx))
    received = jnp.concatenate(received, axis=0)
    returned = jnp.concatenate(returned, axis=0)
    position_index = jnp.arange(slab_rows, dtype=jnp.int32)
    accept_hot = (position_index[:, None] == acceptors[None, :]).astype(jnp.bfloat16)
    from_acc = jnp.dot(accept_hot, received, preferred_element_type=jnp.float32)
    donor_onehot = (position_index[:, None] == donors[None, :]).astype(jnp.float32)
    query_grad = jnp.dot(
        donor_onehot,
        weighted * returned.astype(jnp.float32) * scale,
        precision=lax.Precision.HIGHEST,
    )
    grad_rows = (
        lax.dot_general(
            query_grad.astype(jnp.bfloat16),
            head_full,
            (((1,), (1,)), ((), ())),
            preferred_element_type=jnp.float32,
        )
        + from_acc
    )
    return (stashed[None], grad_rows[None])


def solution(mesh):
    placed = (
        P(None, "seq", None),
        P("section", "seq", None),
        P("section", None),
        P(),
        P("seq", None),
        P("section", "seq", None),
        P("section", "seq", None),
        P("section", "seq", None),
        P("section", "seq", None),
    )
    return jax.shard_map(
        on_device,
        mesh=mesh,
        in_specs=placed,
        out_specs=(P("section", None, "seq", None), P("section", "seq", None)),
        check_vma=False,
    )
```

time: 665 us -> 432 us (0.65)
  waiting for transfers between devices: 308 us -> 162 us
  starting transfers between devices: 225 us -> 134 us
  Pallas kernels: 0 us -> 61.4 us
  matrix products: 58.9 us -> 7.58 us
  other arithmetic: 24.3 us -> 6.87 us
  local copies, waits for them, and re-layouts: 28.3 us -> 42.8 us
    psum x1 -> x0, waiting for transfers between devices: 118 us -> none  [broadcast(): return lax.psum(block, axis)]
    ppermute x21 -> x6, starting transfers between devices: 105 us -> 17.7 us  [from_behind(): return lax.ppermute(shard, axis, pairs)]
    all_gather x2, waiting for transfers between devices: 131 us -> 47.8 us  [the longest x1 47.8 us: gathered_columns(): lax.all_gather(rows, 'seq', axis_index_groups=same_core, axis=0, tiled=True)]
    ppermute x30 -> x31, waiting for transfers between devices: 23 us -> 91.2 us  [the longest x14 62.2 us: on_device(): lax.ppermute(result, 'section', [(i, (i + 1) % sections) for i in range(s...]
    pallas_call x0 -> x16, Pallas kernels: none -> 61.4 us  [the longest x15 58.5 us: block(): pl.pallas_call(functools.partial(block_kernel, 256), out_shape=(jax.Shape...]
    dot_general x8 -> x0, matrix products: 51.3 us -> none  [compute(): jnp.dot(kernel_tap_rows, weights, preferred_element_type=jnp.float32)]
    ppermute x30 -> x31, starting transfers between devices: 120 us -> 77.4 us  [the longest x14 29.8 us: on_device(): lax.ppermute(result, 'section', [(i, (i + 1) % sections) for i in range(s...]
    all_to_all x0 -> x4, starting transfers between devices: none -> 39.1 us  [the longest x3 35.2 us: to_slabs(): rows = lax.all_to_all(blocks, 'seq', at, at + 1, axis_index_groups=halves)]
  transfers between devices with their start and end apart: 54 -> 43, of which waited for: 47 -> 20; matrix products, arithmetic and copies ran while one was open for 16% -> 8% of each run, Pallas kernels for 0% -> 14%
where the time goes in v1:
time: 432 us; the launch traced here: 430 us
  waiting for transfers between devices  162 us (38%)
  starting transfers between devices  134 us (31%)
  Pallas kernels  61.4 us (14%)
  local copies, waits for them, and re-layouts  42.8 us (10%)
  between operations  15.2 us (4%)
  matrix products  7.58 us (2%)
  other arithmetic  6.87 us (2%)
    ppermute x14, waiting for transfers between devices, on_device(): lax.ppermute(result, 'section', [(i, (i + 1) % sections) for i in range(s...  62.2 us
    pallas_call x15, Pallas kernels, block(): pl.pallas_call(functools.partial(block_kernel, 256), out_shape=(jax.Shape...  58.5 us
    all_gather x1, waiting for transfers between devices, gathered_columns(): lax.all_gather(rows, 'seq', axis_index_groups=same_core, axis=0, tiled=True)  47.8 us
    all_to_all x3, starting transfers between devices, to_slabs(): rows = lax.all_to_all(blocks, 'seq', at, at + 1, axis_index_groups=halves)  35.2 us
    ppermute x14, starting transfers between devices, on_device(): lax.ppermute(result, 'section', [(i, (i + 1) % sections) for i in range(s...  29.8 us
    ppermute x7, starting transfers between devices, on_device(): landing.append(lax.ppermute(skip, 'section', [(0, home)]))  23.1 us
    unnamed x78, local copies, waits for them, and re-layouts  19.6 us
    ppermute x6, starting transfers between devices, from_behind(): return lax.ppermute(shard, axis, pairs)  17.7 us
  transfers between devices with their start and end apart: 43, of which 20 were waited for; matrix products, arithmetic and copies ran while one was open for 8% of the time, Pallas kernels for 14%

profile of v1, /device:TPU:1, one launch (start us, length us, event | category | flops | bytes accessed | tf_op | source)
XLA Modules:
  0.0 430.4 jit_solution(17187209489062504959)
XLA Ops:
  8.3 8.8 %collective-permute-start = (bf16[66,768]{1,0:T(8,128)(2,1)S(1)}, bf16[66,768]{1,0:T(8,128)(2,1)S(1)}, u32[]{:S(2)}, u32[]{:S(2)}) collective-permute-start(bf16[66,768]{1,0:T(8,128)(2,1)S(1)} %get-tuple-element.152), channel_id=1, source_target_pairs={{0,8},{8,0},{16,24},{24,16},{32,40},{40,32},{48,56},{56,48},{64,72... | collective-permute-start | bytes 304136 | tf_op jit(solution)/shard_map/ppermute | solution.py:22
  19.7 3.9 all-to-all-start
  23.6 9.9 %all-to-all-done = bf16[1,2,32,1408]{3,1,0,2:T(2,128)(2,1)S(1)} async-done(((bf16[1,2,32,1408]{3,1,0,2:T(2,128)(2,1)}), bf16[1,2,32,1408]{3,1,0,2:T(2,128)(2,1)S(1)}, u32[]{:S(2)}, u32[]{:S(2)}) %all-to-all-start) | async-done | bytes 180256 | tf_op jit(solution)/shard_map/all_to_all | solution.py:169
  33.6 3.5 collective-permute-start.1
  46.3 16.4 %collective-permute-done.2.fresh_ref = bf16[72,1408]{1,0:T(8,128)(2,1)S(1)} collective-permute-done((bf16[72,1408]{1,0:T(8,128)(2,1)S(1)}, bf16[72,1408]{1,0:T(8,128)(2,1)S(1)}, u32[]{:S(2)}, u32[]{:S(2)}) %collective-permute-start.2) | collective-permute-done | bytes 202784 | tf_op jit(solution)/shard_map/ppermute | solution.py:195
  65.4 47.8 %all-gather.6.cloned.1.call-done = bf16[32,132,768]{2,1,0:T(8,128)(2,1)} async-done(((bf16[1,132,768]{2,1,0:T(8,128)(2,1)}), bf16[32,132,768]{2,1,0:T(8,128)(2,1)}) %all-gather.6.cloned.1.call-update) | async-done | bytes 6488080 | tf_op jit(solution)/shard_map/all_gather | solution.py:41
  113.1 8.3 %reshape.83.mine_ref = bf16[4224,768]{1,0:T(8,128)(2,1)} reshape(bf16[32,132,768]{2,1,0:T(8,128)(2,1)} %all-gather.6.cloned.1.call-done) | data formatting | bytes 12976128 | tf_op jit(solution)/shard_map/optimization_barrier | solution.py:196
  125.7 9.2 %collective-permute-done.9.other_ref = bf16[4224,768]{1,0:T(8,128)(2,1)} collective-permute-done((bf16[4224,768]{1,0:T(8,128)(2,1)}, bf16[4224,768]{1,0:T(8,128)(2,1)}, u32[]{:S(2)}, u32[]{:S(2)}) %collective-permute-start.9) | collective-permute-done | bytes 6488096 | tf_op jit(solution)/shard_map/ppermute | solution.py:22
  140.6 3.9 shard_map.105
  147.9 7.3 %collective-permute-done.10.incoming_ref = bf16[72,1408]{1,0:T(8,128)(2,1)S(1)} collective-permute-done((bf16[72,1408]{1,0:T(8,128)(2,1)S(1)}, bf16[72,1408]{1,0:T(8,128)(2,1)S(1)}, u32[]{:S(2)}, u32[]{:S(2)}) %collective-permute-start.10) | collective-permute-done | bytes 202784 | tf_op jit(solution)/shard_map/ppermute | solution.py:232
  155.1 3.9 shard_map.106
  161.0 6.7 %collective-permute-done.11.incoming_ref = bf16[72,1408]{1,0:T(8,128)(2,1)S(1)} collective-permute-done((bf16[72,1408]{1,0:T(8,128)(2,1)S(1)}, bf16[72,1408]{1,0:T(8,128)(2,1)S(1)}, u32[]{:S(2)}, u32[]{:S(2)}) %collective-permute-start.11) | collective-permute-done | bytes 202784 | tf_op jit(solution)/shard_map/ppermute | solution.py:232
  167.7 3.9 shard_map.107
  173.6 5.7 %collective-permute-done.12.incoming_ref = bf16[72,1408]{1,0:T(8,128)(2,1)S(1)} collective-permute-done((bf16[72,1408]{1,0:T(8,128)(2,1)S(1)}, bf16[72,1408]{1,0:T(8,128)(2,1)S(1)}, u32[]{:S(2)}, u32[]{:S(2)}) %collective-permute-start.12) | collective-permute-done | bytes 202784 | tf_op jit(solution)/shard_map/ppermute | solution.py:232
  179.3 3.9 shard_map.108
  185.2 6.1 %collective-permute-done.13.incoming_ref = bf16[72,1408]{1,0:T(8,128)(2,1)S(1)} collective-permute-done((bf16[72,1408]{1,0:T(8,128)(2,1)S(1)}, bf16[72,1408]{1,0:T(8,128)(2,1)S(1)}, u32[]{:S(2)}, u32[]{:S(2)}) %collective-permute-start.13) | collective-permute-done | bytes 202784 | tf_op jit(solution)/shard_map/ppermute | solution.py:232
  191.3 3.9 shard_map.109
  197.2 5.7 %collective-permute-done.14.incoming_ref = bf16[72,1408]{1,0:T(8,128)(2,1)S(1)} collective-permute-done((bf16[72,1408]{1,0:T(8,128)(2,1)S(1)}, bf16[72,1408]{1,0:T(8,128)(2,1)S(1)}, u32[]{:S(2)}, u32[]{:S(2)}) %collective-permute-start.14) | collective-permute-done | bytes 202784 | tf_op jit(solution)/shard_map/ppermute | solution.py:232
  202.9 3.9 shard_map.110
  208.8 5.7 %collective-permute-done.15.incoming_ref = bf16[72,1408]{1,0:T(8,128)(2,1)S(1)} collective-permute-done((bf16[72,1408]{1,0:T(8,128)(2,1)S(1)}, bf16[72,1408]{1,0:T(8,128)(2,1)S(1)}, u32[]{:S(2)}, u32[]{:S(2)}) %collective-permute-start.15) | collective-permute-done | bytes 202784 | tf_op jit(solution)/shard_map/ppermute | solution.py:232
  214.5 3.9 shard_map.111
  220.4 5.7 %collective-permute-done.16.incoming_ref = bf16[72,1408]{1,0:T(8,128)(2,1)S(1)} collective-permute-done((bf16[72,1408]{1,0:T(8,128)(2,1)S(1)}, bf16[72,1408]{1,0:T(8,128)(2,1)S(1)}, u32[]{:S(2)}, u32[]{:S(2)}) %collective-permute-start.16) | collective-permute-done | bytes 202784 | tf_op jit(solution)/shard_map/ppermute | solution.py:232
  226.1 3.9 shard_map.112
  232.0 4.8 %collective-permute-start.19 = (bf16[72,1408]{1,0:T(8,128)(2,1)S(1)}, bf16[72,1408]{1,0:T(8,128)(2,1)S(1)}, u32[]{:S(2)}, u32[]{:S(2)}) collective-permute-start(bf16[72,1408]{1,0:T(8,128)(2,1)S(1)} %get-tuple-element.94), channel_id=1, source_target_pairs={{0,7},{8,15},{16,23},{24,31},{32,39},{40,47},{48,55},{56,63},{64,7... | collective-permute-start | bytes 608264 | tf_op jit(solution)/shard_map/ppermute | solution.py:231
  237.7 3.9 shard_map.113
  244.9 4.4 %collective-permute-done.20.incoming_ref.fresh_ref = bf16[72,1408]{1,0:T(8,128)(2,1)S(1)} collective-permute-done((bf16[72,1408]{1,0:T(8,128)(2,1)S(1)}, bf16[72,1408]{1,0:T(8,128)(2,1)S(1)}, u32[]{:S(2)}, u32[]{:S(2)}) %collective-permute-start.20) | collective-permute-done | bytes 202784 | tf_op jit(solution)/shard_map/ppermute | solution.py:232
  249.3 3.9 shard_map.114
  255.2 5.7 %collective-permute-done.21.incoming_ref.fresh_ref = bf16[72,1408]{1,0:T(8,128)(2,1)S(1)} collective-permute-done((bf16[72,1408]{1,0:T(8,128)(2,1)S(1)}, bf16[72,1408]{1,0:T(8,128)(2,1)S(1)}, u32[]{:S(2)}, u32[]{:S(2)}) %collective-permute-start.21) | collective-permute-done | bytes 202784 | tf_op jit(solution)/shard_map/ppermute | solution.py:232
  260.9 3.9 shard_map.115
  266.4 15.4 %all-to-all-start.1 = ((bf16[4,32,2,1,1408]{4,0,2,3,1:T(4,128)(2,1)}), bf16[4,32,2,1,1408]{4,0,2,3,1:T(4,128)(2,1)S(1)}, u32[]{:S(2)}, u32[]{:S(2)}) async-start(bf16[4,32,2,1,1408]{4,0,2,3,1:T(4,128)(2,1)} %bitcast.105), calls=%async_computation.1 | async-start | bytes 1441792 | tf_op jit(solution)/shard_map/all_to_all | solution.py:176
  285.7 6.0 %collective-permute-start.22 = (bf16[72,1408]{1,0:T(8,128)(2,1)S(1)}, bf16[72,1408]{1,0:T(8,128)(2,1)S(1)}, u32[]{:S(2)}, u32[]{:S(2)}) collective-permute-start(bf16[72,1408]{1,0:T(8,128)(2,1)S(1)} %get-tuple-element.101), channel_id=1, source_target_pairs={{0,3},{8,11},{16,19},{24,27},{32,35},{40,43},{48,51},{56,59},{64,6... | collective-permute-start | bytes 608264 | tf_op jit(solution)/shard_map/ppermute | solution.py:231
  292.7 4.4 %copy-done.3 = bf16[4224,1408]{1,0:T(8,128)(2,1)S(1)} copy-done((bf16[4224,1408]{1,0:T(8,128)(2,1)S(1)}, bf16[4224,1408]{1,0:T(8,128)(2,1)}, u32[]{:S(2)}) %copy-start.3) | copy-done | bytes 11894808
  297.1 3.9 shard_map.116
  301.0 5.8 %collective-permute-start.27 = (bf16[72,1408]{1,0:T(8,128)(2,1)S(1)}, bf16[72,1408]{1,0:T(8,128)(2,1)S(1)}, u32[]{:S(2)}, u32[]{:S(2)}) collective-permute-start(bf16[72,1408]{1,0:T(8,128)(2,1)S(1)} %get-tuple-element.122), channel_id=1, source_target_pairs={{0,4},{8,12},{16,20},{24,28},{32,36},{40,44},{48,52},{56,60},{64,6... | collective-permute-start | bytes 608264 | tf_op jit(solution)/shard_map/ppermute | solution.py:231
  309.4 5.7 %collective-permute-done.25.incoming_ref.fresh_ref = bf16[72,1408]{1,0:T(8,128)(2,1)S(1)} collective-permute-done((bf16[72,1408]{1,0:T(8,128)(2,1)S(1)}, bf16[72,1408]{1,0:T(8,128)(2,1)S(1)}, u32[]{:S(2)}, u32[]{:S(2)}) %collective-permute-start.25) | collective-permute-done | bytes 202784 | tf_op jit(solution)/shard_map/ppermute | solution.py:232
  315.1 3.9 shard_map.117
  319.0 3.5 collective-permute-start.28
  327.7 4.4 %copy-done.4 = bf16[4224,1408]{1,0:T(8,128)(2,1)S(1)} copy-done((bf16[4224,1408]{1,0:T(8,128)(2,1)S(1)}, bf16[4224,1408]{1,0:T(8,128)(2,1)}, u32[]{:S(2)}) %copy-start.4) | copy-done | bytes 11894808
  332.0 3.9 shard_map.118
  343.0 11.2 %all-to-all-start.2 = ((bf16[3,32,2,1,1408]{4,2,0,3,1:T(2,128)(2,1)}), bf16[3,32,2,1,1408]{4,2,0,3,1:T(2,128)(2,1)S(1)}, u32[]{:S(2)}, u32[]{:S(2)}) async-start(bf16[3,32,2,1,1408]{4,2,0,3,1:T(2,128)(2,1)} %copy.29), calls=%async_computation.2 | async-start | bytes 1081344 | tf_op jit(solution)/shard_map/all_to_all | solution.py:176
  354.2 6.2 %reshape.62 = bf16[1408,1408]{1,0:T(8,128)(2,1)} reshape(bf16[64,22,1408]{2,1,0:T(8,128)(2,1)} %all-gather.8.cloned.1.call-done) | data formatting | bytes 7929856 | tf_op jit(solution)/shard_map/reshape | solution.py:242
  360.4 4.4 %copy-done.5 = bf16[4224,1408]{1,0:T(8,128)(2,1)S(1)} copy-done((bf16[4224,1408]{1,0:T(8,128)(2,1)S(1)}, bf16[4224,1408]{1,0:T(8,128)(2,1)}, u32[]{:S(2)}) %copy-start.5) | copy-done | bytes 11894808
  364.8 3.9 shard_map.119
  374.0 8.5 %all-to-all-start.3 = ((bf16[2,32,2,1,1408]{4,2,3,0,1:T(2,128)(2,1)}), bf16[2,32,2,1,1408]{4,2,3,0,1:T(2,128)(2,1)S(1)}, u32[]{:S(2)}, u32[]{:S(2)}) async-start(bf16[2,32,2,1,1408]{4,2,3,0,1:T(2,128)(2,1)} %pad_maximum_fusion), calls=%async_computation.3 | async-start | bytes 720896 | tf_op jit(solution)/shard_map/all_to_all | solution.py:176
  382.6 13.4 %all-to-all-done.3 = bf16[2,32,2,1,1408]{4,2,3,0,1:T(2,128)(2,1)S(1)} async-done(((bf16[2,32,2,1,1408]{4,2,3,0,1:T(2,128)(2,1)}), bf16[2,32,2,1,1408]{4,2,3,0,1:T(2,128)(2,1)S(1)}, u32[]{:S(2)}, u32[]{:S(2)}) %all-to-all-start.3) | async-done | bytes 360480 | tf_op jit(solution)/shard_map/all_to_all | solution.py:176
  399.8 3.8 collective-permute-start.31
  407.4 6.0 %collective-permute-start.36 = (bf16[16,1408]{1,0:T(8,128)(2,1)S(1)}, bf16[16,1408]{1,0:T(8,128)(2,1)S(1)}, u32[]{:S(2)}, u32[]{:S(2)}) collective-permute-start(bf16[16,1408]{1,0:T(8,128)(2,1)S(1)} %get-tuple-element.154), channel_id=1, source_target_pairs={{0,24},{8,32},{16,40},{24,48},{32,56},{40,64},{48,72},{56,80},{64,... | collective-permute-start | bytes 135176 | tf_op jit(solution)/shard_map/ppermute | solution.py:14
  419.2 3.4 fusion.29
  (188 shorter events, 88.9 us)
Async XLA Ops:
  7.2 105.9 %all-gather.6.cloned.1.call-start = ((), (), s32[]{:S(2)}) async-start(), calls=%async_computation.4 | async-start | bytes 6893568 | tf_op jit(solution)/shard_map/all_gather | solution.py:41
  8.3 9.7 %collective-permute-start = (bf16[66,768]{1,0:T(8,128)(2,1)S(1)}, bf16[66,768]{1,0:T(8,128)(2,1)S(1)}, u32[]{:S(2)}, u32[]{:S(2)}) collective-permute-start(bf16[66,768]{1,0:T(8,128)(2,1)S(1)} %get-tuple-element.152), channel_id=1, source_target_pairs={{0,8},{8,0},{16,24},{24,16},{32,40},{40,32},{48,56},{56,48},{64,72... | collective-permute-start | bytes 304136 | tf_op jit(solution)/shard_map/ppermute | solution.py:22
  19.7 13.8 %all-to-all-start = ((bf16[1,2,32,1408]{3,1,0,2:T(2,128)(2,1)}), bf16[1,2,32,1408]{3,1,0,2:T(2,128)(2,1)S(1)}, u32[]{:S(2)}, u32[]{:S(2)}) async-start(bf16[1,2,32,1408]{3,1,0,2:T(2,128)(2,1)} %copy.25), calls=%async_computation | async-start | bytes 360448 | tf_op jit(solution)/shard_map/all_to_all | solution.py:169
  23.6 304.1 %all-gather.8.cloned.1.call-start = ((), (), s32[]{:S(2)}) async-start(), calls=%async_computation.5 | async-start | bytes 4392960 | tf_op jit(solution)/shard_map/all_gather | solution.py:200
  33.6 6.1 %collective-permute-start.1 = (bf16[8,1408]{1,0:T(8,128)(2,1)S(1)}, bf16[8,1408]{1,0:T(8,128)(2,1)S(1)}, u32[]{:S(2)}, u32[]{:S(2)}) collective-permute-start(bf16[8,1408]{1,0:T(8,128)(2,1)S(1)} %select_n.159), channel_id=1, source_target_pairs={{0,256},{8,264},{16,272},{24,280},{32,288},{40,296},{48,304},{56,3... | collective-permute-start | bytes 67592 | tf_op jit(solution)/shard_map/ppermute | solution.py:184
  39.7 85.0 %copy-start.20 = (s32[1,1,64]{2,1,0:T(1,128)S(1)}, s32[1,1,64]{2,1,0:T(1,128)}, u32[]{:S(2)}) copy-start(s32[1,1,64]{2,1,0:T(1,128)} %param.17) | copy-start | bytes 772
  39.7 85.0 %copy-start.24 = (s32[1,1,64]{2,1,0:T(1,128)S(1)}, s32[1,1,64]{2,1,0:T(1,128)}, u32[]{:S(2)}) copy-start(s32[1,1,64]{2,1,0:T(1,128)} %param.16) | copy-start | bytes 772
  39.7 85.8 %copy-start.27 = (s32[1,1,4]{2,1,0:T(1,128)S(1)}, s32[1,1,4]{2,1,0:T(1,128)}, u32[]{:S(2)}) copy-start(s32[1,1,4]{2,1,0:T(1,128)} %param.18) | copy-start | bytes 52
  39.7 23.1 %collective-permute-start.2 = (bf16[72,1408]{1,0:T(8,128)(2,1)S(1)}, bf16[72,1408]{1,0:T(8,128)(2,1)S(1)}, u32[]{:S(2)}, u32[]{:S(2)}) collective-permute-start(bf16[72,1408]{1,0:T(8,128)(2,1)S(1)} %maximum_select_fusion.1.fresh_ref), channel_id=1, source_target_pairs={{6,0},{14,8},{22,16},{30,24},{38,32},{46,40},{54,48},{62,56},{70,6... | collective-permute-start | bytes 608264 | tf_op jit(solution)/shard_map/ppermute | solution.py:195
  41.1 22.9 %collective-permute-start.3 = (bf16[72,1408]{1,0:T(8,128)(2,1)S(1)}, bf16[72,1408]{1,0:T(8,128)(2,1)S(1)}, u32[]{:S(2)}, u32[]{:S(2)}) collective-permute-start(bf16[72,1408]{1,0:T(8,128)(2,1)S(1)} %maximum_select_fusion.1.fresh_ref), channel_id=1, source_target_pairs={{5,0},{13,8},{21,16},{29,24},{37,32},{45,40},{53,48},{61,56},{69,6... | collective-permute-start | bytes 608264 | tf_op jit(solution)/shard_map/ppermute | solution.py:195
  42.4 79.0 %collective-permute-start.4 = (bf16[72,1408]{1,0:T(8,128)(2,1)S(1)}, bf16[72,1408]{1,0:T(8,128)(2,1)S(1)}, u32[]{:S(2)}, u32[]{:S(2)}) collective-permute-start(bf16[72,1408]{1,0:T(8,128)(2,1)S(1)} %maximum_select_fusion.1.fresh_ref), channel_id=1, source_target_pairs={{4,0},{12,8},{20,16},{28,24},{36,32},{44,40},{52,48},{60,56},{68,6... | collective-permute-start | bytes 608264 | tf_op jit(solution)/shard_map/ppermute | solution.py:195
  43.7 77.7 %collective-permute-start.5 = (bf16[72,1408]{1,0:T(8,128)(2,1)S(1)}, bf16[72,1408]{1,0:T(8,128)(2,1)S(1)}, u32[]{:S(2)}, u32[]{:S(2)}) collective-permute-start(bf16[72,1408]{1,0:T(8,128)(2,1)S(1)} %maximum_select_fusion.1.fresh_ref), channel_id=1, source_target_pairs={{3,0},{11,8},{19,16},{27,24},{35,32},{43,40},{51,48},{59,56},{67,6... | collective-permute-start | bytes 608264 | tf_op jit(solution)/shard_map/ppermute | solution.py:195
  45.0 76.4 %collective-permute-start.6 = (bf16[72,1408]{1,0:T(8,128)(2,1)S(1)}, bf16[72,1408]{1,0:T(8,128)(2,1)S(1)}, u32[]{:S(2)}, u32[]{:S(2)}) collective-permute-start(bf16[72,1408]{1,0:T(8,128)(2,1)S(1)} %maximum_select_fusion.1.fresh_ref), channel_id=1, source_target_pairs={{2,0},{10,8},{18,16},{26,24},{34,32},{42,40},{50,48},{58,56},{66,6... | collective-permute-start | bytes 608264 | tf_op jit(solution)/shard_map/ppermute | solution.py:195
  62.8 58.7 %collective-permute-start.7 = (bf16[72,1408]{1,0:T(8,128)(2,1)S(1)}, bf16[72,1408]{1,0:T(8,128)(2,1)S(1)}, u32[]{:S(2)}, u32[]{:S(2)}) collective-permute-start(bf16[72,1408]{1,0:T(8,128)(2,1)S(1)} %maximum_select_fusion.1.fresh_ref), channel_id=1, source_target_pairs={{1,0},{9,8},{17,16},{25,24},{33,32},{41,40},{49,48},{57,56},{65,64... | collective-permute-start | bytes 608264 | tf_op jit(solution)/shard_map/ppermute | solution.py:195
  64.1 57.4 %collective-permute-start.8 = (bf16[72,1408]{1,0:T(8,128)(2,1)S(1)}, bf16[72,1408]{1,0:T(8,128)(2,1)S(1)}, u32[]{:S(2)}, u32[]{:S(2)}) collective-permute-start(bf16[72,1408]{1,0:T(8,128)(2,1)S(1)} %maximum_select_fusion.1.fresh_ref), channel_id=1, source_target_pairs={{7,0},{15,8},{23,16},{31,24},{39,32},{47,40},{55,48},{63,56},{71,6... | collective-permute-start | bytes 608264 | tf_op jit(solution)/shard_map/ppermute | solution.py:195
  121.5 13.3 %collective-permute-start.9 = (bf16[4224,768]{1,0:T(8,128)(2,1)}, bf16[4224,768]{1,0:T(8,128)(2,1)}, u32[]{:S(2)}, u32[]{:S(2)}) collective-permute-start(bf16[4224,768]{1,0:T(8,128)(2,1)} %reshape.83.mine_ref), channel_id=1, source_target_pairs={{0,8},{8,0},{16,24},{24,16},{32,40},{40,32},{48,56},{56,48},{64,72... | collective-permute-start | bytes 19464200 | tf_op jit(solution)/shard_map/ppermute | solution.py:22
  140.6 120.3 %copy-start.2 = (bf16[4224,1408]{1,0:T(8,128)(2,1)}, bf16[4224,1408]{1,0:T(8,128)(2,1)S(1)}, u32[]{:S(2)}) copy-start(bf16[4224,1408]{1,0:T(8,128)(2,1)S(1)} %shard_map.104.weights_ref) | copy-start | bytes 35684356
  144.5 10.6 %collective-permute-start.10 = (bf16[72,1408]{1,0:T(8,128)(2,1)S(1)}, bf16[72,1408]{1,0:T(8,128)(2,1)S(1)}, u32[]{:S(2)}, u32[]{:S(2)}) collective-permute-start(bf16[72,1408]{1,0:T(8,128)(2,1)S(1)} %get-tuple-element.136), channel_id=1, source_target_pairs={{0,1},{1,2},{2,3},{3,4},{4,5},{5,6},{6,7},{7,0},{8,9},{9,10},{10,1... | collective-permute-start | bytes 608264 | tf_op jit(solution)/shard_map/ppermute | solution.py:232
  159.0 8.7 %collective-permute-start.11 = (bf16[72,1408]{1,0:T(8,128)(2,1)S(1)}, bf16[72,1408]{1,0:T(8,128)(2,1)S(1)}, u32[]{:S(2)}, u32[]{:S(2)}) collective-permute-start(bf16[72,1408]{1,0:T(8,128)(2,1)S(1)} %get-tuple-element.109), channel_id=1, source_target_pairs={{0,1},{1,2},{2,3},{3,4},{4,5},{5,6},{6,7},{7,0},{8,9},{9,10},{10,1... | collective-permute-start | bytes 608264 | tf_op jit(solution)/shard_map/ppermute | solution.py:232
  171.6 7.7 %collective-permute-start.12 = (bf16[72,1408]{1,0:T(8,128)(2,1)S(1)}, bf16[72,1408]{1,0:T(8,128)(2,1)S(1)}, u32[]{:S(2)}, u32[]{:S(2)}) collective-permute-start(bf16[72,1408]{1,0:T(8,128)(2,1)S(1)} %get-tuple-element.122), channel_id=1, source_target_pairs={{0,1},{1,2},{2,3},{3,4},{4,5},{5,6},{6,7},{7,0},{8,9},{9,10},{10,1... | collective-permute-start | bytes 608264 | tf_op jit(solution)/shard_map/ppermute | solution.py:232
  183.2 8.1 %collective-permute-start.13 = (bf16[72,1408]{1,0:T(8,128)(2,1)S(1)}, bf16[72,1408]{1,0:T(8,128)(2,1)S(1)}, u32[]{:S(2)}, u32[]{:S(2)}) collective-permute-start(bf16[72,1408]{1,0:T(8,128)(2,1)S(1)} %get-tuple-element.101), channel_id=1, source_target_pairs={{0,1},{1,2},{2,3},{3,4},{4,5},{5,6},{6,7},{7,0},{8,9},{9,10},{10,1... | collective-permute-start | bytes 608264 | tf_op jit(solution)/shard_map/ppermute | solution.py:232
  195.2 7.7 %collective-permute-start.14 = (bf16[72,1408]{1,0:T(8,128)(2,1)S(1)}, bf16[72,1408]{1,0:T(8,128)(2,1)S(1)}, u32[]{:S(2)}, u32[]{:S(2)}) collective-permute-start(bf16[72,1408]{1,0:T(8,128)(2,1)S(1)} %get-tuple-element.102), channel_id=1, source_target_pairs={{0,1},{1,2},{2,3},{3,4},{4,5},{5,6},{6,7},{7,0},{8,9},{9,10},{10,1... | collective-permute-start | bytes 608264 | tf_op jit(solution)/shard_map/ppermute | solution.py:232
  206.8 7.7 %collective-permute-start.15 = (bf16[72,1408]{1,0:T(8,128)(2,1)S(1)}, bf16[72,1408]{1,0:T(8,128)(2,1)S(1)}, u32[]{:S(2)}, u32[]{:S(2)}) collective-permute-start(bf16[72,1408]{1,0:T(8,128)(2,1)S(1)} %get-tuple-element.93), channel_id=1, source_target_pairs={{0,1},{1,2},{2,3},{3,4},{4,5},{5,6},{6,7},{7,0},{8,9},{9,10},{10,1... | collective-permute-start | bytes 608264 | tf_op jit(solution)/shard_map/ppermute | solution.py:232
  218.4 7.7 %collective-permute-start.16 = (bf16[72,1408]{1,0:T(8,128)(2,1)S(1)}, bf16[72,1408]{1,0:T(8,128)(2,1)S(1)}, u32[]{:S(2)}, u32[]{:S(2)}) collective-permute-start(bf16[72,1408]{1,0:T(8,128)(2,1)S(1)} %get-tuple-element.88), channel_id=1, source_target_pairs={{0,1},{1,2},{2,3},{3,4},{4,5},{5,6},{6,7},{7,0},{8,9},{9,10},{10,1... | collective-permute-start | bytes 608264 | tf_op jit(solution)/shard_map/ppermute | solution.py:232
  230.0 7.7 %collective-permute-start.17 = (bf16[72,1408]{1,0:T(8,128)(2,1)S(1)}, bf16[72,1408]{1,0:T(8,128)(2,1)S(1)}, u32[]{:S(2)}, u32[]{:S(2)}) collective-permute-start(bf16[72,1408]{1,0:T(8,128)(2,1)S(1)} %get-tuple-element.94), channel_id=1, source_target_pairs={{0,1},{1,2},{2,3},{3,4},{4,5},{5,6},{6,7},{7,0},{8,9},{9,10},{10,1... | collective-permute-start | bytes 608264 | tf_op jit(solution)/shard_map/ppermute | solution.py:232
  232.0 13.0 %collective-permute-start.19 = (bf16[72,1408]{1,0:T(8,128)(2,1)S(1)}, bf16[72,1408]{1,0:T(8,128)(2,1)S(1)}, u32[]{:S(2)}, u32[]{:S(2)}) collective-permute-start(bf16[72,1408]{1,0:T(8,128)(2,1)S(1)} %get-tuple-element.94), channel_id=1, source_target_pairs={{0,7},{8,15},{16,23},{24,31},{32,39},{40,47},{48,55},{56,63},{64,7... | collective-permute-start | bytes 608264 | tf_op jit(solution)/shard_map/ppermute | solution.py:231
  241.6 7.7 %collective-permute-start.20 = (bf16[72,1408]{1,0:T(8,128)(2,1)S(1)}, bf16[72,1408]{1,0:T(8,128)(2,1)S(1)}, u32[]{:S(2)}, u32[]{:S(2)}) collective-permute-start(bf16[72,1408]{1,0:T(8,128)(2,1)S(1)} %get-tuple-element.95), channel_id=1, source_target_pairs={{0,1},{1,2},{2,3},{3,4},{4,5},{5,6},{6,7},{7,0},{8,9},{9,10},{10,1... | collective-permute-start | bytes 608264 | tf_op jit(solution)/shard_map/ppermute | solution.py:232
  243.6 11.6 %collective-permute-start.18 = (bf16[72,1408]{1,0:T(8,128)(2,1)S(1)}, bf16[72,1408]{1,0:T(8,128)(2,1)S(1)}, u32[]{:S(2)}, u32[]{:S(2)}) collective-permute-start(bf16[72,1408]{1,0:T(8,128)(2,1)S(1)} %get-tuple-element.93), channel_id=1, source_target_pairs={{0,1},{8,9},{16,17},{24,25},{32,33},{40,41},{48,49},{56,57},{64,65... | collective-permute-start | bytes 608264 | tf_op jit(solution)/shard_map/ppermute | solution.py:231
  253.2 7.7 %collective-permute-start.21 = (bf16[72,1408]{1,0:T(8,128)(2,1)S(1)}, bf16[72,1408]{1,0:T(8,128)(2,1)S(1)}, u32[]{:S(2)}, u32[]{:S(2)}) collective-permute-start(bf16[72,1408]{1,0:T(8,128)(2,1)S(1)} %get-tuple-element.98), channel_id=1, source_target_pairs={{0,1},{1,2},{2,3},{3,4},{4,5},{5,6},{6,7},{7,0},{8,9},{9,10},{10,1... | collective-permute-start | bytes 608264 | tf_op jit(solution)/shard_map/ppermute | solution.py:232
  265.0 20.2 %copy-start.28 = (f32[1,1,64]{2,1,0:T(1,128)S(1)}, f32[1,1,64]{2,1,0:T(1,128)}, u32[]{:S(2)}) copy-start(f32[1,1,64]{2,1,0:T(1,128)} %param.19) | copy-start | bytes 772
  266.4 60.3 %all-to-all-start.1 = ((bf16[4,32,2,1,1408]{4,0,2,3,1:T(4,128)(2,1)}), bf16[4,32,2,1,1408]{4,0,2,3,1:T(4,128)(2,1)S(1)}, u32[]{:S(2)}, u32[]{:S(2)}) async-start(bf16[4,32,2,1,1408]{4,0,2,3,1:T(4,128)(2,1)} %bitcast.105), calls=%async_computation.1 | async-start | bytes 1441792 | tf_op jit(solution)/shard_map/all_to_all | solution.py:176
  281.9 9.9 %collective-permute-start.23 = (bf16[72,1408]{1,0:T(8,128)(2,1)S(1)}, bf16[72,1408]{1,0:T(8,128)(2,1)S(1)}, u32[]{:S(2)}, u32[]{:S(2)}) collective-permute-start(bf16[72,1408]{1,0:T(8,128)(2,1)S(1)} %get-tuple-element.102), channel_id=1, source_target_pairs={{0,2},{8,10},{16,18},{24,26},{32,34},{40,42},{48,50},{56,58},{64,6... | collective-permute-start | bytes 608264 | tf_op jit(solution)/shard_map/ppermute | solution.py:231
  283.2 9.5 %collective-permute-start.24 = (bf16[72,1408]{1,0:T(8,128)(2,1)S(1)}, bf16[72,1408]{1,0:T(8,128)(2,1)S(1)}, u32[]{:S(2)}, u32[]{:S(2)}) collective-permute-start(bf16[72,1408]{1,0:T(8,128)(2,1)S(1)} %get-tuple-element.103), channel_id=1, source_target_pairs={{0,1},{1,2},{2,3},{3,4},{4,5},{5,6},{6,7},{7,0},{8,9},{9,10},{10,1... | collective-permute-start | bytes 608264 | tf_op jit(solution)/shard_map/ppermute | solution.py:232
  285.7 23.7 %collective-permute-start.22 = (bf16[72,1408]{1,0:T(8,128)(2,1)S(1)}, bf16[72,1408]{1,0:T(8,128)(2,1)S(1)}, u32[]{:S(2)}, u32[]{:S(2)}) collective-permute-start(bf16[72,1408]{1,0:T(8,128)(2,1)S(1)} %get-tuple-element.101), channel_id=1, source_target_pairs={{0,3},{8,11},{16,19},{24,27},{32,35},{40,43},{48,51},{56,59},{64,6... | collective-permute-start | bytes 608264 | tf_op jit(solution)/shard_map/ppermute | solution.py:231
  301.0 24.2 %collective-permute-start.27 = (bf16[72,1408]{1,0:T(8,128)(2,1)S(1)}, bf16[72,1408]{1,0:T(8,128)(2,1)S(1)}, u32[]{:S(2)}, u32[]{:S(2)}) collective-permute-start(bf16[72,1408]{1,0:T(8,128)(2,1)S(1)} %get-tuple-element.122), channel_id=1, source_target_pairs={{0,4},{8,12},{16,20},{24,28},{32,36},{40,44},{48,52},{56,60},{64,6... | collective-permute-start | bytes 608264 | tf_op jit(solution)/shard_map/ppermute | solution.py:231
  306.8 8.3 %collective-permute-start.25 = (bf16[72,1408]{1,0:T(8,128)(2,1)S(1)}, bf16[72,1408]{1,0:T(8,128)(2,1)S(1)}, u32[]{:S(2)}, u32[]{:S(2)}) collective-permute-start(bf16[72,1408]{1,0:T(8,128)(2,1)S(1)} %get-tuple-element.106), channel_id=1, source_target_pairs={{0,1},{1,2},{2,3},{3,4},{4,5},{5,6},{6,7},{7,0},{8,9},{9,10},{10,1... | collective-permute-start | bytes 608264 | tf_op jit(solution)/shard_map/ppermute | solution.py:232
  319.0 7.7 %collective-permute-start.28 = (bf16[72,1408]{1,0:T(8,128)(2,1)S(1)}, bf16[72,1408]{1,0:T(8,128)(2,1)S(1)}, u32[]{:S(2)}, u32[]{:S(2)}) collective-permute-start(bf16[72,1408]{1,0:T(8,128)(2,1)S(1)} %get-tuple-element.123), channel_id=1, source_target_pairs={{0,1},{1,2},{2,3},{3,4},{4,5},{5,6},{6,7},{7,0},{8,9},{9,10},{10,1... | collective-permute-start | bytes 608264 | tf_op jit(solution)/shard_map/ppermute | solution.py:232
  322.5 37.9 %collective-permute-start.26 = (bf16[72,1408]{1,0:T(8,128)(2,1)S(1)}, bf16[72,1408]{1,0:T(8,128)(2,1)}, u32[]{:S(2)}, u32[]{:S(2)}) collective-permute-start(bf16[72,1408]{1,0:T(8,128)(2,1)S(1)} %get-tuple-element.109), channel_id=1, source_target_pairs={{0,5},{8,13},{16,21},{24,29},{32,37},{40,45},{48,53},{56,61},{64,6... | collective-permute-start | bytes 608264 | tf_op jit(solution)/shard_map/ppermute | solution.py:231
  336.0 33.0 %collective-permute-start.30 = (bf16[72,1408]{1,0:T(8,128)(2,1)S(1)}, bf16[72,1408]{1,0:T(8,128)(2,1)}, u32[]{:S(2)}, u32[]{:S(2)}) collective-permute-start(bf16[72,1408]{1,0:T(8,128)(2,1)S(1)} %get-tuple-element.136), channel_id=1, source_target_pairs={{0,6},{8,14},{16,22},{24,30},{32,38},{40,46},{48,54},{56,62},{64,7... | collective-permute-start | bytes 608264 | tf_op jit(solution)/shard_map/ppermute | solution.py:231
  337.9 22.5 %collective-permute-start.29 = (bf16[72,1408]{1,0:T(8,128)(2,1)S(1)}, bf16[72,1408]{1,0:T(8,128)(2,1)S(1)}, u32[]{:S(2)}, u32[]{:S(2)}) collective-permute-start(bf16[72,1408]{1,0:T(8,128)(2,1)S(1)} %get-tuple-element.127), channel_id=1, source_target_pairs={{0,1},{1,2},{2,3},{3,4},{4,5},{5,6},{6,7},{7,0},{8,9},{9,10},{10,1... | collective-permute-start | bytes 608264 | tf_op jit(solution)/shard_map/ppermute | solution.py:232
  343.0 28.7 %all-to-all-start.2 = ((bf16[3,32,2,1,1408]{4,2,0,3,1:T(2,128)(2,1)}), bf16[3,32,2,1,1408]{4,2,0,3,1:T(2,128)(2,1)S(1)}, u32[]{:S(2)}, u32[]{:S(2)}) async-start(bf16[3,32,2,1,1408]{4,2,0,3,1:T(2,128)(2,1)} %copy.29), calls=%async_computation.2 | async-start | bytes 1081344 | tf_op jit(solution)/shard_map/all_to_all | solution.py:176
  374.0 22.1 %all-to-all-start.3 = ((bf16[2,32,2,1,1408]{4,2,3,0,1:T(2,128)(2,1)}), bf16[2,32,2,1,1408]{4,2,3,0,1:T(2,128)(2,1)S(1)}, u32[]{:S(2)}, u32[]{:S(2)}) async-start(bf16[2,32,2,1,1408]{4,2,3,0,1:T(2,128)(2,1)} %pad_maximum_fusion), calls=%async_computation.3 | async-start | bytes 720896 | tf_op jit(solution)/shard_map/all_to_all | solution.py:176
  397.2 19.6 %collective-permute-start.33 = (bf16[16,1408]{1,0:T(8,128)(2,1)S(1)}, bf16[16,1408]{1,0:T(8,128)(2,1)S(1)}, u32[]{:S(2)}, u32[]{:S(2)}) collective-permute-start(bf16[16,1408]{1,0:T(8,128)(2,1)S(1)} %get-tuple-element.158), channel_id=1, source_target_pairs={{24,0},{32,8},{40,16},{48,24},{56,32},{64,40},{72,48},{80,56},{88,... | collective-permute-start | bytes 135176 | tf_op jit(solution)/shard_map/ppermute | solution.py:14
  398.5 20.2 %collective-permute-start.32 = (bf16[16,1408]{1,0:T(8,128)(2,1)S(1)}, bf16[16,1408]{1,0:T(8,128)(2,1)S(1)}, u32[]{:S(2)}, u32[]{:S(2)}) collective-permute-start(bf16[16,1408]{1,0:T(8,128)(2,1)S(1)} %get-tuple-element.159), channel_id=1, source_target_pairs={{16,0},{24,8},{32,16},{40,24},{48,32},{56,40},{64,48},{72,56},{80,... | collective-permute-start | bytes 135176 | tf_op jit(solution)/shard_map/ppermute | solution.py:14
  399.8 18.9 %collective-permute-start.31 = (bf16[16,1408]{1,0:T(8,128)(2,1)S(1)}, bf16[16,1408]{1,0:T(8,128)(2,1)S(1)}, u32[]{:S(2)}, u32[]{:S(2)}) collective-permute-start(bf16[16,1408]{1,0:T(8,128)(2,1)S(1)} %get-tuple-element.160), channel_id=1, source_target_pairs={{8,0},{16,8},{24,16},{32,24},{40,32},{48,40},{56,48},{64,56},{72,6... | collective-permute-start | bytes 135176 | tf_op jit(solution)/shard_map/ppermute | solution.py:14
  407.4 15.2 %collective-permute-start.36 = (bf16[16,1408]{1,0:T(8,128)(2,1)S(1)}, bf16[16,1408]{1,0:T(8,128)(2,1)S(1)}, u32[]{:S(2)}, u32[]{:S(2)}) collective-permute-start(bf16[16,1408]{1,0:T(8,128)(2,1)S(1)} %get-tuple-element.154), channel_id=1, source_target_pairs={{0,24},{8,32},{16,40},{24,48},{32,56},{40,64},{48,72},{56,80},{64,... | collective-permute-start | bytes 135176 | tf_op jit(solution)/shard_map/ppermute | solution.py:14
  413.4 9.3 %collective-permute-start.35 = (bf16[16,1408]{1,0:T(8,128)(2,1)S(1)}, bf16[16,1408]{1,0:T(8,128)(2,1)S(1)}, u32[]{:S(2)}, u32[]{:S(2)}) collective-permute-start(bf16[16,1408]{1,0:T(8,128)(2,1)S(1)} %get-tuple-element.155), channel_id=1, source_target_pairs={{0,16},{8,24},{16,32},{24,40},{32,48},{40,56},{48,64},{56,72},{64,... | collective-permute-start | bytes 135176 | tf_op jit(solution)/shard_map/ppermute | solution.py:14
  416.8 5.9 %collective-permute-start.34 = (bf16[16,1408]{1,0:T(8,128)(2,1)S(1)}, bf16[16,1408]{1,0:T(8,128)(2,1)S(1)}, u32[]{:S(2)}, u32[]{:S(2)}) collective-permute-start(bf16[16,1408]{1,0:T(8,128)(2,1)S(1)} %get-tuple-element.156), channel_id=1, source_target_pairs={{0,8},{8,16},{16,24},{24,32},{32,40},{40,48},{48,56},{56,64},{64,7... | collective-permute-start | bytes 135176 | tf_op jit(solution)/shard_map/ppermute | solution.py:14
  (24 other events, 130.1 us)
Sparse Core Ops, SparseCore 0:
  18.9 94.1 all-gather.5
  125.5 82.1 all-gather.7

commit v2 on v1

--- a/solution.py
+++ b/solution.py
@@ -78,7 +78,7 @@
         scratch_shapes=[pltpu.SemaphoreType.DMA((2,))],
         compiler_params=pltpu.CompilerParams(vmem_limit_bytes=16 << 20),
         cost_estimate=pl.CostEstimate(flops=0, bytes_accessed=2 * rows * columns * 2, transcendentals=0),
-    )(core, mine, other)
+    )(core, *(pltpu.with_memory_space_constraint(part, pltpu.HBM) for part in (mine, other)))
 
 
 def block_kernel(
@@ -87,7 +87,7 @@
     rows, channels = incoming_ref.shape
     kept_rows = own_ref.shape[0]
     padded_rows = taps_ref.shape[0]
-    fresh, low_half, forward = (flags_ref[i] != 0 for i in range(3))
+    fresh, low_half = (flags_ref[i] != 0 for i in range(2))
     acts = jnp.where(fresh, fresh_ref[...].astype(jnp.float32), incoming_ref[...].astype(jnp.float32))
     acts_ref[...] = acts
     normed = rms_scaled(acts, gain_ref[...])
@@ -101,8 +101,7 @@
         result = acts_ref[:, at] + jax.nn.gelu(mixed[:rows])
         own = jnp.where(low_half, result[:kept_rows], result[rows - kept_rows :])
         own_ref[:, at] = own.astype(jnp.bfloat16)
-        sent = jnp.where(forward, incoming_ref[:, at].astype(jnp.float32), result)
-        result_ref[:, at] = sent.astype(jnp.bfloat16)
+        result_ref[:, at] = result.astype(jnp.bfloat16)
 
     whole = channels // wide_columns
 
@@ -191,69 +190,57 @@
         jnp.concatenate([chains, edge], axis=0),
         jnp.concatenate([edge, chains], axis=0),
     )
-    order = list(range(last - 1, -1, -1)) + [last]
-    fresh = [wide if m == 0 else lax.ppermute(wide, "section", [(m, 0)]) for m in order]
+    fresh = [wide if m == 0 else lax.ppermute(wide, "section", [(m, 0)]) for m in range(micro_count)]
     weight_part, *fresh = lax.optimization_barrier((weight_part, *fresh))
     core = (lax.axis_index("seq") % 2).astype(jnp.int32)
     weights = placed_weights(core[None], weight_part, core_swap(weight_part), channels)
     head_weight, weight_part = lax.optimization_barrier((head_weight, weight_part))
     head_parts = lax.all_gather(head_weight, "seq")
 
-    ticks = micro_count + last
     def gathered_outputs(owns, first, count):
-        held = jnp.stack(owns[first : first + count + last])
-        return lax.dynamic_slice_in_dim(held, section_pos, count, 0)
-
-    early = micro_count // 2
-    results, owns, landing = [], [], []
-    skip_input = 0.0
-    incoming = jnp.zeros_like(wide)
+        held = jnp.stack([jnp.stack(pair) for pair in owns[first : first + count + last]])
+        taken = lax.dynamic_slice_in_dim(held, section_pos, count, 0)
+        return taken.reshape(2 * count, slab_rows, channels)
+
+    pairs = micro_count // 2
+    ticks = pairs + last
+    early = pairs // 2
+    flags = jnp.stack([section_pos == 0, low_half]).astype(jnp.int32)
+    results, owns, landing, landed = [], [], [], []
+    incoming = [jnp.zeros_like(wide)] * 2
     for tick in range(ticks):
-        rank = tick - section_pos
-        flags = jnp.stack(
-            [
-                (section_pos == 0) & (tick < micro_count),
-                low_half,
-                rank >= micro_count,
-            ]
-        ).astype(jnp.int32)
-        result, own = block(
-            flags, weights, section_gain, incoming, fresh[tick] if tick < micro_count else incoming, slab_rows
-        )
-        results.append(result)
-        owns.append(own)
-        if tick == ticks - 1:
-            final = jnp.where(section_pos == last, result, incoming)
-            break
-        if tick >= micro_count - 1:
-            home = tick - micro_count + 1 or last
-            skip, result = lax.optimization_barrier((results[order.index(home)], result))
-            landing.append(lax.ppermute(skip, "section", [(0, home)]))
-        incoming = lax.ppermute(
-            result, "section", [(i, (i + 1) % sections) for i in range(sections)]
-        )
-        if len(landing) > 1:
-            landed, incoming = lax.optimization_barrier((landing.pop(0), incoming))
-            skip_input = skip_input + landed.astype(jnp.float32)
+        owns.append([])
+        for lane in range(2):
+            entered = 2 * tick + lane
+            before = incoming[lane]
+            if results:
+                before, _ = lax.optimization_barrier((before, results[-1]))
+            if len(landing) > 2:
+                arrived, before = lax.optimization_barrier((landing.pop(0), before))
+                landed.append(arrived)
+            now = fresh[entered] if entered < micro_count else before
+            result, own = block(flags, weights, section_gain, before, now, slab_rows)
+            results.append(result)
+            owns[-1].append(own)
+            if tick < ticks - 1:
+                incoming[lane] = lax.ppermute(result, "section", [(i, i + 1) for i in range(last)])
+            done = entered - 2 * last
+            if 0 <= done < micro_count - 1:
+                leaving = jnp.where(section_pos == 0, results[done + 1], result)
+                landing.append(lax.ppermute(leaving, "section", [(last, done), (0, done + 1)]))
         if tick == early - 1 + last:
             early_rows = to_slabs(gathered_outputs(owns, 0, early))
-        if tick == early + 1 + last:
-            head_parts, early_rows, incoming = lax.optimization_barrier((head_parts, early_rows, incoming))
-            head_full = head_parts.reshape(channels, channels)
-        if tick == ticks - 2:
-            late_rows = to_slabs(gathered_outputs(owns, early, last - early))
-    for landed in landing:
-        skip_input = skip_input + landed.astype(jnp.float32)
-    skip_input = skip_input + jnp.where(section_pos == 0, results[order.index(0)], 0).astype(jnp.float32)
-    head_input = final.astype(jnp.float32) + skip_input
+    head_input = sum(rows.astype(jnp.float32) for rows in landed + landing)
+    head_input = head_input + jnp.where(section_pos == 0, results[0], 0).astype(jnp.float32)
+    head_input = head_input + jnp.where(section_pos == last, results[-1], 0).astype(jnp.float32)
     embed = own_rows(rms_scaled(head_input, head_gain).astype(jnp.bfloat16))
-    newest = functools.reduce(
-        lambda total, s: jnp.where(section_pos == s, owns[last + s], total), range(1, sections), owns[last]
-    )
-    embed, late_rows = lax.optimization_barrier((embed, late_rows))
-    embed, newest_rows = to_slabs(jnp.stack([embed, newest]))
-    entered = jnp.concatenate([early_rows, late_rows, newest_rows[None]], axis=0)
-    stashed = jnp.stack([entered[order.index(m)] for m in range(micro_count)])
+    embed, head_parts, early_rows = lax.optimization_barrier((embed, head_parts, early_rows))
+    head_full = head_parts.reshape(channels, channels)
+    embed = to_slabs(embed)
+    late_outputs = gathered_outputs(owns, early, pairs - early)
+    embed, late_outputs = lax.optimization_barrier((embed, late_outputs))
+    late_rows = to_slabs(late_outputs)
+    stashed = jnp.concatenate([early_rows, late_rows], axis=0)
 
     scale = channels ** (-0.5)
     reach_count = pair_count.shape[2]

time: 432 us -> 390 us (0.903)
  waiting for transfers between devices: 162 us -> 94.7 us
  Pallas kernels: 61.4 us -> 90 us
  local copies, waits for them, and re-layouts: 42.8 us -> 28.4 us
  starting transfers between devices: 134 us -> 142 us
    ppermute x21 -> x27, waiting for transfers between devices: 62.2 us -> 3.91 us  [the longest x7 3.86 us: on_device(): lax.ppermute(leaving, 'section', [(last, done), (0, done + 1)])]
    pallas_call x15 -> x22, Pallas kernels: 58.5 us -> 85.5 us  [block(): pl.pallas_call(functools.partial(block_kernel, 256), out_shape=(jax.Shape...]
    all_gather x1, waiting for transfers between devices: 47.8 us -> 63.2 us  [gathered_columns(): lax.all_gather(rows, 'seq', axis_index_groups=same_core, axis=0, tiled=True)]
    ppermute x7, waiting for transfers between devices: 16.4 us -> 0.99 us  [on_device(): lax.ppermute(wide, 'section', [(m, 0)])]
    unnamed x78 -> x26, local copies, waits for them, and re-layouts: 19.6 us -> 6.16 us
    all_to_all x3, waiting for transfers between devices: 13.5 us -> 1.66 us  [to_slabs(): rows = lax.all_to_all(blocks, 'seq', at, at + 1, axis_index_groups=halves)]
    ppermute x21 -> x27, starting transfers between devices: 53 us -> 63.7 us  [the longest x20 50.2 us: on_device(): lax.ppermute(result, 'section', [(i, i + 1) for i in range(last)])]
  transfers between devices with their start and end apart: 43 -> 49, of which waited for: 20 -> 11; matrix products, arithmetic and copies ran while one was open for 8% -> 9% of each run, Pallas kernels for 14% -> 23%
where the time goes in v2:
time: 390 us; the launch traced here: 387 us
  starting transfers between devices  142 us (36%)
  waiting for transfers between devices  94.7 us (24%)
  Pallas kernels  90 us (23%)
  local copies, waits for them, and re-layouts  28.4 us (7%)
  between operations  15.2 us (4%)
  other arithmetic  9.05 us (2%)
  matrix products  7.68 us (2%)
    pallas_call x22, Pallas kernels, block(): pl.pallas_call(functools.partial(block_kernel, 256), out_shape=(jax.Shape...  85.5 us
    all_gather x1, waiting for transfers between devices, gathered_columns(): lax.all_gather(rows, 'seq', axis_index_groups=same_core, axis=0, tiled=True)  63.2 us
    ppermute x20, starting transfers between devices, on_device(): lax.ppermute(result, 'section', [(i, i + 1) for i in range(last)])  50.2 us
    all_to_all x3, starting transfers between devices, to_slabs(): rows = lax.all_to_all(blocks, 'seq', at, at + 1, axis_index_groups=halves)  34.2 us
    ppermute x6, starting transfers between devices, from_behind(): return lax.ppermute(shard, axis, pairs)  16 us
    ppermute x7, starting transfers between devices, on_device(): lax.ppermute(leaving, 'section', [(last, done), (0, done + 1)])  13.6 us
    ppermute x2, starting transfers between devices, core_swap(): lax.ppermute(shard, 'seq', [(i, i ^ 1) for i in range(lax.axis_size('seq'...  11.7 us
    ppermute x2, waiting for transfers between devices, core_swap(): lax.ppermute(shard, 'seq', [(i, i ^ 1) for i in range(lax.axis_size('seq'...  11 us
  transfers between devices with their start and end apart: 49, of which 11 were waited for; matrix products, arithmetic and copies ran while one was open for 9% of the time, Pallas kernels for 23%

profile of v2, /device:TPU:1, one launch (start us, length us, event | category | flops | bytes accessed | tf_op | source)
XLA Modules:
  0.0 387.4 jit_solution(2547469349163443041)
XLA Ops:
  8.3 8.8 %collective-permute-start = (bf16[66,768]{1,0:T(8,128)(2,1)S(1)}, bf16[66,768]{1,0:T(8,128)(2,1)S(1)}, u32[]{:S(2)}, u32[]{:S(2)}) collective-permute-start(bf16[66,768]{1,0:T(8,128)(2,1)S(1)} %get-tuple-element.200), channel_id=1, source_target_pairs={{0,8},{8,0},{16,24},{24,16},{32,40},{40,32},{48,56},{56,48},{64,72... | collective-permute-start | bytes 304136 | tf_op jit(solution)/shard_map/ppermute | solution.py:22
  19.7 3.9 %all-to-all-start = ((bf16[1,2,32,1408]{3,1,0,2:T(2,128)(2,1)}), bf16[1,2,32,1408]{3,1,0,2:T(2,128)(2,1)S(1)}, u32[]{:S(2)}, u32[]{:S(2)}) async-start(bf16[1,2,32,1408]{3,1,0,2:T(2,128)(2,1)} %copy.21), calls=%async_computation | async-start | bytes 360448 | tf_op jit(solution)/shard_map/all_to_all | solution.py:168
  23.6 9.9 %all-to-all-done = bf16[1,2,32,1408]{3,1,0,2:T(2,128)(2,1)S(1)} async-done(((bf16[1,2,32,1408]{3,1,0,2:T(2,128)(2,1)}), bf16[1,2,32,1408]{3,1,0,2:T(2,128)(2,1)S(1)}, u32[]{:S(2)}, u32[]{:S(2)}) %all-to-all-start) | async-done | bytes 180256 | tf_op jit(solution)/shard_map/all_to_all | solution.py:168
  33.6 3.5 collective-permute-start.1
  49.9 63.2 %all-gather.6.cloned.1.call-done = bf16[32,132,768]{2,1,0:T(8,128)(2,1)} async-done(((bf16[1,132,768]{2,1,0:T(8,128)(2,1)}), bf16[32,132,768]{2,1,0:T(8,128)(2,1)}) %all-gather.6.cloned.1.call-update) | async-done | bytes 6488080 | tf_op jit(solution)/shard_map/all_gather | solution.py:41
  113.1 8.3 %reshape.80.mine_ref = bf16[4224,768]{1,0:T(8,128)(2,1)} reshape(bf16[32,132,768]{2,1,0:T(8,128)(2,1)} %all-gather.6.cloned.1.call-done) | data formatting | bytes 12976128 | tf_op jit(solution)/shard_map/optimization_barrier | solution.py:194
  121.5 2.9 collective-permute-start.9
  124.8 10.0 %collective-permute-done.9.other_ref = bf16[4224,768]{1,0:T(8,128)(2,1)} collective-permute-done((bf16[4224,768]{1,0:T(8,128)(2,1)}, bf16[4224,768]{1,0:T(8,128)(2,1)}, u32[]{:S(2)}, u32[]{:S(2)}) %collective-permute-start.9) | collective-permute-done | bytes 6488096 | tf_op jit(solution)/shard_map/ppermute | solution.py:22
  134.8 4.5 %shard_map.104.weights_ref = bf16[4224,1408]{1,0:T(8,128)(2,1)S(1)} custom-call(s32[1]{0:T(128)} %bitcast.2.core_ref, bf16[4224,768]{1,0:T(8,128)(2,1)} %reshape.80.mine_ref, bf16[4224,768]{1,0:T(8,128)(2,1)} %collective-permute-done.9.other_ref), custom_call_target="tpu_custom_call" | custom-call | bytes 23789568 | tf_op jit(solution)/shard_map/pallas_call | solution.py:69
  139.4 3.9 %shard_map.105 = (bf16[72,1408]{1,0:T(8,128)(2,1)S(1)}, bf16[64,1408]{1,0:T(8,128)(2,1)S(1)}) custom-call(s32[2]{0:T(128)S(1)} %add_convert_fusion.flags_ref, bf16[4224,1408]{1,0:T(8,128)(2,1)S(1)} %shard_map.104.weights_ref, f32[1,1408]{1,0:T(1,128)S(1)} %copy-done.4, bf16[72,1408]{1,0:T(8,128)(2,1)S(1)} %broadcast_in_dim.36.incoming_ref, ...), custom_call_target="tpu_custom_call" | custom-call | flops 856424448 | bytes 811008 | tf_op jit(solution)/shard_map/pallas_call | solution.py:121
  143.2 3.3 collective-permute-start.10
  146.5 3.9 %shard_map.106 = (bf16[72,1408]{1,0:T(8,128)(2,1)S(1)}, bf16[64,1408]{1,0:T(8,128)(2,1)S(1)}) custom-call(s32[2]{0:T(128)S(1)} %add_convert_fusion.flags_ref, bf16[4224,1408]{1,0:T(8,128)(2,1)S(1)} %shard_map.104.weights_ref, f32[1,1408]{1,0:T(1,128)S(1)} %copy-done.4, bf16[72,1408]{1,0:T(8,128)(2,1)S(1)} %broadcast_in_dim.36.incoming_ref, ...), custom_call_target="tpu_custom_call" | custom-call | flops 856424448 | bytes 811008 | tf_op jit(solution)/shard_map/pallas_call | solution.py:121
  150.4 3.3 collective-permute-start.12
  153.8 3.9 %shard_map.107 = (bf16[72,1408]{1,0:T(8,128)(2,1)S(1)}, bf16[64,1408]{1,0:T(8,128)(2,1)S(1)}) custom-call(s32[2]{0:T(128)S(1)} %add_convert_fusion.flags_ref, bf16[4224,1408]{1,0:T(8,128)(2,1)S(1)} %shard_map.104.weights_ref, f32[1,1408]{1,0:T(1,128)S(1)} %copy-done.4, bf16[72,1408]{1,0:T(8,128)(2,1)S(1)} %collective-permute-done.10.incoming_ref, ...), custom_call_target="tpu_custom_call" | custom-call | flops 856424448 | bytes 811008 | tf_op jit(solution)/shard_map/pallas_call | solution.py:121
  157.7 3.3 collective-permute-start.11
  160.9 3.9 %shard_map.108 = (bf16[72,1408]{1,0:T(8,128)(2,1)S(1)}, bf16[64,1408]{1,0:T(8,128)(2,1)S(1)}) custom-call(s32[2]{0:T(128)S(1)} %add_convert_fusion.flags_ref, bf16[4224,1408]{1,0:T(8,128)(2,1)S(1)} %shard_map.104.weights_ref, f32[1,1408]{1,0:T(1,128)S(1)} %copy-done.4, bf16[72,1408]{1,0:T(8,128)(2,1)S(1)} %collective-permute-done.12.incoming_ref, ...), custom_call_target="tpu_custom_call" | custom-call | flops 856424448 | bytes 811008 | tf_op jit(solution)/shard_map/pallas_call | solution.py:121
  164.8 4.5 %collective-permute-start.14 = (bf16[72,1408]{1,0:T(8,128)(2,1)S(1)}, bf16[72,1408]{1,0:T(8,128)(2,1)S(1)}, u32[]{:S(2)}, u32[]{:S(2)}) collective-permute-start(bf16[72,1408]{1,0:T(8,128)(2,1)S(1)} %get-tuple-element.104), channel_id=1, source_target_pairs={{0,1},{1,2},{2,3},{3,4},{4,5},{5,6},{6,7},{8,9},{9,10},{10,11},{11... | collective-permute-start | bytes 608264 | tf_op jit(solution)/shard_map/ppermute | solution.py:226
  169.4 3.9 %shard_map.109 = (bf16[72,1408]{1,0:T(8,128)(2,1)S(1)}, bf16[64,1408]{1,0:T(8,128)(2,1)S(1)}) custom-call(s32[2]{0:T(128)S(1)} %add_convert_fusion.flags_ref, bf16[4224,1408]{1,0:T(8,128)(2,1)S(1)} %shard_map.104.weights_ref, f32[1,1408]{1,0:T(1,128)S(1)} %copy-done.4, bf16[72,1408]{1,0:T(8,128)(2,1)S(1)} %collective-permute-done.11.incoming_ref, ...), custom_call_target="tpu_custom_call" | custom-call | flops 856424448 | bytes 811008 | tf_op jit(solution)/shard_map/pallas_call | solution.py:121
  175.7 3.9 %shard_map.110 = (bf16[72,1408]{1,0:T(8,128)(2,1)S(1)}, bf16[64,1408]{1,0:T(8,128)(2,1)S(1)}) custom-call(s32[2]{0:T(128)S(1)} %add_convert_fusion.flags_ref, bf16[4224,1408]{1,0:T(8,128)(2,1)S(1)} %shard_map.104.weights_ref, f32[1,1408]{1,0:T(1,128)S(1)} %copy-done.4, bf16[72,1408]{1,0:T(8,128)(2,1)S(1)} %collective-permute-done.14.incoming_ref, ...), custom_call_target="tpu_custom_call" | custom-call | flops 856424448 | bytes 811008 | tf_op jit(solution)/shard_map/pallas_call | solution.py:121
  179.6 3.0 collective-permute-start.16
  182.7 3.9 %shard_map.111 = (bf16[72,1408]{1,0:T(8,128)(2,1)S(1)}, bf16[64,1408]{1,0:T(8,128)(2,1)S(1)}) custom-call(s32[2]{0:T(128)S(1)} %add_convert_fusion.flags_ref, bf16[4224,1408]{1,0:T(8,128)(2,1)S(1)} %shard_map.104.weights_ref, f32[1,1408]{1,0:T(1,128)S(1)} %copy-done.4, bf16[72,1408]{1,0:T(8,128)(2,1)S(1)} %collective-permute-done.13.incoming_ref, ...), custom_call_target="tpu_custom_call" | custom-call | flops 856424448 | bytes 811008 | tf_op jit(solution)/shard_map/pallas_call | solution.py:121
  188.7 3.9 %shard_map.112 = (bf16[72,1408]{1,0:T(8,128)(2,1)S(1)}, bf16[64,1408]{1,0:T(8,128)(2,1)S(1)}) custom-call(s32[2]{0:T(128)S(1)} %add_convert_fusion.flags_ref, bf16[4224,1408]{1,0:T(8,128)(2,1)S(1)} %shard_map.104.weights_ref, f32[1,1408]{1,0:T(1,128)S(1)} %copy-done.4, bf16[72,1408]{1,0:T(8,128)(2,1)S(1)} %collective-permute-done.16.incoming_ref, ...), custom_call_target="tpu_custom_call" | custom-call | flops 856424448 | bytes 811008 | tf_op jit(solution)/shard_map/pallas_call | solution.py:121
  195.0 3.9 %shard_map.113 = (bf16[72,1408]{1,0:T(8,128)(2,1)S(1)}, bf16[64,1408]{1,0:T(8,128)(2,1)S(1)}) custom-call(s32[2]{0:T(128)S(1)} %add_convert_fusion.flags_ref, bf16[4224,1408]{1,0:T(8,128)(2,1)S(1)} %shard_map.104.weights_ref, f32[1,1408]{1,0:T(1,128)S(1)} %copy-done.4, bf16[72,1408]{1,0:T(8,128)(2,1)S(1)} %collective-permute-done.15.incoming_ref.fresh_ref, ...), custom_call_target="tpu_custom_call" | custom-call | flops 856424448 | bytes 811008 | tf_op jit(solution)/shard_map/pallas_call | solution.py:121
  201.0 3.9 %shard_map.114 = (bf16[72,1408]{1,0:T(8,128)(2,1)S(1)}, bf16[64,1408]{1,0:T(8,128)(2,1)S(1)}) custom-call(s32[2]{0:T(128)S(1)} %add_convert_fusion.flags_ref, bf16[4224,1408]{1,0:T(8,128)(2,1)S(1)} %shard_map.104.weights_ref, f32[1,1408]{1,0:T(1,128)S(1)} %copy-done.4, bf16[72,1408]{1,0:T(8,128)(2,1)S(1)} %collective-permute-done.18.incoming_ref.fresh_ref, ...), custom_call_target="tpu_custom_call" | custom-call | flops 856424448 | bytes 811008 | tf_op jit(solution)/shard_map/pallas_call | solution.py:121
  207.0 3.9 %shard_map.115 = (bf16[72,1408]{1,0:T(8,128)(2,1)S(1)}, bf16[64,1408]{1,0:T(8,128)(2,1)S(1)}) custom-call(s32[2]{0:T(128)S(1)} %add_convert_fusion.flags_ref, bf16[4224,1408]{1,0:T(8,128)(2,1)S(1)} %shard_map.104.weights_ref, f32[1,1408]{1,0:T(1,128)S(1)} %copy-done.4, bf16[72,1408]{1,0:T(8,128)(2,1)S(1)} %collective-permute-done.17.incoming_ref.fresh_ref, ...), custom_call_target="tpu_custom_call" | custom-call | flops 856424448 | bytes 811008 | tf_op jit(solution)/shard_map/pallas_call | solution.py:121
  213.0 3.9 %shard_map.116 = (bf16[72,1408]{1,0:T(8,128)(2,1)S(1)}, bf16[64,1408]{1,0:T(8,128)(2,1)S(1)}) custom-call(s32[2]{0:T(128)S(1)} %add_convert_fusion.flags_ref, bf16[4224,1408]{1,0:T(8,128)(2,1)S(1)} %shard_map.104.weights_ref, f32[1,1408]{1,0:T(1,128)S(1)} %copy-done.4, bf16[72,1408]{1,0:T(8,128)(2,1)S(1)} %collective-permute-done.20.incoming_ref.fresh_ref, ...), custom_call_target="tpu_custom_call" | custom-call | flops 856424448 | bytes 811008 | tf_op jit(solution)/shard_map/pallas_call | solution.py:121
  219.0 3.9 %shard_map.117 = (bf16[72,1408]{1,0:T(8,128)(2,1)S(1)}, bf16[64,1408]{1,0:T(8,128)(2,1)S(1)}) custom-call(s32[2]{0:T(128)S(1)} %add_convert_fusion.flags_ref, bf16[4224,1408]{1,0:T(8,128)(2,1)S(1)} %shard_map.104.weights_ref, f32[1,1408]{1,0:T(1,128)S(1)} %copy-done.4, bf16[72,1408]{1,0:T(8,128)(2,1)S(1)} %collective-permute-done.19.incoming_ref.fresh_ref, ...), custom_call_target="tpu_custom_call" | custom-call | flops 856424448 | bytes 811008 | tf_op jit(solution)/shard_map/pallas_call | solution.py:121
  224.8 3.9 %shard_map.118 = (bf16[72,1408]{1,0:T(8,128)(2,1)S(1)}, bf16[64,1408]{1,0:T(8,128)(2,1)S(1)}) custom-call(s32[2]{0:T(128)S(1)} %add_convert_fusion.flags_ref, bf16[4224,1408]{1,0:T(8,128)(2,1)S(1)} %shard_map.104.weights_ref, f32[1,1408]{1,0:T(1,128)S(1)} %copy-done.4, bf16[72,1408]{1,0:T(8,128)(2,1)S(1)} %collective-permute-done.22.incoming_ref.fresh_ref, ...), custom_call_target="tpu_custom_call" | custom-call | flops 856424448 | bytes 811008 | tf_op jit(solution)/shard_map/pallas_call | solution.py:121
  230.7 3.9 %shard_map.119 = (bf16[72,1408]{1,0:T(8,128)(2,1)S(1)}, bf16[64,1408]{1,0:T(8,128)(2,1)S(1)}) custom-call(s32[2]{0:T(128)S(1)} %add_convert_fusion.flags_ref, bf16[4224,1408]{1,0:T(8,128)(2,1)S(1)} %shard_map.104.weights_ref, f32[1,1408]{1,0:T(1,128)S(1)} %copy-done.4, bf16[72,1408]{1,0:T(8,128)(2,1)S(1)} %collective-permute-done.21.incoming_ref.fresh_ref, ...), custom_call_target="tpu_custom_call" | custom-call | flops 856424448 | bytes 811008 | tf_op jit(solution)/shard_map/pallas_call | solution.py:121
  236.9 3.9 %shard_map.120 = (bf16[72,1408]{1,0:T(8,128)(2,1)S(1)}, bf16[64,1408]{1,0:T(8,128)(2,1)S(1)}) custom-call(s32[2]{0:T(128)S(1)} %add_convert_fusion.flags_ref, bf16[4224,1408]{1,0:T(8,128)(2,1)S(1)} %shard_map.104.weights_ref, f32[1,1408]{1,0:T(1,128)S(1)} %copy-done.4, bf16[72,1408]{1,0:T(8,128)(2,1)S(1)} %collective-permute-done.24.incoming_ref.fresh_ref, ...), custom_call_target="tpu_custom_call" | custom-call | flops 856424448 | bytes 811008 | tf_op jit(solution)/shard_map/pallas_call | solution.py:121
  242.8 3.8 collective-permute-start.27
  248.7 3.9 %shard_map.121 = (bf16[72,1408]{1,0:T(8,128)(2,1)S(1)}, bf16[64,1408]{1,0:T(8,128)(2,1)S(1)}) custom-call(s32[2]{0:T(128)S(1)} %add_convert_fusion.flags_ref, bf16[4224,1408]{1,0:T(8,128)(2,1)S(1)} %shard_map.104.weights_ref, f32[1,1408]{1,0:T(1,128)S(1)} %copy-done.4, bf16[72,1408]{1,0:T(8,128)(2,1)S(1)} %collective-permute-done.26.incoming_ref.fresh_ref, ...), custom_call_target="tpu_custom_call" | custom-call | flops 856424448 | bytes 811008 | tf_op jit(solution)/shard_map/pallas_call | solution.py:121
  253.9 2.5 collective-permute-done.23
  259.1 3.9 %shard_map.122 = (bf16[72,1408]{1,0:T(8,128)(2,1)S(1)}, bf16[64,1408]{1,0:T(8,128)(2,1)S(1)}) custom-call(s32[2]{0:T(128)S(1)} %add_convert_fusion.flags_ref, bf16[4224,1408]{1,0:T(8,128)(2,1)S(1)} %shard_map.104.weights_ref, f32[1,1408]{1,0:T(1,128)S(1)} %copy-done.4, bf16[72,1408]{1,0:T(8,128)(2,1)S(1)} %collective-permute-done.25.incoming_ref.fresh_ref, ...), custom_call_target="tpu_custom_call" | custom-call | flops 856424448 | bytes 811008 | tf_op jit(solution)/shard_map/pallas_call | solution.py:121
  263.0 5.6 %collective-permute-start.30 = (bf16[72,1408]{1,0:T(8,128)(2,1)S(1)}, bf16[72,1408]{1,0:T(8,128)(2,1)S(1)}, u32[]{:S(2)}, u32[]{:S(2)}) collective-permute-start(bf16[72,1408]{1,0:T(8,128)(2,1)S(1)} %get-tuple-element.138), channel_id=1, source_target_pairs={{0,1},{1,2},{2,3},{3,4},{4,5},{5,6},{6,7},{8,9},{9,10},{10,11},{11... | collective-permute-start | bytes 608264 | tf_op jit(solution)/shard_map/ppermute | solution.py:226
  274.8 18.3 %all-to-all-start.1 = ((bf16[4,32,2,1,1408]{4,2,0,3,1:T(2,128)(2,1)}), bf16[4,32,2,1,1408]{4,2,0,3,1:T(2,128)(2,1)S(1)}, u32[]{:S(2)}, u32[]{:S(2)}) async-start(bf16[4,32,2,1,1408]{4,2,0,3,1:T(2,128)(2,1)} %copy.22), calls=%async_computation.1 | async-start | bytes 1441792 | tf_op jit(solution)/shard_map/all_to_all | solution.py:175
  293.2 4.4 %copy-done.3 = bf16[4224,1408]{1,0:T(8,128)(2,1)S(1)} copy-done((bf16[4224,1408]{1,0:T(8,128)(2,1)S(1)}, bf16[4224,1408]{1,0:T(8,128)(2,1)}, u32[]{:S(2)}) %copy-start.3) | copy-done | bytes 11894808
  297.5 3.9 %shard_map.123 = (bf16[72,1408]{1,0:T(8,128)(2,1)S(1)}, bf16[64,1408]{1,0:T(8,128)(2,1)S(1)}) custom-call(s32[2]{0:T(128)S(1)} %add_convert_fusion.flags_ref, bf16[4224,1408]{1,0:T(8,128)(2,1)S(1)} %copy-done.3, f32[1,1408]{1,0:T(1,128)S(1)} %copy-done.4, bf16[72,1408]{1,0:T(8,128)(2,1)S(1)} %collective-permute-done.28.incoming_ref.fresh_ref, ...), custom_call_target="tpu_custom_call" | custom-call | flops 856424448 | bytes 811008 | tf_op jit(solution)/shard_map/pallas_call | solution.py:121
  302.8 3.9 %shard_map.124 = (bf16[72,1408]{1,0:T(8,128)(2,1)S(1)}, bf16[64,1408]{1,0:T(8,128)(2,1)S(1)}) custom-call(s32[2]{0:T(128)S(1)} %add_convert_fusion.flags_ref, bf16[4224,1408]{1,0:T(8,128)(2,1)S(1)} %copy-done.3, f32[1,1408]{1,0:T(1,128)S(1)} %copy-done.4, bf16[72,1408]{1,0:T(8,128)(2,1)S(1)} %collective-permute-done.30.incoming_ref.fresh_ref, ...), custom_call_target="tpu_custom_call" | custom-call | flops 856424448 | bytes 811008 | tf_op jit(solution)/shard_map/pallas_call | solution.py:121
  311.0 3.9 %shard_map.125 = (bf16[72,1408]{1,0:T(8,128)(2,1)S(1)}, bf16[64,1408]{1,0:T(8,128)(2,1)S(1)}) custom-call(s32[2]{0:T(128)S(1)} %add_convert_fusion.flags_ref, bf16[4224,1408]{1,0:T(8,128)(2,1)S(1)} %copy-done.3, f32[1,1408]{1,0:T(1,128)S(1)} %copy-done.4, bf16[72,1408]{1,0:T(8,128)(2,1)S(1)} %collective-permute-done.32.incoming_ref.fresh_ref, ...), custom_call_target="tpu_custom_call" | custom-call | flops 856424448 | bytes 811008 | tf_op jit(solution)/shard_map/pallas_call | solution.py:121
  317.1 3.9 %shard_map.126 = (bf16[72,1408]{1,0:T(8,128)(2,1)S(1)}, bf16[64,1408]{1,0:T(8,128)(2,1)S(1)}) custom-call(s32[2]{0:T(128)S(1)} %add_convert_fusion.flags_ref, bf16[4224,1408]{1,0:T(8,128)(2,1)S(1)} %copy-done.3, f32[1,1408]{1,0:T(1,128)S(1)} %copy-done.4, bf16[72,1408]{1,0:T(8,128)(2,1)S(1)} %collective-permute-done.34.incoming_ref.fresh_ref, ...), custom_call_target="tpu_custom_call" | custom-call | flops 856424448 | bytes 811008 | tf_op jit(solution)/shard_map/pallas_call | solution.py:121
  324.9 9.2 %all-to-all-start.2 = ((bf16[32,2,1,1408]{3,1,2,0:T(2,128)(2,1)}), bf16[32,2,1,1408]{3,1,2,0:T(2,128)(2,1)S(1)}, u32[]{:S(2)}, u32[]{:S(2)}) async-start(bf16[32,2,1,1408]{3,1,2,0:T(2,128)(2,1)} %bitcast.40), calls=%async_computation.2 | async-start | bytes 360448 | tf_op jit(solution)/shard_map/all_to_all | solution.py:175
  336.1 6.2 %reshape.59 = bf16[1408,1408]{1,0:T(8,128)(2,1)} reshape(bf16[64,22,1408]{2,1,0:T(8,128)(2,1)} %all-gather.8.cloned.1.call-done) | data formatting | bytes 7929856 | tf_op jit(solution)/shard_map/reshape | solution.py:238
  345.4 6.7 %all-to-all-start.3 = ((bf16[4,32,2,1,1408]{4,0,2,3,1:T(4,128)(2,1)}), bf16[4,32,2,1,1408]{4,0,2,3,1:T(4,128)(2,1)S(1)}, u32[]{:S(2)}, u32[]{:S(2)}) async-start(bf16[4,32,2,1,1408]{4,0,2,3,1:T(4,128)(2,1)} %bitcast.52), calls=%async_computation.3 | async-start | bytes 1441792 | tf_op jit(solution)/shard_map/all_to_all | solution.py:175
  357.7 2.8 convolution_convert_fusion
  361.4 6.0 %collective-permute-start.42 = (bf16[16,1408]{1,0:T(8,128)(2,1)S(1)}, bf16[16,1408]{1,0:T(8,128)(2,1)S(1)}, u32[]{:S(2)}, u32[]{:S(2)}) collective-permute-start(bf16[16,1408]{1,0:T(8,128)(2,1)S(1)} %get-tuple-element.202), channel_id=1, source_target_pairs={{0,24},{8,32},{16,40},{24,48},{32,56},{40,64},{48,72},{56,80},{64,... | collective-permute-start | bytes 135176 | tf_op jit(solution)/shard_map/ppermute | solution.py:14
  367.4 3.4 collective-permute-start.41
  374.8 3.5 fusion.46
  (162 shorter events, 81.9 us)
Async XLA Ops:
  7.2 105.9 %all-gather.6.cloned.1.call-start = ((), (), s32[]{:S(2)}) async-start(), calls=%async_computation.4 | async-start | bytes 6893568 | tf_op jit(solution)/shard_map/all_gather | solution.py:41
  8.3 9.7 %collective-permute-start = (bf16[66,768]{1,0:T(8,128)(2,1)S(1)}, bf16[66,768]{1,0:T(8,128)(2,1)S(1)}, u32[]{:S(2)}, u32[]{:S(2)}) collective-permute-start(bf16[66,768]{1,0:T(8,128)(2,1)S(1)} %get-tuple-element.200), channel_id=1, source_target_pairs={{0,8},{8,0},{16,24},{24,16},{32,40},{40,32},{48,56},{56,48},{64,72... | collective-permute-start | bytes 304136 | tf_op jit(solution)/shard_map/ppermute | solution.py:22
  19.7 13.8 %all-to-all-start = ((bf16[1,2,32,1408]{3,1,0,2:T(2,128)(2,1)}), bf16[1,2,32,1408]{3,1,0,2:T(2,128)(2,1)S(1)}, u32[]{:S(2)}, u32[]{:S(2)}) async-start(bf16[1,2,32,1408]{3,1,0,2:T(2,128)(2,1)} %copy.21), calls=%async_computation | async-start | bytes 360448 | tf_op jit(solution)/shard_map/all_to_all | solution.py:168
  23.6 300.6 %all-gather.8.cloned.1.call-start = ((), (), s32[]{:S(2)}) async-start(), calls=%async_computation.5 | async-start | bytes 4392960 | tf_op jit(solution)/shard_map/all_gather | solution.py:198
  33.6 6.1 %collective-permute-start.1 = (bf16[8,1408]{1,0:T(8,128)(2,1)S(1)}, bf16[8,1408]{1,0:T(8,128)(2,1)S(1)}, u32[]{:S(2)}, u32[]{:S(2)}) collective-permute-start(bf16[8,1408]{1,0:T(8,128)(2,1)S(1)} %select_n.143), channel_id=1, source_target_pairs={{0,256},{8,264},{16,272},{24,280},{32,288},{40,296},{48,304},{56,3... | collective-permute-start | bytes 67592 | tf_op jit(solution)/shard_map/ppermute | solution.py:183
  39.7 7.0 %collective-permute-start.2 = (bf16[72,1408]{1,0:T(8,128)(2,1)S(1)}, bf16[72,1408]{1,0:T(8,128)(2,1)S(1)}, u32[]{:S(2)}, u32[]{:S(2)}) collective-permute-start(bf16[72,1408]{1,0:T(8,128)(2,1)S(1)} %maximum_select_fusion.1.fresh_ref), channel_id=1, source_target_pairs={{1,0},{9,8},{17,16},{25,24},{33,32},{41,40},{49,48},{57,56},{65,64... | collective-permute-start | bytes 608264 | tf_op jit(solution)/shard_map/ppermute | solution.py:193
  41.1 7.5 %collective-permute-start.3 = (bf16[72,1408]{1,0:T(8,128)(2,1)S(1)}, bf16[72,1408]{1,0:T(8,128)(2,1)S(1)}, u32[]{:S(2)}, u32[]{:S(2)}) collective-permute-start(bf16[72,1408]{1,0:T(8,128)(2,1)S(1)} %maximum_select_fusion.1.fresh_ref), channel_id=1, source_target_pairs={{2,0},{10,8},{18,16},{26,24},{34,32},{42,40},{50,48},{58,56},{66,6... | collective-permute-start | bytes 608264 | tf_op jit(solution)/shard_map/ppermute | solution.py:193
  42.4 79.0 %collective-permute-start.4 = (bf16[72,1408]{1,0:T(8,128)(2,1)S(1)}, bf16[72,1408]{1,0:T(8,128)(2,1)S(1)}, u32[]{:S(2)}, u32[]{:S(2)}) collective-permute-start(bf16[72,1408]{1,0:T(8,128)(2,1)S(1)} %maximum_select_fusion.1.fresh_ref), channel_id=1, source_target_pairs={{3,0},{11,8},{19,16},{27,24},{35,32},{43,40},{51,48},{59,56},{67,6... | collective-permute-start | bytes 608264 | tf_op jit(solution)/shard_map/ppermute | solution.py:193
  43.7 77.7 %collective-permute-start.5 = (bf16[72,1408]{1,0:T(8,128)(2,1)S(1)}, bf16[72,1408]{1,0:T(8,128)(2,1)S(1)}, u32[]{:S(2)}, u32[]{:S(2)}) collective-permute-start(bf16[72,1408]{1,0:T(8,128)(2,1)S(1)} %maximum_select_fusion.1.fresh_ref), channel_id=1, source_target_pairs={{4,0},{12,8},{20,16},{28,24},{36,32},{44,40},{52,48},{60,56},{68,6... | collective-permute-start | bytes 608264 | tf_op jit(solution)/shard_map/ppermute | solution.py:193
  45.0 76.4 %collective-permute-start.6 = (bf16[72,1408]{1,0:T(8,128)(2,1)S(1)}, bf16[72,1408]{1,0:T(8,128)(2,1)S(1)}, u32[]{:S(2)}, u32[]{:S(2)}) collective-permute-start(bf16[72,1408]{1,0:T(8,128)(2,1)S(1)} %maximum_select_fusion.1.fresh_ref), channel_id=1, source_target_pairs={{5,0},{13,8},{21,16},{29,24},{37,32},{45,40},{53,48},{61,56},{69,6... | collective-permute-start | bytes 608264 | tf_op jit(solution)/shard_map/ppermute | solution.py:193
  46.7 74.7 %collective-permute-start.7 = (bf16[72,1408]{1,0:T(8,128)(2,1)S(1)}, bf16[72,1408]{1,0:T(8,128)(2,1)S(1)}, u32[]{:S(2)}, u32[]{:S(2)}) collective-permute-start(bf16[72,1408]{1,0:T(8,128)(2,1)S(1)} %maximum_select_fusion.1.fresh_ref), channel_id=1, source_target_pairs={{6,0},{14,8},{22,16},{30,24},{38,32},{46,40},{54,48},{62,56},{70,6... | collective-permute-start | bytes 608264 | tf_op jit(solution)/shard_map/ppermute | solution.py:193
  48.6 72.8 %collective-permute-start.8 = (bf16[72,1408]{1,0:T(8,128)(2,1)S(1)}, bf16[72,1408]{1,0:T(8,128)(2,1)S(1)}, u32[]{:S(2)}, u32[]{:S(2)}) collective-permute-start(bf16[72,1408]{1,0:T(8,128)(2,1)S(1)} %maximum_select_fusion.1.fresh_ref), channel_id=1, source_target_pairs={{7,0},{15,8},{23,16},{31,24},{39,32},{47,40},{55,48},{63,56},{71,6... | collective-permute-start | bytes 608264 | tf_op jit(solution)/shard_map/ppermute | solution.py:193
  121.5 13.3 %collective-permute-start.9 = (bf16[4224,768]{1,0:T(8,128)(2,1)}, bf16[4224,768]{1,0:T(8,128)(2,1)}, u32[]{:S(2)}, u32[]{:S(2)}) collective-permute-start(bf16[4224,768]{1,0:T(8,128)(2,1)} %reshape.80.mine_ref), channel_id=1, source_target_pairs={{0,8},{8,0},{16,24},{24,16},{32,40},{40,32},{48,56},{56,48},{64,72... | collective-permute-start | bytes 19464200 | tf_op jit(solution)/shard_map/ppermute | solution.py:22
  143.2 10.5 %collective-permute-start.10 = (bf16[72,1408]{1,0:T(8,128)(2,1)S(1)}, bf16[72,1408]{1,0:T(8,128)(2,1)S(1)}, u32[]{:S(2)}, u32[]{:S(2)}) collective-permute-start(bf16[72,1408]{1,0:T(8,128)(2,1)S(1)} %get-tuple-element.95), channel_id=1, source_target_pairs={{0,1},{1,2},{2,3},{3,4},{4,5},{5,6},{6,7},{8,9},{9,10},{10,11},{11... | collective-permute-start | bytes 608264 | tf_op jit(solution)/shard_map/ppermute | solution.py:226
  150.4 10.5 %collective-permute-start.12 = (bf16[72,1408]{1,0:T(8,128)(2,1)S(1)}, bf16[72,1408]{1,0:T(8,128)(2,1)S(1)}, u32[]{:S(2)}, u32[]{:S(2)}) collective-permute-start(bf16[72,1408]{1,0:T(8,128)(2,1)S(1)} %get-tuple-element.98), channel_id=1, source_target_pairs={{0,1},{1,2},{2,3},{3,4},{4,5},{5,6},{6,7},{8,9},{9,10},{10,11},{11... | collective-permute-start | bytes 608264 | tf_op jit(solution)/shard_map/ppermute | solution.py:226
  157.7 11.7 %collective-permute-start.11 = (bf16[72,1408]{1,0:T(8,128)(2,1)S(1)}, bf16[72,1408]{1,0:T(8,128)(2,1)S(1)}, u32[]{:S(2)}, u32[]{:S(2)}) collective-permute-start(bf16[72,1408]{1,0:T(8,128)(2,1)S(1)} %get-tuple-element.101), channel_id=1, source_target_pairs={{0,1},{1,2},{2,3},{3,4},{4,5},{5,6},{6,7},{8,9},{9,10},{10,11},{11... | collective-permute-start | bytes 608264 | tf_op jit(solution)/shard_map/ppermute | solution.py:226
  164.8 10.8 %collective-permute-start.14 = (bf16[72,1408]{1,0:T(8,128)(2,1)S(1)}, bf16[72,1408]{1,0:T(8,128)(2,1)S(1)}, u32[]{:S(2)}, u32[]{:S(2)}) collective-permute-start(bf16[72,1408]{1,0:T(8,128)(2,1)S(1)} %get-tuple-element.104), channel_id=1, source_target_pairs={{0,1},{1,2},{2,3},{3,4},{4,5},{5,6},{6,7},{8,9},{9,10},{10,11},{11... | collective-permute-start | bytes 608264 | tf_op jit(solution)/shard_map/ppermute | solution.py:226
  173.3 9.4 %collective-permute-start.13 = (bf16[72,1408]{1,0:T(8,128)(2,1)S(1)}, bf16[72,1408]{1,0:T(8,128)(2,1)S(1)}, u32[]{:S(2)}, u32[]{:S(2)}) collective-permute-start(bf16[72,1408]{1,0:T(8,128)(2,1)S(1)} %get-tuple-element.107), channel_id=1, source_target_pairs={{0,1},{1,2},{2,3},{3,4},{4,5},{5,6},{6,7},{8,9},{9,10},{10,11},{11... | collective-permute-start | bytes 608264 | tf_op jit(solution)/shard_map/ppermute | solution.py:226
  179.6 9.1 %collective-permute-start.16 = (bf16[72,1408]{1,0:T(8,128)(2,1)S(1)}, bf16[72,1408]{1,0:T(8,128)(2,1)S(1)}, u32[]{:S(2)}, u32[]{:S(2)}) collective-permute-start(bf16[72,1408]{1,0:T(8,128)(2,1)S(1)} %get-tuple-element.110), channel_id=1, source_target_pairs={{0,1},{1,2},{2,3},{3,4},{4,5},{5,6},{6,7},{8,9},{9,10},{10,11},{11... | collective-permute-start | bytes 608264 | tf_op jit(solution)/shard_map/ppermute | solution.py:226
  186.6 8.4 %collective-permute-start.15 = (bf16[72,1408]{1,0:T(8,128)(2,1)S(1)}, bf16[72,1408]{1,0:T(8,128)(2,1)S(1)}, u32[]{:S(2)}, u32[]{:S(2)}) collective-permute-start(bf16[72,1408]{1,0:T(8,128)(2,1)S(1)} %get-tuple-element.113), channel_id=1, source_target_pairs={{0,1},{1,2},{2,3},{3,4},{4,5},{5,6},{6,7},{8,9},{9,10},{10,11},{11... | collective-permute-start | bytes 608264 | tf_op jit(solution)/shard_map/ppermute | solution.py:226
  192.6 8.5 %collective-permute-start.18 = (bf16[72,1408]{1,0:T(8,128)(2,1)S(1)}, bf16[72,1408]{1,0:T(8,128)(2,1)S(1)}, u32[]{:S(2)}, u32[]{:S(2)}) collective-permute-start(bf16[72,1408]{1,0:T(8,128)(2,1)S(1)} %get-tuple-element.116), channel_id=1, source_target_pairs={{0,1},{1,2},{2,3},{3,4},{4,5},{5,6},{6,7},{8,9},{9,10},{10,11},{11... | collective-permute-start | bytes 608264 | tf_op jit(solution)/shard_map/ppermute | solution.py:226
  198.9 8.1 %collective-permute-start.17 = (bf16[72,1408]{1,0:T(8,128)(2,1)S(1)}, bf16[72,1408]{1,0:T(8,128)(2,1)S(1)}, u32[]{:S(2)}, u32[]{:S(2)}) collective-permute-start(bf16[72,1408]{1,0:T(8,128)(2,1)S(1)} %get-tuple-element.118), channel_id=1, source_target_pairs={{0,1},{1,2},{2,3},{3,4},{4,5},{5,6},{6,7},{8,9},{9,10},{10,11},{11... | collective-permute-start | bytes 608264 | tf_op jit(solution)/shard_map/ppermute | solution.py:226
  204.9 8.1 %collective-permute-start.20 = (bf16[72,1408]{1,0:T(8,128)(2,1)S(1)}, bf16[72,1408]{1,0:T(8,128)(2,1)S(1)}, u32[]{:S(2)}, u32[]{:S(2)}) collective-permute-start(bf16[72,1408]{1,0:T(8,128)(2,1)S(1)} %get-tuple-element.120), channel_id=1, source_target_pairs={{0,1},{1,2},{2,3},{3,4},{4,5},{5,6},{6,7},{8,9},{9,10},{10,11},{11... | collective-permute-start | bytes 608264 | tf_op jit(solution)/shard_map/ppermute | solution.py:226
  210.9 8.1 %collective-permute-start.19 = (bf16[72,1408]{1,0:T(8,128)(2,1)S(1)}, bf16[72,1408]{1,0:T(8,128)(2,1)S(1)}, u32[]{:S(2)}, u32[]{:S(2)}) collective-permute-start(bf16[72,1408]{1,0:T(8,128)(2,1)S(1)} %get-tuple-element.122), channel_id=1, source_target_pairs={{0,1},{1,2},{2,3},{3,4},{4,5},{5,6},{6,7},{8,9},{9,10},{10,11},{11... | collective-permute-start | bytes 608264 | tf_op jit(solution)/shard_map/ppermute | solution.py:226
  216.9 7.9 %collective-permute-start.22 = (bf16[72,1408]{1,0:T(8,128)(2,1)S(1)}, bf16[72,1408]{1,0:T(8,128)(2,1)S(1)}, u32[]{:S(2)}, u32[]{:S(2)}) collective-permute-start(bf16[72,1408]{1,0:T(8,128)(2,1)S(1)} %get-tuple-element.124), channel_id=1, source_target_pairs={{0,1},{1,2},{2,3},{3,4},{4,5},{5,6},{6,7},{8,9},{9,10},{10,11},{11... | collective-permute-start | bytes 608264 | tf_op jit(solution)/shard_map/ppermute | solution.py:226
  222.9 7.9 %collective-permute-start.21 = (bf16[72,1408]{1,0:T(8,128)(2,1)S(1)}, bf16[72,1408]{1,0:T(8,128)(2,1)S(1)}, u32[]{:S(2)}, u32[]{:S(2)}) collective-permute-start(bf16[72,1408]{1,0:T(8,128)(2,1)S(1)} %get-tuple-element.126), channel_id=1, source_target_pairs={{0,1},{1,2},{2,3},{3,4},{4,5},{5,6},{6,7},{8,9},{9,10},{10,11},{11... | collective-permute-start | bytes 608264 | tf_op jit(solution)/shard_map/ppermute | solution.py:226
  228.7 8.2 %collective-permute-start.24 = (bf16[72,1408]{1,0:T(8,128)(2,1)S(1)}, bf16[72,1408]{1,0:T(8,128)(2,1)S(1)}, u32[]{:S(2)}, u32[]{:S(2)}) collective-permute-start(bf16[72,1408]{1,0:T(8,128)(2,1)S(1)} %get-tuple-element.128), channel_id=1, source_target_pairs={{0,1},{1,2},{2,3},{3,4},{4,5},{5,6},{6,7},{8,9},{9,10},{10,11},{11... | collective-permute-start | bytes 608264 | tf_op jit(solution)/shard_map/ppermute | solution.py:226
  234.6 14.0 %collective-permute-start.26 = (bf16[72,1408]{1,0:T(8,128)(2,1)S(1)}, bf16[72,1408]{1,0:T(8,128)(2,1)S(1)}, u32[]{:S(2)}, u32[]{:S(2)}) collective-permute-start(bf16[72,1408]{1,0:T(8,128)(2,1)S(1)} %get-tuple-element.130), channel_id=1, source_target_pairs={{0,1},{1,2},{2,3},{3,4},{4,5},{5,6},{6,7},{8,9},{9,10},{10,11},{11... | collective-permute-start | bytes 608264 | tf_op jit(solution)/shard_map/ppermute | solution.py:226
  240.8 13.1 %collective-permute-start.25 = (bf16[72,1408]{1,0:T(8,128)(2,1)S(1)}, bf16[72,1408]{1,0:T(8,128)(2,1)S(1)}, u32[]{:S(2)}, u32[]{:S(2)}) collective-permute-start(bf16[72,1408]{1,0:T(8,128)(2,1)S(1)} %get-tuple-element.132), channel_id=1, source_target_pairs={{0,1},{1,2},{2,3},{3,4},{4,5},{5,6},{6,7},{8,9},{9,10},{10,11},{11... | collective-permute-start | bytes 608264 | tf_op jit(solution)/shard_map/ppermute | solution.py:226
  242.8 50.4 %collective-permute-start.27 = (bf16[72,1408]{1,0:T(8,128)(2,1)S(1)}, bf16[72,1408]{1,0:T(8,128)(2,1)}, u32[]{:S(2)}, u32[]{:S(2)}) collective-permute-start(bf16[72,1408]{1,0:T(8,128)(2,1)S(1)} %broadcast_select_fusion.5), channel_id=1, source_target_pairs={{7,1},{0,2},{15,9},{8,10},{23,17},{16,18},{31,25},{24,26},{39,33},... | collective-permute-start | bytes 608264 | tf_op jit(solution)/shard_map/ppermute | solution.py:230
  246.6 9.7 %collective-permute-start.23 = (bf16[72,1408]{1,0:T(8,128)(2,1)S(1)}, bf16[72,1408]{1,0:T(8,128)(2,1)S(1)}, u32[]{:S(2)}, u32[]{:S(2)}) collective-permute-start(bf16[72,1408]{1,0:T(8,128)(2,1)S(1)} %broadcast_select_fusion.6), channel_id=1, source_target_pairs={{7,0},{0,1},{15,8},{8,9},{23,16},{16,17},{31,24},{24,25},{39,32},{... | collective-permute-start | bytes 608264 | tf_op jit(solution)/shard_map/ppermute | solution.py:230
  252.6 40.6 %collective-permute-start.28 = (bf16[72,1408]{1,0:T(8,128)(2,1)S(1)}, bf16[72,1408]{1,0:T(8,128)(2,1)S(1)}, u32[]{:S(2)}, u32[]{:S(2)}) collective-permute-start(bf16[72,1408]{1,0:T(8,128)(2,1)S(1)} %get-tuple-element.134), channel_id=1, source_target_pairs={{0,1},{1,2},{2,3},{3,4},{4,5},{5,6},{6,7},{8,9},{9,10},{10,11},{11... | collective-permute-start | bytes 608264 | tf_op jit(solution)/shard_map/ppermute | solution.py:226
  257.1 45.6 %collective-permute-start.29 = (bf16[72,1408]{1,0:T(8,128)(2,1)}, bf16[72,1408]{1,0:T(8,128)(2,1)}, u32[]{:S(2)}, u32[]{:S(2)}) collective-permute-start(bf16[72,1408]{1,0:T(8,128)(2,1)} %broadcast_select_fusion.4), channel_id=1, source_target_pairs={{7,2},{0,3},{15,10},{8,11},{23,18},{16,19},{31,26},{24,27},{39,34}... | collective-permute-start | bytes 608264 | tf_op jit(solution)/shard_map/ppermute | solution.py:230
  263.0 39.7 %collective-permute-start.30 = (bf16[72,1408]{1,0:T(8,128)(2,1)S(1)}, bf16[72,1408]{1,0:T(8,128)(2,1)S(1)}, u32[]{:S(2)}, u32[]{:S(2)}) collective-permute-start(bf16[72,1408]{1,0:T(8,128)(2,1)S(1)} %get-tuple-element.138), channel_id=1, source_target_pairs={{0,1},{1,2},{2,3},{3,4},{4,5},{5,6},{6,7},{8,9},{9,10},{10,11},{11... | collective-permute-start | bytes 608264 | tf_op jit(solution)/shard_map/ppermute | solution.py:226
  269.4 41.6 %collective-permute-start.31 = (bf16[72,1408]{1,0:T(8,128)(2,1)}, bf16[72,1408]{1,0:T(8,128)(2,1)}, u32[]{:S(2)}, u32[]{:S(2)}) collective-permute-start(bf16[72,1408]{1,0:T(8,128)(2,1)} %broadcast_select_fusion.3), channel_id=1, source_target_pairs={{7,3},{0,4},{15,11},{8,12},{23,19},{16,20},{31,27},{24,28},{39,35}... | collective-permute-start | bytes 608264 | tf_op jit(solution)/shard_map/ppermute | solution.py:230
  274.8 49.2 %all-to-all-start.1 = ((bf16[4,32,2,1,1408]{4,2,0,3,1:T(2,128)(2,1)}), bf16[4,32,2,1,1408]{4,2,0,3,1:T(2,128)(2,1)S(1)}, u32[]{:S(2)}, u32[]{:S(2)}) async-start(bf16[4,32,2,1,1408]{4,2,0,3,1:T(2,128)(2,1)} %copy.22), calls=%async_computation.1 | async-start | bytes 1441792 | tf_op jit(solution)/shard_map/all_to_all | solution.py:175
  301.4 9.6 %collective-permute-start.32 = (bf16[72,1408]{1,0:T(8,128)(2,1)S(1)}, bf16[72,1408]{1,0:T(8,128)(2,1)S(1)}, u32[]{:S(2)}, u32[]{:S(2)}) collective-permute-start(bf16[72,1408]{1,0:T(8,128)(2,1)S(1)} %get-tuple-element.142), channel_id=1, source_target_pairs={{0,1},{1,2},{2,3},{3,4},{4,5},{5,6},{6,7},{8,9},{9,10},{10,11},{11... | collective-permute-start | bytes 608264 | tf_op jit(solution)/shard_map/ppermute | solution.py:226
  306.7 10.4 %collective-permute-start.34 = (bf16[72,1408]{1,0:T(8,128)(2,1)S(1)}, bf16[72,1408]{1,0:T(8,128)(2,1)S(1)}, u32[]{:S(2)}, u32[]{:S(2)}) collective-permute-start(bf16[72,1408]{1,0:T(8,128)(2,1)S(1)} %get-tuple-element.146), channel_id=1, source_target_pairs={{0,1},{1,2},{2,3},{3,4},{4,5},{5,6},{6,7},{8,9},{9,10},{10,11},{11... | collective-permute-start | bytes 608264 | tf_op jit(solution)/shard_map/ppermute | solution.py:226
  308.4 8.7 %collective-permute-start.33 = (bf16[72,1408]{1,0:T(8,128)(2,1)S(1)}, bf16[72,1408]{1,0:T(8,128)(2,1)S(1)}, u32[]{:S(2)}, u32[]{:S(2)}) collective-permute-start(bf16[72,1408]{1,0:T(8,128)(2,1)S(1)} %broadcast_select_fusion.2), channel_id=1, source_target_pairs={{7,4},{0,5},{15,12},{8,13},{23,20},{16,21},{31,28},{24,29},{39,36}... | collective-permute-start | bytes 608264 | tf_op jit(solution)/shard_map/ppermute | solution.py:230
  309.7 11.3 %collective-permute-start.35 = (bf16[72,1408]{1,0:T(8,128)(2,1)S(1)}, bf16[72,1408]{1,0:T(8,128)(2,1)S(1)}, u32[]{:S(2)}, u32[]{:S(2)}) collective-permute-start(bf16[72,1408]{1,0:T(8,128)(2,1)S(1)} %broadcast_select_fusion.1), channel_id=1, source_target_pairs={{7,5},{0,6},{15,13},{8,14},{23,21},{16,22},{31,29},{24,30},{39,37}... | collective-permute-start | bytes 608264 | tf_op jit(solution)/shard_map/ppermute | solution.py:230
  314.9 7.4 %collective-permute-start.36 = (bf16[72,1408]{1,0:T(8,128)(2,1)S(1)}, bf16[72,1408]{1,0:T(8,128)(2,1)S(1)}, u32[]{:S(2)}, u32[]{:S(2)}) collective-permute-start(bf16[72,1408]{1,0:T(8,128)(2,1)S(1)} %broadcast_select_fusion), channel_id=1, source_target_pairs={{7,6},{0,7},{15,14},{8,15},{23,22},{16,23},{31,30},{24,31},{39,38}... | collective-permute-start | bytes 608264 | tf_op jit(solution)/shard_map/ppermute | solution.py:230
  324.9 19.1 %all-to-all-start.2 = ((bf16[32,2,1,1408]{3,1,2,0:T(2,128)(2,1)}), bf16[32,2,1,1408]{3,1,2,0:T(2,128)(2,1)S(1)}, u32[]{:S(2)}, u32[]{:S(2)}) async-start(bf16[32,2,1,1408]{3,1,2,0:T(2,128)(2,1)} %bitcast.40), calls=%async_computation.2 | async-start | bytes 360448 | tf_op jit(solution)/shard_map/all_to_all | solution.py:175
  345.4 33.8 %all-to-all-start.3 = ((bf16[4,32,2,1,1408]{4,0,2,3,1:T(4,128)(2,1)}), bf16[4,32,2,1,1408]{4,0,2,3,1:T(4,128)(2,1)S(1)}, u32[]{:S(2)}, u32[]{:S(2)}) async-start(bf16[4,32,2,1,1408]{4,0,2,3,1:T(4,128)(2,1)} %bitcast.52), calls=%async_computation.3 | async-start | bytes 1441792 | tf_op jit(solution)/shard_map/all_to_all | solution.py:175
  352.9 19.5 %collective-permute-start.39 = (bf16[16,1408]{1,0:T(8,128)(2,1)S(1)}, bf16[16,1408]{1,0:T(8,128)(2,1)S(1)}, u32[]{:S(2)}, u32[]{:S(2)}) collective-permute-start(bf16[16,1408]{1,0:T(8,128)(2,1)S(1)} %get-tuple-element.206), channel_id=1, source_target_pairs={{24,0},{32,8},{40,16},{48,24},{56,32},{64,40},{72,48},{80,56},{88,... | collective-permute-start | bytes 135176 | tf_op jit(solution)/shard_map/ppermute | solution.py:14
  354.2 20.1 %collective-permute-start.38 = (bf16[16,1408]{1,0:T(8,128)(2,1)S(1)}, bf16[16,1408]{1,0:T(8,128)(2,1)S(1)}, u32[]{:S(2)}, u32[]{:S(2)}) collective-permute-start(bf16[16,1408]{1,0:T(8,128)(2,1)S(1)} %get-tuple-element.207), channel_id=1, source_target_pairs={{16,0},{24,8},{32,16},{40,24},{48,32},{56,40},{64,48},{72,56},{80,... | collective-permute-start | bytes 135176 | tf_op jit(solution)/shard_map/ppermute | solution.py:14
  355.5 18.8 %collective-permute-start.37 = (bf16[16,1408]{1,0:T(8,128)(2,1)S(1)}, bf16[16,1408]{1,0:T(8,128)(2,1)S(1)}, u32[]{:S(2)}, u32[]{:S(2)}) collective-permute-start(bf16[16,1408]{1,0:T(8,128)(2,1)S(1)} %get-tuple-element.208), channel_id=1, source_target_pairs={{8,0},{16,8},{24,16},{32,24},{40,32},{48,40},{56,48},{64,56},{72,6... | collective-permute-start | bytes 135176 | tf_op jit(solution)/shard_map/ppermute | solution.py:14
  361.4 16.9 %collective-permute-start.42 = (bf16[16,1408]{1,0:T(8,128)(2,1)S(1)}, bf16[16,1408]{1,0:T(8,128)(2,1)S(1)}, u32[]{:S(2)}, u32[]{:S(2)}) collective-permute-start(bf16[16,1408]{1,0:T(8,128)(2,1)S(1)} %get-tuple-element.202), channel_id=1, source_target_pairs={{0,24},{8,32},{16,40},{24,48},{32,56},{40,64},{48,72},{56,80},{64,... | collective-permute-start | bytes 135176 | tf_op jit(solution)/shard_map/ppermute | solution.py:14
  367.4 10.9 %collective-permute-start.41 = (bf16[16,1408]{1,0:T(8,128)(2,1)S(1)}, bf16[16,1408]{1,0:T(8,128)(2,1)S(1)}, u32[]{:S(2)}, u32[]{:S(2)}) collective-permute-start(bf16[16,1408]{1,0:T(8,128)(2,1)S(1)} %get-tuple-element.203), channel_id=1, source_target_pairs={{0,16},{8,24},{16,32},{24,40},{32,48},{40,56},{48,64},{56,72},{64,... | collective-permute-start | bytes 135176 | tf_op jit(solution)/shard_map/ppermute | solution.py:14
  (14 other events, 512.3 us)
Sparse Core Ops, SparseCore 0:
  18.9 94.1 all-gather.5
  124.9 82.3 all-gather.7

commit v3 on v2

--- a/solution.py
+++ b/solution.py
@@ -76,7 +76,7 @@
         ],
         out_specs=pl.BlockSpec(memory_space=pltpu.VMEM),
         scratch_shapes=[pltpu.SemaphoreType.DMA((2,))],
-        compiler_params=pltpu.CompilerParams(vmem_limit_bytes=16 << 20),
+        compiler_params=pltpu.CompilerParams(vmem_limit_bytes=4 << 20),
         cost_estimate=pl.CostEstimate(flops=0, bytes_accessed=2 * rows * columns * 2, transcendentals=0),
     )(core, *(pltpu.with_memory_space_constraint(part, pltpu.HBM) for part in (mine, other)))
 
@@ -87,14 +87,7 @@
     rows, channels = incoming_ref.shape
     kept_rows = own_ref.shape[0]
     padded_rows = taps_ref.shape[0]
-    fresh, low_half = (flags_ref[i] != 0 for i in range(2))
-    acts = jnp.where(fresh, fresh_ref[...].astype(jnp.float32), incoming_ref[...].astype(jnp.float32))
-    acts_ref[...] = acts
-    normed = rms_scaled(acts, gain_ref[...])
-    normed = jnp.concatenate([normed, jnp.zeros((padded_rows - rows, channels), jnp.float32)], axis=0)
-    taps_ref[:, :channels] = pltpu.roll(normed, 1, 0).astype(jnp.bfloat16)
-    taps_ref[:, channels : 2 * channels] = normed.astype(jnp.bfloat16)
-    taps_ref[:, 2 * channels :] = pltpu.roll(normed, padded_rows - 1, 0).astype(jnp.bfloat16)
+    fresh, low_half, active = (flags_ref[i] != 0 for i in range(3))
 
     def columns(at):
         mixed = jnp.dot(taps_ref[...], weights_ref[:, at], preferred_element_type=jnp.float32)
@@ -103,15 +96,32 @@
         own_ref[:, at] = own.astype(jnp.bfloat16)
         result_ref[:, at] = result.astype(jnp.bfloat16)
 
-    whole = channels // wide_columns
-
-    def step(i, _):
-        columns(pl.ds(pl.multiple_of(i * wide_columns, wide_columns), wide_columns))
-        return 0
-
-    lax.fori_loop(0, whole, step, 0)
-    if channels > whole * wide_columns:
-        columns(pl.ds(whole * wide_columns, channels - whole * wide_columns))
+    @pl.when(active)
+    def _():
+        acts = jnp.where(
+            fresh, fresh_ref[...].astype(jnp.float32), incoming_ref[...].astype(jnp.float32)
+        )
+        acts_ref[...] = acts
+        normed = rms_scaled(acts, gain_ref[...])
+        spare = jnp.zeros((padded_rows - rows, channels), jnp.float32)
+        normed = jnp.concatenate([normed, spare], axis=0)
+        taps_ref[:, :channels] = pltpu.roll(normed, 1, 0).astype(jnp.bfloat16)
+        taps_ref[:, channels : 2 * channels] = normed.astype(jnp.bfloat16)
+        taps_ref[:, 2 * channels :] = pltpu.roll(normed, padded_rows - 1, 0).astype(jnp.bfloat16)
+        whole = channels // wide_columns
+
+        def step(i, _):
+            columns(pl.ds(pl.multiple_of(i * wide_columns, wide_columns), wide_columns))
+            return 0
+
+        lax.fori_loop(0, whole, step, 0)
+        if channels > whole * wide_columns:
+            columns(pl.ds(whole * wide_columns, channels - whole * wide_columns))
+
+    @pl.when(jnp.logical_not(active))
+    def _():
+        result_ref[...] = jnp.zeros_like(result_ref)
+        own_ref[...] = jnp.zeros_like(own_ref)
 
 
 def block(flags, weights, gains, incoming, fresh, kept_rows):
@@ -130,7 +140,7 @@
             pltpu.VMEM((padded_rows, weights.shape[0]), jnp.bfloat16),
             pltpu.VMEM((rows, channels), jnp.float32),
         ],
-        compiler_params=pltpu.CompilerParams(vmem_limit_bytes=20 << 20),
+        compiler_params=pltpu.CompilerParams(vmem_limit_bytes=8 << 20),
         cost_estimate=pl.CostEstimate(
             flops=2 * rows * weights.shape[0] * channels,
             bytes_accessed=4 * rows * channels * 2,
@@ -205,11 +215,13 @@
     pairs = micro_count // 2
     ticks = pairs + last
     early = pairs // 2
-    flags = jnp.stack([section_pos == 0, low_half]).astype(jnp.int32)
     results, owns, landing, landed = [], [], [], []
     incoming = [jnp.zeros_like(wide)] * 2
     for tick in range(ticks):
         owns.append([])
+        busy = [i for i in range(sections) if 0 <= tick - i < pairs]
+        active = (section_pos >= busy[0]) & (section_pos <= busy[-1])
+        flags = jnp.stack([section_pos == 0, low_half, active]).astype(jnp.int32)
         for lane in range(2):
             entered = 2 * tick + lane
             before = incoming[lane]
@@ -223,7 +235,9 @@
             results.append(result)
             owns[-1].append(own)
             if tick < ticks - 1:
-                incoming[lane] = lax.ppermute(result, "section", [(i, i + 1) for i in range(last)])
+                incoming[lane] = lax.ppermute(
+                    result, "section", [(i, i + 1) for i in busy if i < last]
+                )
             done = entered - 2 * last
             if 0 <= done < micro_count - 1:
                 leaving = jnp.where(section_pos == 0, results[done + 1], result)

time: 390 us -> 440 us (1.13)
  starting transfers between devices: 142 us -> 239 us
  Pallas kernels: 90 us -> 44.2 us
    ppermute x6, starting transfers between devices: 16 us -> 102 us  [from_behind(): return lax.ppermute(shard, axis, pairs)]
    pallas_call x22, Pallas kernels: 85.5 us -> 39.7 us  [block(): pl.pallas_call(functools.partial(block_kernel, 256), out_shape=(jax.Shape...]
    ppermute x7, starting transfers between devices: 13.6 us -> 49.5 us  [on_device(): lax.ppermute(leaving, 'section', [(last, done), (0, done + 1)])]
    ppermute x20, starting transfers between devices: 50.2 us -> 24.2 us  [on_device(): lax.ppermute(result, 'section', [(i, i + 1) for i in busy if i < last])]
    all_gather x1, waiting for transfers between devices: 63.2 us -> 46.6 us  [gathered_columns(): lax.all_gather(rows, 'seq', axis_index_groups=same_core, axis=0, tiled=True)]
    ppermute x1, starting transfers between devices: 3.53 us -> 13.8 us  [on_device(): lax.ppermute(jnp.where(low_half, chains[slab_rows - spare:], chains[:spar...]
    ppermute x7, waiting for transfers between devices: 3.86 us -> 13.1 us  [on_device(): lax.ppermute(leaving, 'section', [(last, done), (0, done + 1)])]
    all_to_all x3, starting transfers between devices: 34.2 us -> 25.1 us  [to_slabs(): rows = lax.all_to_all(blocks, 'seq', at, at + 1, axis_index_groups=halves)]
  transfers between devices with their start and end apart: 49 -> 49, of which waited for: 11 -> 12; matrix products, arithmetic and copies ran while one was open for 9% -> 8% of each run, Pallas kernels for 23% -> 10%
where the time goes in v3:
time: 440 us; the launch traced here: 438 us
  starting transfers between devices  239 us (54%)
  waiting for transfers between devices  94 us (21%)
  Pallas kernels  44.2 us (10%)
  local copies, waits for them, and re-layouts  28.4 us (6%)
  between operations  15.3 us (3%)
  other arithmetic  9 us (2%)
  matrix products  7.67 us (2%)
    ppermute x6, starting transfers between devices, from_behind(): return lax.ppermute(shard, axis, pairs)  102 us
    ppermute x7, starting transfers between devices, on_device(): lax.ppermute(leaving, 'section', [(last, done), (0, done + 1)])  49.5 us
    all_gather x1, waiting for transfers between devices, gathered_columns(): lax.all_gather(rows, 'seq', axis_index_groups=same_core, axis=0, tiled=True)  46.6 us
    pallas_call x22, Pallas kernels, block(): pl.pallas_call(functools.partial(block_kernel, 256), out_shape=(jax.Shape...  39.7 us
    all_to_all x3, starting transfers between devices, to_slabs(): rows = lax.all_to_all(blocks, 'seq', at, at + 1, axis_index_groups=halves)  25.1 us
    ppermute x20, starting transfers between devices, on_device(): lax.ppermute(result, 'section', [(i, i + 1) for i in busy if i < last])  24.2 us
    ppermute x1, starting transfers between devices, on_device(): lax.ppermute(jnp.where(low_half, chains[slab_rows - spare:], chains[:spar...  13.8 us
    ppermute x7, waiting for transfers between devices, on_device(): lax.ppermute(leaving, 'section', [(last, done), (0, done + 1)])  13.1 us
  transfers between devices with their start and end apart: 49, of which 12 were waited for; matrix products, arithmetic and copies ran while one was open for 8% of the time, Pallas kernels for 10%

profile of v3, /device:TPU:1, one launch (start us, length us, event | category | flops | bytes accessed | tf_op | source)
XLA Modules:
  0.0 438.1 jit_solution(8407592209463408774)
XLA Ops:
  8.3 8.8 %collective-permute-start = (bf16[66,768]{1,0:T(8,128)(2,1)S(1)}, bf16[66,768]{1,0:T(8,128)(2,1)S(1)}, u32[]{:S(2)}, u32[]{:S(2)}) collective-permute-start(bf16[66,768]{1,0:T(8,128)(2,1)S(1)} %get-tuple-element.202), channel_id=1, source_target_pairs={{0,8},{8,0},{16,24},{24,16},{32,40},{40,32},{48,56},{56,48},{64,72... | collective-permute-start | bytes 304136 | tf_op jit(solution)/shard_map/ppermute | solution.py:22
  19.7 3.9 all-to-all-start
  23.6 9.9 %all-to-all-done = bf16[1,2,32,1408]{3,1,0,2:T(2,128)(2,1)S(1)} async-done(((bf16[1,2,32,1408]{3,1,0,2:T(2,128)(2,1)}), bf16[1,2,32,1408]{3,1,0,2:T(2,128)(2,1)S(1)}, u32[]{:S(2)}, u32[]{:S(2)}) %all-to-all-start) | async-done | bytes 180256 | tf_op jit(solution)/shard_map/all_to_all | solution.py:178
  33.6 13.8 %collective-permute-start.1 = (bf16[8,1408]{1,0:T(8,128)(2,1)S(1)}, bf16[8,1408]{1,0:T(8,128)(2,1)S(1)}, u32[]{:S(2)}, u32[]{:S(2)}) collective-permute-start(bf16[8,1408]{1,0:T(8,128)(2,1)S(1)} %select_n.143), channel_id=1, source_target_pairs={{0,256},{8,264},{16,272},{24,280},{32,288},{40,296},{48,304},{56,3... | collective-permute-start | bytes 67592 | tf_op jit(solution)/shard_map/ppermute | solution.py:193
  47.4 4.0 collective-permute-done.1
  59.9 5.2 %collective-permute-done.3.fresh_ref = bf16[72,1408]{1,0:T(8,128)(2,1)S(1)} collective-permute-done((bf16[72,1408]{1,0:T(8,128)(2,1)S(1)}, bf16[72,1408]{1,0:T(8,128)(2,1)S(1)}, u32[]{:S(2)}, u32[]{:S(2)}) %collective-permute-start.3) | collective-permute-done | bytes 202784 | tf_op jit(solution)/shard_map/ppermute | solution.py:203
  66.4 46.6 %all-gather.6.cloned.1.call-done = bf16[32,132,768]{2,1,0:T(8,128)(2,1)} async-done(((bf16[1,132,768]{2,1,0:T(8,128)(2,1)}), bf16[32,132,768]{2,1,0:T(8,128)(2,1)}) %all-gather.6.cloned.1.call-update) | async-done | bytes 6488080 | tf_op jit(solution)/shard_map/all_gather | solution.py:41
  113.0 8.3 %reshape.80.mine_ref = bf16[4224,768]{1,0:T(8,128)(2,1)} reshape(bf16[32,132,768]{2,1,0:T(8,128)(2,1)} %all-gather.6.cloned.1.call-done) | data formatting | bytes 12976128 | tf_op jit(solution)/shard_map/optimization_barrier | solution.py:204
  121.4 2.9 collective-permute-start.9
  124.8 9.9 %collective-permute-done.9.other_ref = bf16[4224,768]{1,0:T(8,128)(2,1)} collective-permute-done((bf16[4224,768]{1,0:T(8,128)(2,1)}, bf16[4224,768]{1,0:T(8,128)(2,1)}, u32[]{:S(2)}, u32[]{:S(2)}) %collective-permute-start.9) | collective-permute-done | bytes 6488096 | tf_op jit(solution)/shard_map/ppermute | solution.py:22
  134.7 4.5 %shard_map.104.weights_ref = bf16[4224,1408]{1,0:T(8,128)(2,1)S(1)} custom-call(s32[1]{0:T(128)} %bitcast.3.core_ref, bf16[4224,768]{1,0:T(8,128)(2,1)} %reshape.80.mine_ref, bf16[4224,768]{1,0:T(8,128)(2,1)} %collective-permute-done.9.other_ref), custom_call_target="tpu_custom_call" | custom-call | bytes 23789568 | tf_op jit(solution)/shard_map/pallas_call | solution.py:69
  139.3 3.9 shard_map.105
  144.5 3.9 shard_map.106
  149.8 3.9 shard_map.107
  153.8 3.3 collective-permute-start.11
  157.1 3.9 shard_map.108
  161.0 1.9 collective-permute-start.14
  163.0 3.9 shard_map.109
  166.9 1.9 collective-permute-start.13
  168.9 3.9 shard_map.110
  172.8 2.2 collective-permute-start.16
  175.1 3.9 shard_map.111
  179.1 1.9 collective-permute-start.15
  181.0 3.9 shard_map.112
  184.9 1.9 collective-permute-start.18
  198.7 20.7 %collective-permute-start.27 = (bf16[72,1408]{1,0:T(8,128)(2,1)S(1)}, bf16[72,1408]{1,0:T(8,128)(2,1)}, u32[]{:S(2)}, u32[]{:S(2)}) collective-permute-start(bf16[72,1408]{1,0:T(8,128)(2,1)S(1)} %broadcast_select_fusion.5), channel_id=1, source_target_pairs={{7,1},{0,2},{15,9},{8,10},{23,17},{16,18},{31,25},{24,26},{39,33},... | collective-permute-start | bytes 608264 | tf_op jit(solution)/shard_map/ppermute | solution.py:244
  219.5 1.9 collective-permute-start.23
  222.8 9.4 %collective-permute-done.23 = bf16[72,1408]{1,0:T(8,128)(2,1)S(1)} collective-permute-done((bf16[72,1408]{1,0:T(8,128)(2,1)S(1)}, bf16[72,1408]{1,0:T(8,128)(2,1)S(1)}, u32[]{:S(2)}, u32[]{:S(2)}) %collective-permute-start.23) | collective-permute-done | bytes 202784 | tf_op jit(solution)/shard_map/ppermute | solution.py:244
  233.0 2.0 collective-permute-start.29
  237.0 7.8 %collective-permute-start.31 = (bf16[72,1408]{1,0:T(8,128)(2,1)}, bf16[72,1408]{1,0:T(8,128)(2,1)}, u32[]{:S(2)}, u32[]{:S(2)}) collective-permute-start(bf16[72,1408]{1,0:T(8,128)(2,1)} %broadcast_select_fusion.3), channel_id=1, source_target_pairs={{7,3},{0,4},{15,11},{8,12},{23,19},{16,20},{31,27},{24,28},{39,35}... | collective-permute-start | bytes 608264 | tf_op jit(solution)/shard_map/ppermute | solution.py:244
  244.8 1.7 copy-done.5
  248.2 9.4 %all-to-all-start.1 = ((bf16[4,32,2,1,1408]{4,2,0,3,1:T(2,128)(2,1)}), bf16[4,32,2,1,1408]{4,2,0,3,1:T(2,128)(2,1)S(1)}, u32[]{:S(2)}, u32[]{:S(2)}) async-start(bf16[4,32,2,1,1408]{4,2,0,3,1:T(2,128)(2,1)} %copy.22), calls=%async_computation.1 | async-start | bytes 1441792 | tf_op jit(solution)/shard_map/all_to_all | solution.py:185
  257.7 4.4 copy-done.3
  265.0 7.3 %collective-permute-start.33 = (bf16[72,1408]{1,0:T(8,128)(2,1)S(1)}, bf16[72,1408]{1,0:T(8,128)(2,1)S(1)}, u32[]{:S(2)}, u32[]{:S(2)}) collective-permute-start(bf16[72,1408]{1,0:T(8,128)(2,1)S(1)} %broadcast_select_fusion.2), channel_id=1, source_target_pairs={{7,4},{0,5},{15,12},{8,13},{23,20},{16,21},{31,28},{24,29},{39,36}... | collective-permute-start | bytes 608264 | tf_op jit(solution)/shard_map/ppermute | solution.py:244
  272.3 7.0 %collective-permute-start.35 = (bf16[72,1408]{1,0:T(8,128)(2,1)S(1)}, bf16[72,1408]{1,0:T(8,128)(2,1)S(1)}, u32[]{:S(2)}, u32[]{:S(2)}) collective-permute-start(bf16[72,1408]{1,0:T(8,128)(2,1)S(1)} %broadcast_select_fusion.1), channel_id=1, source_target_pairs={{7,5},{0,6},{15,13},{8,14},{23,21},{16,22},{31,29},{24,30},{39,37}... | collective-permute-start | bytes 608264 | tf_op jit(solution)/shard_map/ppermute | solution.py:244
  280.0 2.8 collective-permute-start.36
  284.2 3.7 collective-permute-done.36
  290.4 9.0 %all-to-all-start.2 = ((bf16[32,2,1,1408]{3,1,2,0:T(2,128)(2,1)}), bf16[32,2,1,1408]{3,1,2,0:T(2,128)(2,1)S(1)}, u32[]{:S(2)}, u32[]{:S(2)}) async-start(bf16[32,2,1,1408]{3,1,2,0:T(2,128)(2,1)} %bitcast.51), calls=%async_computation.2 | async-start | bytes 360448 | tf_op jit(solution)/shard_map/all_to_all | solution.py:185
  301.4 6.2 %reshape.59 = bf16[1408,1408]{1,0:T(8,128)(2,1)} reshape(bf16[64,22,1408]{2,1,0:T(8,128)(2,1)} %all-gather.8.cloned.1.call-done) | data formatting | bytes 7929856 | tf_op jit(solution)/shard_map/reshape | solution.py:252
  310.7 6.6 %all-to-all-start.3 = ((bf16[4,32,2,1,1408]{4,0,2,3,1:T(4,128)(2,1)}), bf16[4,32,2,1,1408]{4,0,2,3,1:T(4,128)(2,1)S(1)}, u32[]{:S(2)}, u32[]{:S(2)}) async-start(bf16[4,32,2,1,1408]{4,0,2,3,1:T(4,128)(2,1)} %bitcast.63), calls=%async_computation.3 | async-start | bytes 1441792 | tf_op jit(solution)/shard_map/all_to_all | solution.py:185
  318.2 17.8 %collective-permute-start.39 = (bf16[16,1408]{1,0:T(8,128)(2,1)S(1)}, bf16[16,1408]{1,0:T(8,128)(2,1)S(1)}, u32[]{:S(2)}, u32[]{:S(2)}) collective-permute-start(bf16[16,1408]{1,0:T(8,128)(2,1)S(1)} %get-tuple-element.208), channel_id=1, source_target_pairs={{24,0},{32,8},{40,16},{48,24},{56,32},{64,40},{72,48},{80,56},{88,... | collective-permute-start | bytes 135176 | tf_op jit(solution)/shard_map/ppermute | solution.py:14
  336.0 16.7 %collective-permute-start.38 = (bf16[16,1408]{1,0:T(8,128)(2,1)S(1)}, bf16[16,1408]{1,0:T(8,128)(2,1)S(1)}, u32[]{:S(2)}, u32[]{:S(2)}) collective-permute-start(bf16[16,1408]{1,0:T(8,128)(2,1)S(1)} %get-tuple-element.209), channel_id=1, source_target_pairs={{16,0},{24,8},{32,16},{40,24},{48,32},{56,40},{64,48},{72,56},{80,... | collective-permute-start | bytes 135176 | tf_op jit(solution)/shard_map/ppermute | solution.py:14
  352.7 17.4 %collective-permute-start.37 = (bf16[16,1408]{1,0:T(8,128)(2,1)S(1)}, bf16[16,1408]{1,0:T(8,128)(2,1)S(1)}, u32[]{:S(2)}, u32[]{:S(2)}) collective-permute-start(bf16[16,1408]{1,0:T(8,128)(2,1)S(1)} %get-tuple-element.210), channel_id=1, source_target_pairs={{8,0},{16,8},{24,16},{32,24},{40,32},{48,40},{56,48},{64,56},{72,6... | collective-permute-start | bytes 135176 | tf_op jit(solution)/shard_map/ppermute | solution.py:14
  370.1 2.8 convolution_convert_fusion
  373.9 16.7 %collective-permute-start.42 = (bf16[16,1408]{1,0:T(8,128)(2,1)S(1)}, bf16[16,1408]{1,0:T(8,128)(2,1)S(1)}, u32[]{:S(2)}, u32[]{:S(2)}) collective-permute-start(bf16[16,1408]{1,0:T(8,128)(2,1)S(1)} %get-tuple-element.204), channel_id=1, source_target_pairs={{0,24},{8,32},{16,40},{24,48},{32,56},{40,64},{48,72},{56,80},{64,... | collective-permute-start | bytes 135176 | tf_op jit(solution)/shard_map/ppermute | solution.py:14
  390.6 16.7 %collective-permute-start.41 = (bf16[16,1408]{1,0:T(8,128)(2,1)S(1)}, bf16[16,1408]{1,0:T(8,128)(2,1)S(1)}, u32[]{:S(2)}, u32[]{:S(2)}) collective-permute-start(bf16[16,1408]{1,0:T(8,128)(2,1)S(1)} %get-tuple-element.205), channel_id=1, source_target_pairs={{0,16},{8,24},{16,32},{24,40},{32,48},{40,56},{48,64},{56,72},{64,... | collective-permute-start | bytes 135176 | tf_op jit(solution)/shard_map/ppermute | solution.py:14
  407.4 16.7 %collective-permute-start.40 = (bf16[16,1408]{1,0:T(8,128)(2,1)S(1)}, bf16[16,1408]{1,0:T(8,128)(2,1)S(1)}, u32[]{:S(2)}, u32[]{:S(2)}) collective-permute-start(bf16[16,1408]{1,0:T(8,128)(2,1)S(1)} %get-tuple-element.206), channel_id=1, source_target_pairs={{0,8},{8,16},{16,24},{24,32},{32,40},{40,48},{48,56},{56,64},{64,7... | collective-permute-start | bytes 135176 | tf_op jit(solution)/shard_map/ppermute | solution.py:14
  424.6 3.5 fusion.46
  (170 shorter events, 51.9 us)
Async XLA Ops:
  7.2 105.9 %all-gather.6.cloned.1.call-start = ((), (), s32[]{:S(2)}) async-start(), calls=%async_computation.4 | async-start | bytes 6893568 | tf_op jit(solution)/shard_map/all_gather | solution.py:41
  8.3 9.7 %collective-permute-start = (bf16[66,768]{1,0:T(8,128)(2,1)S(1)}, bf16[66,768]{1,0:T(8,128)(2,1)S(1)}, u32[]{:S(2)}, u32[]{:S(2)}) collective-permute-start(bf16[66,768]{1,0:T(8,128)(2,1)S(1)} %get-tuple-element.202), channel_id=1, source_target_pairs={{0,8},{8,0},{16,24},{24,16},{32,40},{40,32},{48,56},{56,48},{64,72... | collective-permute-start | bytes 304136 | tf_op jit(solution)/shard_map/ppermute | solution.py:22
  19.7 13.8 %all-to-all-start = ((bf16[1,2,32,1408]{3,1,0,2:T(2,128)(2,1)}), bf16[1,2,32,1408]{3,1,0,2:T(2,128)(2,1)S(1)}, u32[]{:S(2)}, u32[]{:S(2)}) async-start(bf16[1,2,32,1408]{3,1,0,2:T(2,128)(2,1)} %copy.21), calls=%async_computation | async-start | bytes 360448 | tf_op jit(solution)/shard_map/all_to_all | solution.py:178
  23.6 266.1 %all-gather.8.cloned.1.call-start = ((), (), s32[]{:S(2)}) async-start(), calls=%async_computation.5 | async-start | bytes 4392960 | tf_op jit(solution)/shard_map/all_gather | solution.py:208
  33.6 17.8 %collective-permute-start.1 = (bf16[8,1408]{1,0:T(8,128)(2,1)S(1)}, bf16[8,1408]{1,0:T(8,128)(2,1)S(1)}, u32[]{:S(2)}, u32[]{:S(2)}) collective-permute-start(bf16[8,1408]{1,0:T(8,128)(2,1)S(1)} %select_n.143), channel_id=1, source_target_pairs={{0,256},{8,264},{16,272},{24,280},{32,288},{40,296},{48,304},{56,3... | collective-permute-start | bytes 67592 | tf_op jit(solution)/shard_map/ppermute | solution.py:193
  51.5 7.1 %collective-permute-start.2 = (bf16[72,1408]{1,0:T(8,128)(2,1)S(1)}, bf16[72,1408]{1,0:T(8,128)(2,1)S(1)}, u32[]{:S(2)}, u32[]{:S(2)}) collective-permute-start(bf16[72,1408]{1,0:T(8,128)(2,1)S(1)} %maximum_select_fusion.1.fresh_ref), channel_id=1, source_target_pairs={{1,0},{9,8},{17,16},{25,24},{33,32},{41,40},{49,48},{57,56},{65,64... | collective-permute-start | bytes 608264 | tf_op jit(solution)/shard_map/ppermute | solution.py:203
  52.9 12.2 %collective-permute-start.3 = (bf16[72,1408]{1,0:T(8,128)(2,1)S(1)}, bf16[72,1408]{1,0:T(8,128)(2,1)S(1)}, u32[]{:S(2)}, u32[]{:S(2)}) collective-permute-start(bf16[72,1408]{1,0:T(8,128)(2,1)S(1)} %maximum_select_fusion.1.fresh_ref), channel_id=1, source_target_pairs={{2,0},{10,8},{18,16},{26,24},{34,32},{42,40},{50,48},{58,56},{66,6... | collective-permute-start | bytes 608264 | tf_op jit(solution)/shard_map/ppermute | solution.py:203
  54.2 67.1 %collective-permute-start.4 = (bf16[72,1408]{1,0:T(8,128)(2,1)S(1)}, bf16[72,1408]{1,0:T(8,128)(2,1)S(1)}, u32[]{:S(2)}, u32[]{:S(2)}) collective-permute-start(bf16[72,1408]{1,0:T(8,128)(2,1)S(1)} %maximum_select_fusion.1.fresh_ref), channel_id=1, source_target_pairs={{3,0},{11,8},{19,16},{27,24},{35,32},{43,40},{51,48},{59,56},{67,6... | collective-permute-start | bytes 608264 | tf_op jit(solution)/shard_map/ppermute | solution.py:203
  55.5 65.8 %collective-permute-start.5 = (bf16[72,1408]{1,0:T(8,128)(2,1)S(1)}, bf16[72,1408]{1,0:T(8,128)(2,1)S(1)}, u32[]{:S(2)}, u32[]{:S(2)}) collective-permute-start(bf16[72,1408]{1,0:T(8,128)(2,1)S(1)} %maximum_select_fusion.1.fresh_ref), channel_id=1, source_target_pairs={{4,0},{12,8},{20,16},{28,24},{36,32},{44,40},{52,48},{60,56},{68,6... | collective-permute-start | bytes 608264 | tf_op jit(solution)/shard_map/ppermute | solution.py:203
  56.8 64.5 %collective-permute-start.6 = (bf16[72,1408]{1,0:T(8,128)(2,1)S(1)}, bf16[72,1408]{1,0:T(8,128)(2,1)S(1)}, u32[]{:S(2)}, u32[]{:S(2)}) collective-permute-start(bf16[72,1408]{1,0:T(8,128)(2,1)S(1)} %maximum_select_fusion.1.fresh_ref), channel_id=1, source_target_pairs={{5,0},{13,8},{21,16},{29,24},{37,32},{45,40},{53,48},{61,56},{69,6... | collective-permute-start | bytes 608264 | tf_op jit(solution)/shard_map/ppermute | solution.py:203
  58.6 62.8 %collective-permute-start.7 = (bf16[72,1408]{1,0:T(8,128)(2,1)S(1)}, bf16[72,1408]{1,0:T(8,128)(2,1)S(1)}, u32[]{:S(2)}, u32[]{:S(2)}) collective-permute-start(bf16[72,1408]{1,0:T(8,128)(2,1)S(1)} %maximum_select_fusion.1.fresh_ref), channel_id=1, source_target_pairs={{6,0},{14,8},{22,16},{30,24},{38,32},{46,40},{54,48},{62,56},{70,6... | collective-permute-start | bytes 608264 | tf_op jit(solution)/shard_map/ppermute | solution.py:203
  65.1 56.3 %collective-permute-start.8 = (bf16[72,1408]{1,0:T(8,128)(2,1)S(1)}, bf16[72,1408]{1,0:T(8,128)(2,1)S(1)}, u32[]{:S(2)}, u32[]{:S(2)}) collective-permute-start(bf16[72,1408]{1,0:T(8,128)(2,1)S(1)} %maximum_select_fusion.1.fresh_ref), channel_id=1, source_target_pairs={{7,0},{15,8},{23,16},{31,24},{39,32},{47,40},{55,48},{63,56},{71,6... | collective-permute-start | bytes 608264 | tf_op jit(solution)/shard_map/ppermute | solution.py:203
  121.4 13.3 %collective-permute-start.9 = (bf16[4224,768]{1,0:T(8,128)(2,1)}, bf16[4224,768]{1,0:T(8,128)(2,1)}, u32[]{:S(2)}, u32[]{:S(2)}) collective-permute-start(bf16[4224,768]{1,0:T(8,128)(2,1)} %reshape.80.mine_ref), channel_id=1, source_target_pairs={{0,8},{8,0},{16,24},{24,16},{32,40},{40,32},{48,56},{56,48},{64,72... | collective-permute-start | bytes 19464200 | tf_op jit(solution)/shard_map/ppermute | solution.py:22
  143.2 6.6 %collective-permute-start.10 = (bf16[72,1408]{1,0:T(8,128)(2,1)S(1)}, bf16[72,1408]{1,0:T(8,128)(2,1)S(1)}, u32[]{:S(2)}, u32[]{:S(2)}) collective-permute-start(bf16[72,1408]{1,0:T(8,128)(2,1)S(1)} %get-tuple-element.95), channel_id=1, source_target_pairs={{0,1},{8,9},{16,17},{24,25},{32,33},{40,41},{48,49},{56,57},{64,65... | collective-permute-start | bytes 608264 | tf_op jit(solution)/shard_map/ppermute | solution.py:238
  148.5 8.6 %collective-permute-start.12 = (bf16[72,1408]{1,0:T(8,128)(2,1)S(1)}, bf16[72,1408]{1,0:T(8,128)(2,1)S(1)}, u32[]{:S(2)}, u32[]{:S(2)}) collective-permute-start(bf16[72,1408]{1,0:T(8,128)(2,1)S(1)} %get-tuple-element.98), channel_id=1, source_target_pairs={{0,1},{8,9},{16,17},{24,25},{32,33},{40,41},{48,49},{56,57},{64,65... | collective-permute-start | bytes 608264 | tf_op jit(solution)/shard_map/ppermute | solution.py:238
  153.8 9.2 %collective-permute-start.11 = (bf16[72,1408]{1,0:T(8,128)(2,1)S(1)}, bf16[72,1408]{1,0:T(8,128)(2,1)S(1)}, u32[]{:S(2)}, u32[]{:S(2)}) collective-permute-start(bf16[72,1408]{1,0:T(8,128)(2,1)S(1)} %get-tuple-element.101), channel_id=1, source_target_pairs={{0,1},{1,2},{8,9},{9,10},{16,17},{17,18},{24,25},{25,26},{32,33},{... | collective-permute-start | bytes 608264 | tf_op jit(solution)/shard_map/ppermute | solution.py:238
  161.0 7.8 %collective-permute-start.14 = (bf16[72,1408]{1,0:T(8,128)(2,1)S(1)}, bf16[72,1408]{1,0:T(8,128)(2,1)S(1)}, u32[]{:S(2)}, u32[]{:S(2)}) collective-permute-start(bf16[72,1408]{1,0:T(8,128)(2,1)S(1)} %get-tuple-element.104), channel_id=1, source_target_pairs={{0,1},{1,2},{8,9},{9,10},{16,17},{17,18},{24,25},{25,26},{32,33},{... | collective-permute-start | bytes 608264 | tf_op jit(solution)/shard_map/ppermute | solution.py:238
  166.9 8.2 %collective-permute-start.13 = (bf16[72,1408]{1,0:T(8,128)(2,1)S(1)}, bf16[72,1408]{1,0:T(8,128)(2,1)S(1)}, u32[]{:S(2)}, u32[]{:S(2)}) collective-permute-start(bf16[72,1408]{1,0:T(8,128)(2,1)S(1)} %get-tuple-element.107), channel_id=1, source_target_pairs={{0,1},{1,2},{2,3},{8,9},{9,10},{10,11},{16,17},{17,18},{18,19},{24... | collective-permute-start | bytes 608264 | tf_op jit(solution)/shard_map/ppermute | solution.py:238
  172.8 8.2 %collective-permute-start.16 = (bf16[72,1408]{1,0:T(8,128)(2,1)S(1)}, bf16[72,1408]{1,0:T(8,128)(2,1)S(1)}, u32[]{:S(2)}, u32[]{:S(2)}) collective-permute-start(bf16[72,1408]{1,0:T(8,128)(2,1)S(1)} %get-tuple-element.110), channel_id=1, source_target_pairs={{0,1},{1,2},{2,3},{8,9},{9,10},{10,11},{16,17},{17,18},{18,19},{24... | collective-permute-start | bytes 608264 | tf_op jit(solution)/shard_map/ppermute | solution.py:238
  179.1 7.9 %collective-permute-start.15 = (bf16[72,1408]{1,0:T(8,128)(2,1)S(1)}, bf16[72,1408]{1,0:T(8,128)(2,1)S(1)}, u32[]{:S(2)}, u32[]{:S(2)}) collective-permute-start(bf16[72,1408]{1,0:T(8,128)(2,1)S(1)} %get-tuple-element.113), channel_id=1, source_target_pairs={{0,1},{1,2},{2,3},{3,4},{8,9},{9,10},{10,11},{11,12},{16,17},{17,1... | collective-permute-start | bytes 608264 | tf_op jit(solution)/shard_map/ppermute | solution.py:238
  184.9 4.6 %collective-permute-start.18 = (bf16[72,1408]{1,0:T(8,128)(2,1)S(1)}, bf16[72,1408]{1,0:T(8,128)(2,1)S(1)}, u32[]{:S(2)}, u32[]{:S(2)}) collective-permute-start(bf16[72,1408]{1,0:T(8,128)(2,1)S(1)} %get-tuple-element.116), channel_id=1, source_target_pairs={{0,1},{1,2},{2,3},{3,4},{8,9},{9,10},{10,11},{11,12},{16,17},{17,1... | collective-permute-start | bytes 608264 | tf_op jit(solution)/shard_map/ppermute | solution.py:238
  187.7 3.1 collective-permute-start.17
  191.5 2.0 collective-permute-start.19
  192.7 2.0 collective-permute-start.22
  194.1 2.0 collective-permute-start.21
  195.4 2.0 collective-permute-start.24
  196.7 24.8 %collective-permute-start.26 = (bf16[72,1408]{1,0:T(8,128)(2,1)S(1)}, bf16[72,1408]{1,0:T(8,128)(2,1)S(1)}, u32[]{:S(2)}, u32[]{:S(2)}) collective-permute-start(bf16[72,1408]{1,0:T(8,128)(2,1)S(1)} %get-tuple-element.130), channel_id=1, source_target_pairs={{4,5},{5,6},{6,7},{12,13},{13,14},{14,15},{20,21},{21,22},{22,23},... | collective-permute-start | bytes 608264 | tf_op jit(solution)/shard_map/ppermute | solution.py:238
  198.0 24.8 %collective-permute-start.25 = (bf16[72,1408]{1,0:T(8,128)(2,1)S(1)}, bf16[72,1408]{1,0:T(8,128)(2,1)S(1)}, u32[]{:S(2)}, u32[]{:S(2)}) collective-permute-start(bf16[72,1408]{1,0:T(8,128)(2,1)S(1)} %get-tuple-element.132), channel_id=1, source_target_pairs={{4,5},{5,6},{6,7},{12,13},{13,14},{14,15},{20,21},{21,22},{22,23},... | collective-permute-start | bytes 608264 | tf_op jit(solution)/shard_map/ppermute | solution.py:238
  198.7 59.0 %collective-permute-start.27 = (bf16[72,1408]{1,0:T(8,128)(2,1)S(1)}, bf16[72,1408]{1,0:T(8,128)(2,1)}, u32[]{:S(2)}, u32[]{:S(2)}) collective-permute-start(bf16[72,1408]{1,0:T(8,128)(2,1)S(1)} %broadcast_select_fusion.5), channel_id=1, source_target_pairs={{7,1},{0,2},{15,9},{8,10},{23,17},{16,18},{31,25},{24,26},{39,33},... | collective-permute-start | bytes 608264 | tf_op jit(solution)/shard_map/ppermute | solution.py:244
  219.5 12.8 %collective-permute-start.23 = (bf16[72,1408]{1,0:T(8,128)(2,1)S(1)}, bf16[72,1408]{1,0:T(8,128)(2,1)S(1)}, u32[]{:S(2)}, u32[]{:S(2)}) collective-permute-start(bf16[72,1408]{1,0:T(8,128)(2,1)S(1)} %broadcast_select_fusion.6), channel_id=1, source_target_pairs={{7,0},{0,1},{15,8},{8,9},{23,16},{16,17},{31,24},{24,25},{39,32},{... | collective-permute-start | bytes 608264 | tf_op jit(solution)/shard_map/ppermute | solution.py:244
  222.1 35.5 %collective-permute-start.28 = (bf16[72,1408]{1,0:T(8,128)(2,1)S(1)}, bf16[72,1408]{1,0:T(8,128)(2,1)S(1)}, u32[]{:S(2)}, u32[]{:S(2)}) collective-permute-start(bf16[72,1408]{1,0:T(8,128)(2,1)S(1)} %get-tuple-element.134), channel_id=1, source_target_pairs={{5,6},{6,7},{13,14},{14,15},{21,22},{22,23},{29,30},{30,31},{37,38... | collective-permute-start | bytes 608264 | tf_op jit(solution)/shard_map/ppermute | solution.py:238
  233.0 30.5 %collective-permute-start.29 = (bf16[72,1408]{1,0:T(8,128)(2,1)}, bf16[72,1408]{1,0:T(8,128)(2,1)}, u32[]{:S(2)}, u32[]{:S(2)}) collective-permute-start(bf16[72,1408]{1,0:T(8,128)(2,1)} %broadcast_select_fusion.4), channel_id=1, source_target_pairs={{7,2},{0,3},{15,10},{8,11},{23,18},{16,19},{31,26},{24,27},{39,34}... | collective-permute-start | bytes 608264 | tf_op jit(solution)/shard_map/ppermute | solution.py:244
  235.6 27.9 %collective-permute-start.30 = (bf16[72,1408]{1,0:T(8,128)(2,1)S(1)}, bf16[72,1408]{1,0:T(8,128)(2,1)S(1)}, u32[]{:S(2)}, u32[]{:S(2)}) collective-permute-start(bf16[72,1408]{1,0:T(8,128)(2,1)S(1)} %get-tuple-element.138), channel_id=1, source_target_pairs={{5,6},{6,7},{13,14},{14,15},{21,22},{22,23},{29,30},{30,31},{37,38... | collective-permute-start | bytes 608264 | tf_op jit(solution)/shard_map/ppermute | solution.py:238
  237.0 42.4 %collective-permute-start.31 = (bf16[72,1408]{1,0:T(8,128)(2,1)}, bf16[72,1408]{1,0:T(8,128)(2,1)}, u32[]{:S(2)}, u32[]{:S(2)}) collective-permute-start(bf16[72,1408]{1,0:T(8,128)(2,1)} %broadcast_select_fusion.3), channel_id=1, source_target_pairs={{7,3},{0,4},{15,11},{8,12},{23,19},{16,20},{31,27},{24,28},{39,35}... | collective-permute-start | bytes 608264 | tf_op jit(solution)/shard_map/ppermute | solution.py:244
  248.2 41.4 %all-to-all-start.1 = ((bf16[4,32,2,1,1408]{4,2,0,3,1:T(2,128)(2,1)}), bf16[4,32,2,1,1408]{4,2,0,3,1:T(2,128)(2,1)S(1)}, u32[]{:S(2)}, u32[]{:S(2)}) async-start(bf16[4,32,2,1,1408]{4,2,0,3,1:T(2,128)(2,1)} %copy.22), calls=%async_computation.1 | async-start | bytes 1441792 | tf_op jit(solution)/shard_map/all_to_all | solution.py:185
  262.7 16.7 %collective-permute-start.32 = (bf16[72,1408]{1,0:T(8,128)(2,1)S(1)}, bf16[72,1408]{1,0:T(8,128)(2,1)S(1)}, u32[]{:S(2)}, u32[]{:S(2)}) collective-permute-start(bf16[72,1408]{1,0:T(8,128)(2,1)S(1)} %get-tuple-element.142), channel_id=1, source_target_pairs={{6,7},{14,15},{22,23},{30,31},{38,39},{46,47},{54,55},{62,63},{70,... | collective-permute-start | bytes 608264 | tf_op jit(solution)/shard_map/ppermute | solution.py:238
  264.1 19.5 %collective-permute-start.34 = (bf16[72,1408]{1,0:T(8,128)(2,1)S(1)}, bf16[72,1408]{1,0:T(8,128)(2,1)S(1)}, u32[]{:S(2)}, u32[]{:S(2)}) collective-permute-start(bf16[72,1408]{1,0:T(8,128)(2,1)S(1)} %get-tuple-element.146), channel_id=1, source_target_pairs={{6,7},{14,15},{22,23},{30,31},{38,39},{46,47},{54,55},{62,63},{70,... | collective-permute-start | bytes 608264 | tf_op jit(solution)/shard_map/ppermute | solution.py:238
  265.0 18.6 %collective-permute-start.33 = (bf16[72,1408]{1,0:T(8,128)(2,1)S(1)}, bf16[72,1408]{1,0:T(8,128)(2,1)S(1)}, u32[]{:S(2)}, u32[]{:S(2)}) collective-permute-start(bf16[72,1408]{1,0:T(8,128)(2,1)S(1)} %broadcast_select_fusion.2), channel_id=1, source_target_pairs={{7,4},{0,5},{15,12},{8,13},{23,20},{16,21},{31,28},{24,29},{39,36}... | collective-permute-start | bytes 608264 | tf_op jit(solution)/shard_map/ppermute | solution.py:244
  272.3 11.9 %collective-permute-start.35 = (bf16[72,1408]{1,0:T(8,128)(2,1)S(1)}, bf16[72,1408]{1,0:T(8,128)(2,1)S(1)}, u32[]{:S(2)}, u32[]{:S(2)}) collective-permute-start(bf16[72,1408]{1,0:T(8,128)(2,1)S(1)} %broadcast_select_fusion.1), channel_id=1, source_target_pairs={{7,5},{0,6},{15,13},{8,14},{23,21},{16,22},{31,29},{24,30},{39,37}... | collective-permute-start | bytes 608264 | tf_op jit(solution)/shard_map/ppermute | solution.py:244
  280.0 7.9 %collective-permute-start.36 = (bf16[72,1408]{1,0:T(8,128)(2,1)S(1)}, bf16[72,1408]{1,0:T(8,128)(2,1)S(1)}, u32[]{:S(2)}, u32[]{:S(2)}) collective-permute-start(bf16[72,1408]{1,0:T(8,128)(2,1)S(1)} %broadcast_select_fusion), channel_id=1, source_target_pairs={{7,6},{0,7},{15,14},{8,15},{23,22},{16,23},{31,30},{24,31},{39,38}... | collective-permute-start | bytes 608264 | tf_op jit(solution)/shard_map/ppermute | solution.py:244
  290.4 18.8 %all-to-all-start.2 = ((bf16[32,2,1,1408]{3,1,2,0:T(2,128)(2,1)}), bf16[32,2,1,1408]{3,1,2,0:T(2,128)(2,1)S(1)}, u32[]{:S(2)}, u32[]{:S(2)}) async-start(bf16[32,2,1,1408]{3,1,2,0:T(2,128)(2,1)} %bitcast.51), calls=%async_computation.2 | async-start | bytes 360448 | tf_op jit(solution)/shard_map/all_to_all | solution.py:185
  310.7 119.2 %all-to-all-start.3 = ((bf16[4,32,2,1,1408]{4,0,2,3,1:T(4,128)(2,1)}), bf16[4,32,2,1,1408]{4,0,2,3,1:T(4,128)(2,1)S(1)}, u32[]{:S(2)}, u32[]{:S(2)}) async-start(bf16[4,32,2,1,1408]{4,0,2,3,1:T(4,128)(2,1)} %bitcast.63), calls=%async_computation.3 | async-start | bytes 1441792 | tf_op jit(solution)/shard_map/all_to_all | solution.py:185
  318.2 89.2 %collective-permute-start.39 = (bf16[16,1408]{1,0:T(8,128)(2,1)S(1)}, bf16[16,1408]{1,0:T(8,128)(2,1)S(1)}, u32[]{:S(2)}, u32[]{:S(2)}) collective-permute-start(bf16[16,1408]{1,0:T(8,128)(2,1)S(1)} %get-tuple-element.208), channel_id=1, source_target_pairs={{24,0},{32,8},{40,16},{48,24},{56,32},{64,40},{72,48},{80,56},{88,... | collective-permute-start | bytes 135176 | tf_op jit(solution)/shard_map/ppermute | solution.py:14
  336.0 88.1 %collective-permute-start.38 = (bf16[16,1408]{1,0:T(8,128)(2,1)S(1)}, bf16[16,1408]{1,0:T(8,128)(2,1)S(1)}, u32[]{:S(2)}, u32[]{:S(2)}) collective-permute-start(bf16[16,1408]{1,0:T(8,128)(2,1)S(1)} %get-tuple-element.209), channel_id=1, source_target_pairs={{16,0},{24,8},{32,16},{40,24},{48,32},{56,40},{64,48},{72,56},{80,... | collective-permute-start | bytes 135176 | tf_op jit(solution)/shard_map/ppermute | solution.py:14
  352.7 71.4 %collective-permute-start.37 = (bf16[16,1408]{1,0:T(8,128)(2,1)S(1)}, bf16[16,1408]{1,0:T(8,128)(2,1)S(1)}, u32[]{:S(2)}, u32[]{:S(2)}) collective-permute-start(bf16[16,1408]{1,0:T(8,128)(2,1)S(1)} %get-tuple-element.210), channel_id=1, source_target_pairs={{8,0},{16,8},{24,16},{32,24},{40,32},{48,40},{56,48},{64,56},{72,6... | collective-permute-start | bytes 135176 | tf_op jit(solution)/shard_map/ppermute | solution.py:14
  373.9 54.2 %collective-permute-start.42 = (bf16[16,1408]{1,0:T(8,128)(2,1)S(1)}, bf16[16,1408]{1,0:T(8,128)(2,1)S(1)}, u32[]{:S(2)}, u32[]{:S(2)}) collective-permute-start(bf16[16,1408]{1,0:T(8,128)(2,1)S(1)} %get-tuple-element.204), channel_id=1, source_target_pairs={{0,24},{8,32},{16,40},{24,48},{32,56},{40,64},{48,72},{56,80},{64,... | collective-permute-start | bytes 135176 | tf_op jit(solution)/shard_map/ppermute | solution.py:14
  390.6 37.5 %collective-permute-start.41 = (bf16[16,1408]{1,0:T(8,128)(2,1)S(1)}, bf16[16,1408]{1,0:T(8,128)(2,1)S(1)}, u32[]{:S(2)}, u32[]{:S(2)}) collective-permute-start(bf16[16,1408]{1,0:T(8,128)(2,1)S(1)} %get-tuple-element.205), channel_id=1, source_target_pairs={{0,16},{8,24},{16,32},{24,40},{32,48},{40,56},{48,64},{56,72},{64,... | collective-permute-start | bytes 135176 | tf_op jit(solution)/shard_map/ppermute | solution.py:14
  407.4 21.6 %collective-permute-start.40 = (bf16[16,1408]{1,0:T(8,128)(2,1)S(1)}, bf16[16,1408]{1,0:T(8,128)(2,1)S(1)}, u32[]{:S(2)}, u32[]{:S(2)}) collective-permute-start(bf16[16,1408]{1,0:T(8,128)(2,1)S(1)} %get-tuple-element.206), channel_id=1, source_target_pairs={{0,8},{8,16},{16,24},{24,32},{32,40},{40,48},{48,56},{56,64},{64,7... | collective-permute-start | bytes 135176 | tf_op jit(solution)/shard_map/ppermute | solution.py:14
  (17 other events, 481.3 us)
Sparse Core Ops, SparseCore 0:
  18.9 94.0 all-gather.5
  124.9 82.1 all-gather.7

commit v4 on v3

--- a/solution.py
+++ b/solution.py
@@ -200,7 +200,12 @@
         jnp.concatenate([chains, edge], axis=0),
         jnp.concatenate([edge, chains], axis=0),
     )
-    fresh = [wide if m == 0 else lax.ppermute(wide, "section", [(m, 0)]) for m in range(micro_count)]
+    held, reach = wide[None], 1
+    while reach < micro_count:
+        sent = [(m, m - reach) for m in range(reach, micro_count, 2 * reach)]
+        held = jnp.concatenate([held, lax.ppermute(held, "section", sent)], axis=0)
+        reach *= 2
+    fresh = [held[m] for m in range(micro_count)]
     weight_part, *fresh = lax.optimization_barrier((weight_part, *fresh))
     core = (lax.axis_index("seq") % 2).astype(jnp.int32)
     weights = placed_weights(core[None], weight_part, core_swap(weight_part), channels)
@@ -220,6 +225,7 @@
     for tick in range(ticks):
         owns.append([])
         busy = [i for i in range(sections) if 0 <= tick - i < pairs]
+        senders = last - pairs if tick >= last - 1 else 0
         active = (section_pos >= busy[0]) & (section_pos <= busy[-1])
         flags = jnp.stack([section_pos == 0, low_half, active]).astype(jnp.int32)
         for lane in range(2):
@@ -236,7 +242,7 @@
             owns[-1].append(own)
             if tick < ticks - 1:
                 incoming[lane] = lax.ppermute(
-                    result, "section", [(i, i + 1) for i in busy if i < last]
+                    result, "section", [(i, i + 1) for i in range(senders, last)]
                 )
             done = entered - 2 * last
             if 0 <= done < micro_count - 1:

time: 440 us -> 368 us (0.84)
  starting transfers between devices: 239 us -> 152 us
  waiting for transfers between devices: 94 us -> 108 us
    ppermute x6, starting transfers between devices: 102 us -> 16 us  [from_behind(): return lax.ppermute(shard, axis, pairs)]
    ppermute x27 -> x23, waiting for transfers between devices: 6.84 us -> 38 us  [the longest x3 36.1 us: on_device(): held = jnp.concatenate([held, lax.ppermute(held, 'section', sent)], axis=0)]
    all_gather x1, waiting for transfers between devices: 46.6 us -> 32.1 us  [gathered_columns(): lax.all_gather(rows, 'seq', axis_index_groups=same_core, axis=0, tiled=True)]
    ppermute x1, starting transfers between devices: 13.8 us -> 3.53 us  [on_device(): lax.ppermute(jnp.where(low_half, chains[slab_rows - spare:], chains[:spar...]
    ppermute x27 -> x23, starting transfers between devices: 33.3 us -> 43 us  [the longest x20 39.2 us: on_device(): lax.ppermute(result, 'section', [(i, i + 1) for i in range(senders, last)])]
  transfers between devices with their start and end apart: 49 -> 45, of which waited for: 12 -> 13; matrix products, arithmetic and copies ran while one was open for 8% -> 7% of each run, Pallas kernels for 10% -> 12%
where the time goes in v4:
time: 368 us; the launch traced here: 365 us
  starting transfers between devices  152 us (41%)
  waiting for transfers between devices  108 us (29%)
  Pallas kernels  44.2 us (12%)
  local copies, waits for them, and re-layouts  28.5 us (8%)
  between operations  15.3 us (4%)
  other arithmetic  10.1 us (3%)
  matrix products  7.68 us (2%)
    ppermute x7, starting transfers between devices, on_device(): lax.ppermute(leaving, 'section', [(last, done), (0, done + 1)])  46 us
    pallas_call x22, Pallas kernels, block(): pl.pallas_call(functools.partial(block_kernel, 256), out_shape=(jax.Shape...  39.7 us
    ppermute x20, starting transfers between devices, on_device(): lax.ppermute(result, 'section', [(i, i + 1) for i in range(senders, last)])  39.2 us
    ppermute x3, waiting for transfers between devices, on_device(): held = jnp.concatenate([held, lax.ppermute(held, 'section', sent)], axis=0)  36.1 us
    all_gather x1, waiting for transfers between devices, gathered_columns(): lax.all_gather(rows, 'seq', axis_index_groups=same_core, axis=0, tiled=True)  32.1 us
    all_to_all x3, starting transfers between devices, to_slabs(): rows = lax.all_to_all(blocks, 'seq', at, at + 1, axis_index_groups=halves)  27.8 us
    ppermute x6, starting transfers between devices, from_behind(): return lax.ppermute(shard, axis, pairs)  16 us
    ppermute x2, starting transfers between devices, core_swap(): lax.ppermute(shard, 'seq', [(i, i ^ 1) for i in range(lax.axis_size('seq'...  11.7 us
  transfers between devices with their start and end apart: 45, of which 13 were waited for; matrix products, arithmetic and copies ran while one was open for 7% of the time, Pallas kernels for 12%

profile of v4, /device:TPU:1, one launch (start us, length us, event | category | flops | bytes accessed | tf_op | source)
XLA Modules:
  0.0 365.4 jit_solution(17723175685938767720)
XLA Ops:
  8.3 8.8 %collective-permute-start = (bf16[66,768]{1,0:T(8,128)(2,1)S(1)}, bf16[66,768]{1,0:T(8,128)(2,1)S(1)}, u32[]{:S(2)}, u32[]{:S(2)}) collective-permute-start(bf16[66,768]{1,0:T(8,128)(2,1)S(1)} %get-tuple-element.208), channel_id=1, source_target_pairs={{0,8},{8,0},{16,24},{24,16},{32,40},{40,32},{48,56},{56,48},{64,72... | collective-permute-start | bytes 304136 | tf_op jit(solution)/shard_map/ppermute | solution.py:22
  19.7 3.9 %all-to-all-start = ((bf16[1,2,32,1408]{3,1,0,2:T(2,128)(2,1)}), bf16[1,2,32,1408]{3,1,0,2:T(2,128)(2,1)S(1)}, u32[]{:S(2)}, u32[]{:S(2)}) async-start(bf16[1,2,32,1408]{3,1,0,2:T(2,128)(2,1)} %copy.23), calls=%async_computation | async-start | bytes 360448 | tf_op jit(solution)/shard_map/all_to_all | solution.py:178
  23.6 9.9 %all-to-all-done = bf16[1,2,32,1408]{3,1,0,2:T(2,128)(2,1)S(1)} async-done(((bf16[1,2,32,1408]{3,1,0,2:T(2,128)(2,1)}), bf16[1,2,32,1408]{3,1,0,2:T(2,128)(2,1)S(1)}, u32[]{:S(2)}, u32[]{:S(2)}) %all-to-all-start) | async-done | bytes 180256 | tf_op jit(solution)/shard_map/all_to_all | solution.py:178
  33.6 3.5 collective-permute-start.1
  37.2 2.4 collective-permute-done.1
  41.0 5.6 %collective-permute-done.2 = bf16[1,72,1408]{2,1,0:T(8,128)(2,1)S(1)} collective-permute-done((bf16[1,72,1408]{2,1,0:T(8,128)(2,1)S(1)}, bf16[1,72,1408]{2,1,0:T(8,128)(2,1)S(1)}, u32[]{:S(2)}, u32[]{:S(2)}) %collective-permute-start.2) | collective-permute-done | bytes 202784 | tf_op jit(solution)/shard_map/ppermute | solution.py:206
  47.9 8.7 %collective-permute-done.3 = bf16[2,72,1408]{2,1,0:T(8,128)(2,1)S(1)} collective-permute-done((bf16[2,72,1408]{2,1,0:T(8,128)(2,1)S(1)}, bf16[2,72,1408]{2,1,0:T(8,128)(2,1)S(1)}, u32[]{:S(2)}, u32[]{:S(2)}) %collective-permute-start.3) | collective-permute-done | bytes 405536 | tf_op jit(solution)/shard_map/ppermute | solution.py:206
  59.0 21.9 %collective-permute-done.4 = bf16[4,72,1408]{2,1,0:T(8,128)(2,1)S(1)} collective-permute-done((bf16[4,72,1408]{2,1,0:T(8,128)(2,1)}, bf16[4,72,1408]{2,1,0:T(8,128)(2,1)S(1)}, u32[]{:S(2)}, u32[]{:S(2)}) %collective-permute-start.4) | collective-permute-done | bytes 811040 | tf_op jit(solution)/shard_map/ppermute | solution.py:206
  81.0 32.1 %all-gather.6.cloned.1.call-done = bf16[32,132,768]{2,1,0:T(8,128)(2,1)} async-done(((bf16[1,132,768]{2,1,0:T(8,128)(2,1)}), bf16[32,132,768]{2,1,0:T(8,128)(2,1)}) %all-gather.6.cloned.1.call-update) | async-done | bytes 6488080 | tf_op jit(solution)/shard_map/all_gather | solution.py:41
  113.1 8.3 %reshape.137.mine_ref = bf16[4224,768]{1,0:T(8,128)(2,1)} reshape(bf16[32,132,768]{2,1,0:T(8,128)(2,1)} %all-gather.6.cloned.1.call-done) | data formatting | bytes 12976128 | tf_op jit(solution)/shard_map/optimization_barrier | solution.py:209
  121.4 2.9 collective-permute-start.5
  124.9 9.9 %collective-permute-done.5.other_ref = bf16[4224,768]{1,0:T(8,128)(2,1)} collective-permute-done((bf16[4224,768]{1,0:T(8,128)(2,1)}, bf16[4224,768]{1,0:T(8,128)(2,1)}, u32[]{:S(2)}, u32[]{:S(2)}) %collective-permute-start.5) | collective-permute-done | bytes 6488096 | tf_op jit(solution)/shard_map/ppermute | solution.py:22
  134.8 4.5 %shard_map.104.weights_ref = bf16[4224,1408]{1,0:T(8,128)(2,1)S(1)} custom-call(s32[1]{0:T(128)} %bitcast.3.core_ref, bf16[4224,768]{1,0:T(8,128)(2,1)} %reshape.137.mine_ref, bf16[4224,768]{1,0:T(8,128)(2,1)} %collective-permute-done.5.other_ref), custom_call_target="tpu_custom_call" | custom-call | bytes 23789568 | tf_op jit(solution)/shard_map/pallas_call | solution.py:69
  139.3 3.9 %shard_map.105 = (bf16[72,1408]{1,0:T(8,128)(2,1)S(1)}, bf16[64,1408]{1,0:T(8,128)(2,1)S(1)}) custom-call(s32[3]{0:T(128)S(1)} %get-tuple-element.226.flags_ref, bf16[4224,1408]{1,0:T(8,128)(2,1)S(1)} %shard_map.104.weights_ref, f32[1,1408]{1,0:T(1,128)S(1)} %copy-done.4, bf16[72,1408]{1,0:T(8,128)(2,1)S(1)} %broadcast_in_dim.37.incoming_ref, ...), custom_call_target="tpu_custom_call" | custom-call | flops 856424448 | bytes 811008 | tf_op jit(solution)/shard_map/pallas_call | solution.py:131
  144.6 3.9 %shard_map.106 = (bf16[72,1408]{1,0:T(8,128)(2,1)S(1)}, bf16[64,1408]{1,0:T(8,128)(2,1)S(1)}) custom-call(s32[3]{0:T(128)S(1)} %get-tuple-element.226.flags_ref, bf16[4224,1408]{1,0:T(8,128)(2,1)S(1)} %shard_map.104.weights_ref, f32[1,1408]{1,0:T(1,128)S(1)} %copy-done.4, bf16[72,1408]{1,0:T(8,128)(2,1)S(1)} %broadcast_in_dim.37.incoming_ref, ...), custom_call_target="tpu_custom_call" | custom-call | flops 856424448 | bytes 811008 | tf_op jit(solution)/shard_map/pallas_call | solution.py:131
  149.9 3.9 %shard_map.107 = (bf16[72,1408]{1,0:T(8,128)(2,1)S(1)}, bf16[64,1408]{1,0:T(8,128)(2,1)S(1)}) custom-call(s32[3]{0:T(128)S(1)} %get-tuple-element.219.flags_ref, bf16[4224,1408]{1,0:T(8,128)(2,1)S(1)} %shard_map.104.weights_ref, f32[1,1408]{1,0:T(1,128)S(1)} %copy-done.4, bf16[72,1408]{1,0:T(8,128)(2,1)S(1)} %collective-permute-done.6.incoming_ref, ...), custom_call_target="tpu_custom_call" | custom-call | flops 856424448 | bytes 811008 | tf_op jit(solution)/shard_map/pallas_call | solution.py:131
  153.8 3.3 collective-permute-start.7
  157.1 3.9 %shard_map.108 = (bf16[72,1408]{1,0:T(8,128)(2,1)S(1)}, bf16[64,1408]{1,0:T(8,128)(2,1)S(1)}) custom-call(s32[3]{0:T(128)S(1)} %get-tuple-element.219.flags_ref, bf16[4224,1408]{1,0:T(8,128)(2,1)S(1)} %shard_map.104.weights_ref, f32[1,1408]{1,0:T(1,128)S(1)} %copy-done.4, bf16[72,1408]{1,0:T(8,128)(2,1)S(1)} %collective-permute-done.8.incoming_ref, ...), custom_call_target="tpu_custom_call" | custom-call | flops 856424448 | bytes 811008 | tf_op jit(solution)/shard_map/pallas_call | solution.py:131
  161.1 1.9 collective-permute-start.10
  163.0 3.9 %shard_map.109 = (bf16[72,1408]{1,0:T(8,128)(2,1)S(1)}, bf16[64,1408]{1,0:T(8,128)(2,1)S(1)}) custom-call(s32[3]{0:T(128)S(1)} %get-tuple-element.220.flags_ref, bf16[4224,1408]{1,0:T(8,128)(2,1)S(1)} %shard_map.104.weights_ref, f32[1,1408]{1,0:T(1,128)S(1)} %copy-done.4, bf16[72,1408]{1,0:T(8,128)(2,1)S(1)} %collective-permute-done.7.incoming_ref, ...), custom_call_target="tpu_custom_call" | custom-call | flops 856424448 | bytes 811008 | tf_op jit(solution)/shard_map/pallas_call | solution.py:131
  167.0 1.9 collective-permute-start.9
  168.9 3.9 %shard_map.110 = (bf16[72,1408]{1,0:T(8,128)(2,1)S(1)}, bf16[64,1408]{1,0:T(8,128)(2,1)S(1)}) custom-call(s32[3]{0:T(128)S(1)} %get-tuple-element.220.flags_ref, bf16[4224,1408]{1,0:T(8,128)(2,1)S(1)} %shard_map.104.weights_ref, f32[1,1408]{1,0:T(1,128)S(1)} %copy-done.4, bf16[72,1408]{1,0:T(8,128)(2,1)S(1)} %collective-permute-done.10.incoming_ref, ...), custom_call_target="tpu_custom_call" | custom-call | flops 856424448 | bytes 811008 | tf_op jit(solution)/shard_map/pallas_call | solution.py:131
  172.8 2.2 collective-permute-start.12
  175.1 3.9 %shard_map.111 = (bf16[72,1408]{1,0:T(8,128)(2,1)S(1)}, bf16[64,1408]{1,0:T(8,128)(2,1)S(1)}) custom-call(s32[3]{0:T(128)S(1)} %get-tuple-element.221.flags_ref, bf16[4224,1408]{1,0:T(8,128)(2,1)S(1)} %shard_map.104.weights_ref, f32[1,1408]{1,0:T(1,128)S(1)} %copy-done.4, bf16[72,1408]{1,0:T(8,128)(2,1)S(1)} %collective-permute-done.9.incoming_ref, ...), custom_call_target="tpu_custom_call" | custom-call | flops 856424448 | bytes 811008 | tf_op jit(solution)/shard_map/pallas_call | solution.py:131
  179.1 1.9 collective-permute-start.11
  181.0 3.9 %shard_map.112 = (bf16[72,1408]{1,0:T(8,128)(2,1)S(1)}, bf16[64,1408]{1,0:T(8,128)(2,1)S(1)}) custom-call(s32[3]{0:T(128)S(1)} %get-tuple-element.221.flags_ref, bf16[4224,1408]{1,0:T(8,128)(2,1)S(1)} %shard_map.104.weights_ref, f32[1,1408]{1,0:T(1,128)S(1)} %copy-done.4, bf16[72,1408]{1,0:T(8,128)(2,1)S(1)} %collective-permute-done.12.incoming_ref, ...), custom_call_target="tpu_custom_call" | custom-call | flops 856424448 | bytes 811008 | tf_op jit(solution)/shard_map/pallas_call | solution.py:131
  187.7 5.3 %collective-permute-start.13 = (bf16[72,1408]{1,0:T(8,128)(2,1)S(1)}, bf16[72,1408]{1,0:T(8,128)(2,1)S(1)}, u32[]{:S(2)}, u32[]{:S(2)}) collective-permute-start(bf16[72,1408]{1,0:T(8,128)(2,1)S(1)} %get-tuple-element.118), channel_id=1, source_target_pairs={{0,1},{1,2},{2,3},{3,4},{4,5},{5,6},{6,7},{8,9},{9,10},{10,11},{11... | collective-permute-start | bytes 608264 | tf_op jit(solution)/shard_map/ppermute | solution.py:244
  193.6 5.3 %collective-permute-start.16 = (bf16[72,1408]{1,0:T(8,128)(2,1)S(1)}, bf16[72,1408]{1,0:T(8,128)(2,1)S(1)}, u32[]{:S(2)}, u32[]{:S(2)}) collective-permute-start(bf16[72,1408]{1,0:T(8,128)(2,1)S(1)} %get-tuple-element.120), channel_id=1, source_target_pairs={{0,1},{1,2},{2,3},{3,4},{4,5},{5,6},{6,7},{8,9},{9,10},{10,11},{11... | collective-permute-start | bytes 608264 | tf_op jit(solution)/shard_map/ppermute | solution.py:244
  199.6 1.9 collective-permute-start.15
  202.1 5.2 %collective-permute-start.18 = (bf16[72,1408]{1,0:T(8,128)(2,1)S(1)}, bf16[72,1408]{1,0:T(8,128)(2,1)S(1)}, u32[]{:S(2)}, u32[]{:S(2)}) collective-permute-start(bf16[72,1408]{1,0:T(8,128)(2,1)S(1)} %get-tuple-element.124), channel_id=1, source_target_pairs={{0,1},{1,2},{2,3},{3,4},{4,5},{5,6},{6,7},{8,9},{9,10},{10,11},{11... | collective-permute-start | bytes 608264 | tf_op jit(solution)/shard_map/ppermute | solution.py:244
  214.5 7.1 %collective-permute-start.23 = (bf16[72,1408]{1,0:T(8,128)(2,1)S(1)}, bf16[72,1408]{1,0:T(8,128)(2,1)}, u32[]{:S(2)}, u32[]{:S(2)}) collective-permute-start(bf16[72,1408]{1,0:T(8,128)(2,1)S(1)} %broadcast_select_fusion.5), channel_id=1, source_target_pairs={{7,1},{0,2},{15,9},{8,10},{23,17},{16,18},{31,25},{24,26},{39,33},... | collective-permute-start | bytes 608264 | tf_op jit(solution)/shard_map/ppermute | solution.py:250
  221.6 1.9 collective-permute-start.19
  224.9 7.4 %collective-permute-done.19 = bf16[72,1408]{1,0:T(8,128)(2,1)S(1)} collective-permute-done((bf16[72,1408]{1,0:T(8,128)(2,1)S(1)}, bf16[72,1408]{1,0:T(8,128)(2,1)S(1)}, u32[]{:S(2)}, u32[]{:S(2)}) %collective-permute-start.19) | collective-permute-done | bytes 202784 | tf_op jit(solution)/shard_map/ppermute | solution.py:250
  233.0 9.6 %collective-permute-start.25 = (bf16[72,1408]{1,0:T(8,128)(2,1)}, bf16[72,1408]{1,0:T(8,128)(2,1)}, u32[]{:S(2)}, u32[]{:S(2)}) collective-permute-start(bf16[72,1408]{1,0:T(8,128)(2,1)} %broadcast_select_fusion.4), channel_id=1, source_target_pairs={{7,2},{0,3},{15,10},{8,11},{23,18},{16,19},{31,26},{24,27},{39,34}... | collective-permute-start | bytes 608264 | tf_op jit(solution)/shard_map/ppermute | solution.py:250
  244.6 7.5 %collective-permute-start.27 = (bf16[72,1408]{1,0:T(8,128)(2,1)}, bf16[72,1408]{1,0:T(8,128)(2,1)}, u32[]{:S(2)}, u32[]{:S(2)}) collective-permute-start(bf16[72,1408]{1,0:T(8,128)(2,1)} %broadcast_select_fusion.3), channel_id=1, source_target_pairs={{7,3},{0,4},{15,11},{8,12},{23,19},{16,20},{31,27},{24,28},{39,35}... | collective-permute-start | bytes 608264 | tf_op jit(solution)/shard_map/ppermute | solution.py:250
  255.6 11.8 %all-to-all-start.1 = ((bf16[4,32,2,1,1408]{4,2,0,3,1:T(2,128)(2,1)}), bf16[4,32,2,1,1408]{4,2,0,3,1:T(2,128)(2,1)S(1)}, u32[]{:S(2)}, u32[]{:S(2)}) async-start(bf16[4,32,2,1,1408]{4,2,0,3,1:T(2,128)(2,1)} %copy.24), calls=%async_computation.1 | async-start | bytes 1441792 | tf_op jit(solution)/shard_map/all_to_all | solution.py:185
  267.4 4.4 %copy-done.3 = bf16[4224,1408]{1,0:T(8,128)(2,1)S(1)} copy-done((bf16[4224,1408]{1,0:T(8,128)(2,1)S(1)}, bf16[4224,1408]{1,0:T(8,128)(2,1)}, u32[]{:S(2)}) %copy-start.3) | copy-done | bytes 11894808
  274.7 13.1 %collective-permute-start.29 = (bf16[72,1408]{1,0:T(8,128)(2,1)S(1)}, bf16[72,1408]{1,0:T(8,128)(2,1)S(1)}, u32[]{:S(2)}, u32[]{:S(2)}) collective-permute-start(bf16[72,1408]{1,0:T(8,128)(2,1)S(1)} %broadcast_select_fusion.2), channel_id=1, source_target_pairs={{7,4},{0,5},{15,12},{8,13},{23,20},{16,21},{31,28},{24,29},{39,36}... | collective-permute-start | bytes 608264 | tf_op jit(solution)/shard_map/ppermute | solution.py:250
  289.8 5.5 %collective-permute-start.32 = (bf16[72,1408]{1,0:T(8,128)(2,1)S(1)}, bf16[72,1408]{1,0:T(8,128)(2,1)S(1)}, u32[]{:S(2)}, u32[]{:S(2)}) collective-permute-start(bf16[72,1408]{1,0:T(8,128)(2,1)S(1)} %broadcast_select_fusion), channel_id=1, source_target_pairs={{7,6},{0,7},{15,14},{8,15},{23,22},{16,23},{31,30},{24,31},{39,38}... | collective-permute-start | bytes 608264 | tf_op jit(solution)/shard_map/ppermute | solution.py:250
  296.7 3.5 collective-permute-done.32
  302.7 9.5 %all-to-all-start.2 = ((bf16[32,2,1,1408]{3,1,2,0:T(2,128)(2,1)}), bf16[32,2,1,1408]{3,1,2,0:T(2,128)(2,1)S(1)}, u32[]{:S(2)}, u32[]{:S(2)}) async-start(bf16[32,2,1,1408]{3,1,2,0:T(2,128)(2,1)} %bitcast.59), calls=%async_computation.2 | async-start | bytes 360448 | tf_op jit(solution)/shard_map/all_to_all | solution.py:185
  314.2 6.2 %reshape.116 = bf16[1408,1408]{1,0:T(8,128)(2,1)} reshape(bf16[64,22,1408]{2,1,0:T(8,128)(2,1)} %all-gather.8.cloned.1.call-done) | data formatting | bytes 7929856 | tf_op jit(solution)/shard_map/reshape | solution.py:258
  323.5 6.6 %all-to-all-start.3 = ((bf16[4,32,2,1,1408]{4,0,2,3,1:T(4,128)(2,1)}), bf16[4,32,2,1,1408]{4,0,2,3,1:T(4,128)(2,1)S(1)}, u32[]{:S(2)}, u32[]{:S(2)}) async-start(bf16[4,32,2,1,1408]{4,0,2,3,1:T(4,128)(2,1)} %bitcast.71), calls=%async_computation.3 | async-start | bytes 1441792 | tf_op jit(solution)/shard_map/all_to_all | solution.py:185
  333.6 2.1 collective-permute-start.33
  335.7 2.8 convolution_convert_fusion
  339.4 6.0 %collective-permute-start.38 = (bf16[16,1408]{1,0:T(8,128)(2,1)S(1)}, bf16[16,1408]{1,0:T(8,128)(2,1)S(1)}, u32[]{:S(2)}, u32[]{:S(2)}) collective-permute-start(bf16[16,1408]{1,0:T(8,128)(2,1)S(1)} %get-tuple-element.210), channel_id=1, source_target_pairs={{0,24},{8,32},{16,40},{24,48},{32,56},{40,64},{48,72},{56,80},{64,... | collective-permute-start | bytes 135176 | tf_op jit(solution)/shard_map/ppermute | solution.py:14
  345.4 3.4 collective-permute-start.37
  352.8 3.5 fusion.46
  (168 shorter events, 55.5 us)
Async XLA Ops:
  7.2 105.9 %all-gather.6.cloned.1.call-start = ((), (), s32[]{:S(2)}) async-start(), calls=%async_computation.4 | async-start | bytes 6893568 | tf_op jit(solution)/shard_map/all_gather | solution.py:41
  8.3 9.7 %collective-permute-start = (bf16[66,768]{1,0:T(8,128)(2,1)S(1)}, bf16[66,768]{1,0:T(8,128)(2,1)S(1)}, u32[]{:S(2)}, u32[]{:S(2)}) collective-permute-start(bf16[66,768]{1,0:T(8,128)(2,1)S(1)} %get-tuple-element.208), channel_id=1, source_target_pairs={{0,8},{8,0},{16,24},{24,16},{32,40},{40,32},{48,56},{56,48},{64,72... | collective-permute-start | bytes 304136 | tf_op jit(solution)/shard_map/ppermute | solution.py:22
  19.7 13.8 %all-to-all-start = ((bf16[1,2,32,1408]{3,1,0,2:T(2,128)(2,1)}), bf16[1,2,32,1408]{3,1,0,2:T(2,128)(2,1)S(1)}, u32[]{:S(2)}, u32[]{:S(2)}) async-start(bf16[1,2,32,1408]{3,1,0,2:T(2,128)(2,1)} %copy.23), calls=%async_computation | async-start | bytes 360448 | tf_op jit(solution)/shard_map/all_to_all | solution.py:178
  23.6 278.4 %all-gather.8.cloned.1.call-start = ((), (), s32[]{:S(2)}) async-start(), calls=%async_computation.5 | async-start | bytes 4392960 | tf_op jit(solution)/shard_map/all_gather | solution.py:213
  33.6 6.1 %collective-permute-start.1 = (bf16[8,1408]{1,0:T(8,128)(2,1)S(1)}, bf16[8,1408]{1,0:T(8,128)(2,1)S(1)}, u32[]{:S(2)}, u32[]{:S(2)}) collective-permute-start(bf16[8,1408]{1,0:T(8,128)(2,1)S(1)} %select_n.154), channel_id=1, source_target_pairs={{0,256},{8,264},{16,272},{24,280},{32,288},{40,296},{48,304},{56,3... | collective-permute-start | bytes 67592 | tf_op jit(solution)/shard_map/ppermute | solution.py:193
  39.7 6.9 %collective-permute-start.2 = (bf16[1,72,1408]{2,1,0:T(8,128)(2,1)S(1)}, bf16[1,72,1408]{2,1,0:T(8,128)(2,1)S(1)}, u32[]{:S(2)}, u32[]{:S(2)}) collective-permute-start(bf16[1,72,1408]{2,1,0:T(8,128)(2,1)S(1)} %maximum_select_fusion.2), channel_id=1, source_target_pairs={{1,0},{3,2},{5,4},{7,6},{9,8},{11,10},{13,12},{15,14},{17,16},{19,... | collective-permute-start | bytes 608264 | tf_op jit(solution)/shard_map/ppermute | solution.py:206
  46.6 10.0 %collective-permute-start.3 = (bf16[2,72,1408]{2,1,0:T(8,128)(2,1)S(1)}, bf16[2,72,1408]{2,1,0:T(8,128)(2,1)S(1)}, u32[]{:S(2)}, u32[]{:S(2)}) collective-permute-start(bf16[2,72,1408]{2,1,0:T(8,128)(2,1)S(1)} %pad_maximum_fusion.1), channel_id=1, source_target_pairs={{2,0},{6,4},{10,8},{14,12},{18,16},{22,20},{26,24},{30,28},{34,32}... | collective-permute-start | bytes 1216520 | tf_op jit(solution)/shard_map/ppermute | solution.py:206
  57.6 23.3 %collective-permute-start.4 = (bf16[4,72,1408]{2,1,0:T(8,128)(2,1)}, bf16[4,72,1408]{2,1,0:T(8,128)(2,1)S(1)}, u32[]{:S(2)}, u32[]{:S(2)}) collective-permute-start(bf16[4,72,1408]{2,1,0:T(8,128)(2,1)} %pad_maximum_fusion), channel_id=1, source_target_pairs={{4,0},{12,8},{20,16},{28,24},{36,32},{44,40},{52,48},{60,56},{68,6... | collective-permute-start | bytes 2433032 | tf_op jit(solution)/shard_map/ppermute | solution.py:206
  81.0 43.7 %copy-start.9 = (s32[1,1,64]{2,1,0:T(1,128)S(1)}, s32[1,1,64]{2,1,0:T(1,128)}, u32[]{:S(2)}) copy-start(s32[1,1,64]{2,1,0:T(1,128)} %param.17) | copy-start | bytes 772
  81.0 43.7 %copy-start.12 = (f32[1,1,64]{2,1,0:T(1,128)S(1)}, f32[1,1,64]{2,1,0:T(1,128)}, u32[]{:S(2)}) copy-start(f32[1,1,64]{2,1,0:T(1,128)} %param.19) | copy-start | bytes 772
  121.4 13.3 %collective-permute-start.5 = (bf16[4224,768]{1,0:T(8,128)(2,1)}, bf16[4224,768]{1,0:T(8,128)(2,1)}, u32[]{:S(2)}, u32[]{:S(2)}) collective-permute-start(bf16[4224,768]{1,0:T(8,128)(2,1)} %reshape.137.mine_ref), channel_id=1, source_target_pairs={{0,8},{8,0},{16,24},{24,16},{32,40},{40,32},{48,56},{56,48},{64,72... | collective-permute-start | bytes 19464200 | tf_op jit(solution)/shard_map/ppermute | solution.py:22
  139.3 103.4 %copy-start.2 = (bf16[4224,1408]{1,0:T(8,128)(2,1)}, bf16[4224,1408]{1,0:T(8,128)(2,1)S(1)}, u32[]{:S(2)}) copy-start(bf16[4224,1408]{1,0:T(8,128)(2,1)S(1)} %shard_map.104.weights_ref) | copy-start | bytes 35684356
  143.3 6.6 %collective-permute-start.6 = (bf16[72,1408]{1,0:T(8,128)(2,1)S(1)}, bf16[72,1408]{1,0:T(8,128)(2,1)S(1)}, u32[]{:S(2)}, u32[]{:S(2)}) collective-permute-start(bf16[72,1408]{1,0:T(8,128)(2,1)S(1)} %get-tuple-element.95), channel_id=1, source_target_pairs={{0,1},{1,2},{2,3},{3,4},{4,5},{5,6},{6,7},{8,9},{9,10},{10,11},{11... | collective-permute-start | bytes 608264 | tf_op jit(solution)/shard_map/ppermute | solution.py:244
  148.5 8.6 %collective-permute-start.8 = (bf16[72,1408]{1,0:T(8,128)(2,1)S(1)}, bf16[72,1408]{1,0:T(8,128)(2,1)S(1)}, u32[]{:S(2)}, u32[]{:S(2)}) collective-permute-start(bf16[72,1408]{1,0:T(8,128)(2,1)S(1)} %get-tuple-element.98), channel_id=1, source_target_pairs={{0,1},{1,2},{2,3},{3,4},{4,5},{5,6},{6,7},{8,9},{9,10},{10,11},{11... | collective-permute-start | bytes 608264 | tf_op jit(solution)/shard_map/ppermute | solution.py:244
  153.8 9.2 %collective-permute-start.7 = (bf16[72,1408]{1,0:T(8,128)(2,1)S(1)}, bf16[72,1408]{1,0:T(8,128)(2,1)S(1)}, u32[]{:S(2)}, u32[]{:S(2)}) collective-permute-start(bf16[72,1408]{1,0:T(8,128)(2,1)S(1)} %get-tuple-element.101), channel_id=1, source_target_pairs={{0,1},{1,2},{2,3},{3,4},{4,5},{5,6},{6,7},{8,9},{9,10},{10,11},{11... | collective-permute-start | bytes 608264 | tf_op jit(solution)/shard_map/ppermute | solution.py:244
  161.1 7.8 %collective-permute-start.10 = (bf16[72,1408]{1,0:T(8,128)(2,1)S(1)}, bf16[72,1408]{1,0:T(8,128)(2,1)S(1)}, u32[]{:S(2)}, u32[]{:S(2)}) collective-permute-start(bf16[72,1408]{1,0:T(8,128)(2,1)S(1)} %get-tuple-element.104), channel_id=1, source_target_pairs={{0,1},{1,2},{2,3},{3,4},{4,5},{5,6},{6,7},{8,9},{9,10},{10,11},{11... | collective-permute-start | bytes 608264 | tf_op jit(solution)/shard_map/ppermute | solution.py:244
  167.0 8.2 %collective-permute-start.9 = (bf16[72,1408]{1,0:T(8,128)(2,1)S(1)}, bf16[72,1408]{1,0:T(8,128)(2,1)S(1)}, u32[]{:S(2)}, u32[]{:S(2)}) collective-permute-start(bf16[72,1408]{1,0:T(8,128)(2,1)S(1)} %get-tuple-element.107), channel_id=1, source_target_pairs={{0,1},{1,2},{2,3},{3,4},{4,5},{5,6},{6,7},{8,9},{9,10},{10,11},{11... | collective-permute-start | bytes 608264 | tf_op jit(solution)/shard_map/ppermute | solution.py:244
  172.8 8.2 %collective-permute-start.12 = (bf16[72,1408]{1,0:T(8,128)(2,1)S(1)}, bf16[72,1408]{1,0:T(8,128)(2,1)S(1)}, u32[]{:S(2)}, u32[]{:S(2)}) collective-permute-start(bf16[72,1408]{1,0:T(8,128)(2,1)S(1)} %get-tuple-element.110), channel_id=1, source_target_pairs={{0,1},{1,2},{2,3},{3,4},{4,5},{5,6},{6,7},{8,9},{9,10},{10,11},{11... | collective-permute-start | bytes 608264 | tf_op jit(solution)/shard_map/ppermute | solution.py:244
  179.1 7.9 %collective-permute-start.11 = (bf16[72,1408]{1,0:T(8,128)(2,1)S(1)}, bf16[72,1408]{1,0:T(8,128)(2,1)S(1)}, u32[]{:S(2)}, u32[]{:S(2)}) collective-permute-start(bf16[72,1408]{1,0:T(8,128)(2,1)S(1)} %get-tuple-element.113), channel_id=1, source_target_pairs={{0,1},{1,2},{2,3},{3,4},{4,5},{5,6},{6,7},{8,9},{9,10},{10,11},{11... | collective-permute-start | bytes 608264 | tf_op jit(solution)/shard_map/ppermute | solution.py:244
  184.9 8.1 %collective-permute-start.14 = (bf16[72,1408]{1,0:T(8,128)(2,1)S(1)}, bf16[72,1408]{1,0:T(8,128)(2,1)S(1)}, u32[]{:S(2)}, u32[]{:S(2)}) collective-permute-start(bf16[72,1408]{1,0:T(8,128)(2,1)S(1)} %get-tuple-element.116), channel_id=1, source_target_pairs={{0,1},{1,2},{2,3},{3,4},{4,5},{5,6},{6,7},{8,9},{9,10},{10,11},{11... | collective-permute-start | bytes 608264 | tf_op jit(solution)/shard_map/ppermute | solution.py:244
  187.7 11.2 %collective-permute-start.13 = (bf16[72,1408]{1,0:T(8,128)(2,1)S(1)}, bf16[72,1408]{1,0:T(8,128)(2,1)S(1)}, u32[]{:S(2)}, u32[]{:S(2)}) collective-permute-start(bf16[72,1408]{1,0:T(8,128)(2,1)S(1)} %get-tuple-element.118), channel_id=1, source_target_pairs={{0,1},{1,2},{2,3},{3,4},{4,5},{5,6},{6,7},{8,9},{9,10},{10,11},{11... | collective-permute-start | bytes 608264 | tf_op jit(solution)/shard_map/ppermute | solution.py:244
  193.6 7.9 %collective-permute-start.16 = (bf16[72,1408]{1,0:T(8,128)(2,1)S(1)}, bf16[72,1408]{1,0:T(8,128)(2,1)S(1)}, u32[]{:S(2)}, u32[]{:S(2)}) collective-permute-start(bf16[72,1408]{1,0:T(8,128)(2,1)S(1)} %get-tuple-element.120), channel_id=1, source_target_pairs={{0,1},{1,2},{2,3},{3,4},{4,5},{5,6},{6,7},{8,9},{9,10},{10,11},{11... | collective-permute-start | bytes 608264 | tf_op jit(solution)/shard_map/ppermute | solution.py:244
  199.6 7.9 %collective-permute-start.15 = (bf16[72,1408]{1,0:T(8,128)(2,1)S(1)}, bf16[72,1408]{1,0:T(8,128)(2,1)S(1)}, u32[]{:S(2)}, u32[]{:S(2)}) collective-permute-start(bf16[72,1408]{1,0:T(8,128)(2,1)S(1)} %get-tuple-element.122), channel_id=1, source_target_pairs={{0,1},{1,2},{2,3},{3,4},{4,5},{5,6},{6,7},{8,9},{9,10},{10,11},{11... | collective-permute-start | bytes 608264 | tf_op jit(solution)/shard_map/ppermute | solution.py:244
  202.1 8.4 %collective-permute-start.18 = (bf16[72,1408]{1,0:T(8,128)(2,1)S(1)}, bf16[72,1408]{1,0:T(8,128)(2,1)S(1)}, u32[]{:S(2)}, u32[]{:S(2)}) collective-permute-start(bf16[72,1408]{1,0:T(8,128)(2,1)S(1)} %get-tuple-element.124), channel_id=1, source_target_pairs={{0,1},{1,2},{2,3},{3,4},{4,5},{5,6},{6,7},{8,9},{9,10},{10,11},{11... | collective-permute-start | bytes 608264 | tf_op jit(solution)/shard_map/ppermute | solution.py:244
  208.1 3.8 %collective-permute-start.17 = (bf16[72,1408]{1,0:T(8,128)(2,1)S(1)}, bf16[72,1408]{1,0:T(8,128)(2,1)S(1)}, u32[]{:S(2)}, u32[]{:S(2)}) collective-permute-start(bf16[72,1408]{1,0:T(8,128)(2,1)S(1)} %get-tuple-element.126), channel_id=1, source_target_pairs={{3,4},{4,5},{5,6},{6,7},{11,12},{12,13},{13,14},{14,15},{19,20},{2... | collective-permute-start | bytes 608264 | tf_op jit(solution)/shard_map/ppermute | solution.py:244
  211.1 2.1 collective-permute-start.20
  212.5 11.1 %collective-permute-start.22 = (bf16[72,1408]{1,0:T(8,128)(2,1)S(1)}, bf16[72,1408]{1,0:T(8,128)(2,1)S(1)}, u32[]{:S(2)}, u32[]{:S(2)}) collective-permute-start(bf16[72,1408]{1,0:T(8,128)(2,1)S(1)} %get-tuple-element.130), channel_id=1, source_target_pairs={{3,4},{4,5},{5,6},{6,7},{11,12},{12,13},{13,14},{14,15},{19,20},{2... | collective-permute-start | bytes 608264 | tf_op jit(solution)/shard_map/ppermute | solution.py:244
  213.8 11.1 %collective-permute-start.21 = (bf16[72,1408]{1,0:T(8,128)(2,1)S(1)}, bf16[72,1408]{1,0:T(8,128)(2,1)S(1)}, u32[]{:S(2)}, u32[]{:S(2)}) collective-permute-start(bf16[72,1408]{1,0:T(8,128)(2,1)S(1)} %get-tuple-element.132), channel_id=1, source_target_pairs={{3,4},{4,5},{5,6},{6,7},{11,12},{12,13},{13,14},{14,15},{19,20},{2... | collective-permute-start | bytes 608264 | tf_op jit(solution)/shard_map/ppermute | solution.py:244
  214.5 52.9 %collective-permute-start.23 = (bf16[72,1408]{1,0:T(8,128)(2,1)S(1)}, bf16[72,1408]{1,0:T(8,128)(2,1)}, u32[]{:S(2)}, u32[]{:S(2)}) collective-permute-start(bf16[72,1408]{1,0:T(8,128)(2,1)S(1)} %broadcast_select_fusion.5), channel_id=1, source_target_pairs={{7,1},{0,2},{15,9},{8,10},{23,17},{16,18},{31,25},{24,26},{39,33},... | collective-permute-start | bytes 608264 | tf_op jit(solution)/shard_map/ppermute | solution.py:250
  221.6 10.7 %collective-permute-start.19 = (bf16[72,1408]{1,0:T(8,128)(2,1)S(1)}, bf16[72,1408]{1,0:T(8,128)(2,1)S(1)}, u32[]{:S(2)}, u32[]{:S(2)}) collective-permute-start(bf16[72,1408]{1,0:T(8,128)(2,1)S(1)} %broadcast_select_fusion.6), channel_id=1, source_target_pairs={{7,0},{0,1},{15,8},{8,9},{23,16},{16,17},{31,24},{24,25},{39,32},{... | collective-permute-start | bytes 608264 | tf_op jit(solution)/shard_map/ppermute | solution.py:250
  224.2 43.2 %collective-permute-start.24 = (bf16[72,1408]{1,0:T(8,128)(2,1)S(1)}, bf16[72,1408]{1,0:T(8,128)(2,1)S(1)}, u32[]{:S(2)}, u32[]{:S(2)}) collective-permute-start(bf16[72,1408]{1,0:T(8,128)(2,1)S(1)} %get-tuple-element.134), channel_id=1, source_target_pairs={{3,4},{4,5},{5,6},{6,7},{11,12},{12,13},{13,14},{14,15},{19,20},{2... | collective-permute-start | bytes 608264 | tf_op jit(solution)/shard_map/ppermute | solution.py:244
  233.0 40.2 %collective-permute-start.25 = (bf16[72,1408]{1,0:T(8,128)(2,1)}, bf16[72,1408]{1,0:T(8,128)(2,1)}, u32[]{:S(2)}, u32[]{:S(2)}) collective-permute-start(bf16[72,1408]{1,0:T(8,128)(2,1)} %broadcast_select_fusion.4), channel_id=1, source_target_pairs={{7,2},{0,3},{15,10},{8,11},{23,18},{16,19},{31,26},{24,27},{39,34}... | collective-permute-start | bytes 608264 | tf_op jit(solution)/shard_map/ppermute | solution.py:250
  243.2 30.0 %collective-permute-start.26 = (bf16[72,1408]{1,0:T(8,128)(2,1)S(1)}, bf16[72,1408]{1,0:T(8,128)(2,1)S(1)}, u32[]{:S(2)}, u32[]{:S(2)}) collective-permute-start(bf16[72,1408]{1,0:T(8,128)(2,1)S(1)} %get-tuple-element.138), channel_id=1, source_target_pairs={{3,4},{4,5},{5,6},{6,7},{11,12},{12,13},{13,14},{14,15},{19,20},{2... | collective-permute-start | bytes 608264 | tf_op jit(solution)/shard_map/ppermute | solution.py:244
  244.6 44.5 %collective-permute-start.27 = (bf16[72,1408]{1,0:T(8,128)(2,1)}, bf16[72,1408]{1,0:T(8,128)(2,1)}, u32[]{:S(2)}, u32[]{:S(2)}) collective-permute-start(bf16[72,1408]{1,0:T(8,128)(2,1)} %broadcast_select_fusion.3), channel_id=1, source_target_pairs={{7,3},{0,4},{15,11},{8,12},{23,19},{16,20},{31,27},{24,28},{39,35}... | collective-permute-start | bytes 608264 | tf_op jit(solution)/shard_map/ppermute | solution.py:250
  255.6 46.3 %all-to-all-start.1 = ((bf16[4,32,2,1,1408]{4,2,0,3,1:T(2,128)(2,1)}), bf16[4,32,2,1,1408]{4,2,0,3,1:T(2,128)(2,1)S(1)}, u32[]{:S(2)}, u32[]{:S(2)}) async-start(bf16[4,32,2,1,1408]{4,2,0,3,1:T(2,128)(2,1)} %copy.24), calls=%async_computation.1 | async-start | bytes 1441792 | tf_op jit(solution)/shard_map/all_to_all | solution.py:185
  272.4 16.7 %collective-permute-start.28 = (bf16[72,1408]{1,0:T(8,128)(2,1)S(1)}, bf16[72,1408]{1,0:T(8,128)(2,1)S(1)}, u32[]{:S(2)}, u32[]{:S(2)}) collective-permute-start(bf16[72,1408]{1,0:T(8,128)(2,1)S(1)} %get-tuple-element.142), channel_id=1, source_target_pairs={{3,4},{4,5},{5,6},{6,7},{11,12},{12,13},{13,14},{14,15},{19,20},{2... | collective-permute-start | bytes 608264 | tf_op jit(solution)/shard_map/ppermute | solution.py:244
  273.8 22.3 %collective-permute-start.30 = (bf16[72,1408]{1,0:T(8,128)(2,1)S(1)}, bf16[72,1408]{1,0:T(8,128)(2,1)S(1)}, u32[]{:S(2)}, u32[]{:S(2)}) collective-permute-start(bf16[72,1408]{1,0:T(8,128)(2,1)S(1)} %get-tuple-element.146), channel_id=1, source_target_pairs={{3,4},{4,5},{5,6},{6,7},{11,12},{12,13},{13,14},{14,15},{19,20},{2... | collective-permute-start | bytes 608264 | tf_op jit(solution)/shard_map/ppermute | solution.py:244
  274.7 21.4 %collective-permute-start.29 = (bf16[72,1408]{1,0:T(8,128)(2,1)S(1)}, bf16[72,1408]{1,0:T(8,128)(2,1)S(1)}, u32[]{:S(2)}, u32[]{:S(2)}) collective-permute-start(bf16[72,1408]{1,0:T(8,128)(2,1)S(1)} %broadcast_select_fusion.2), channel_id=1, source_target_pairs={{7,4},{0,5},{15,12},{8,13},{23,20},{16,21},{31,28},{24,29},{39,36}... | collective-permute-start | bytes 608264 | tf_op jit(solution)/shard_map/ppermute | solution.py:250
  287.8 8.9 %collective-permute-start.31 = (bf16[72,1408]{1,0:T(8,128)(2,1)S(1)}, bf16[72,1408]{1,0:T(8,128)(2,1)S(1)}, u32[]{:S(2)}, u32[]{:S(2)}) collective-permute-start(bf16[72,1408]{1,0:T(8,128)(2,1)S(1)} %broadcast_select_fusion.1), channel_id=1, source_target_pairs={{7,5},{0,6},{15,13},{8,14},{23,21},{16,22},{31,29},{24,30},{39,37}... | collective-permute-start | bytes 608264 | tf_op jit(solution)/shard_map/ppermute | solution.py:250
  289.8 10.4 %collective-permute-start.32 = (bf16[72,1408]{1,0:T(8,128)(2,1)S(1)}, bf16[72,1408]{1,0:T(8,128)(2,1)S(1)}, u32[]{:S(2)}, u32[]{:S(2)}) collective-permute-start(bf16[72,1408]{1,0:T(8,128)(2,1)S(1)} %broadcast_select_fusion), channel_id=1, source_target_pairs={{7,6},{0,7},{15,14},{8,15},{23,22},{16,23},{31,30},{24,31},{39,38}... | collective-permute-start | bytes 608264 | tf_op jit(solution)/shard_map/ppermute | solution.py:250
  302.7 19.3 %all-to-all-start.2 = ((bf16[32,2,1,1408]{3,1,2,0:T(2,128)(2,1)}), bf16[32,2,1,1408]{3,1,2,0:T(2,128)(2,1)S(1)}, u32[]{:S(2)}, u32[]{:S(2)}) async-start(bf16[32,2,1,1408]{3,1,2,0:T(2,128)(2,1)} %bitcast.59), calls=%async_computation.2 | async-start | bytes 360448 | tf_op jit(solution)/shard_map/all_to_all | solution.py:185
  323.5 33.8 %all-to-all-start.3 = ((bf16[4,32,2,1,1408]{4,0,2,3,1:T(4,128)(2,1)}), bf16[4,32,2,1,1408]{4,0,2,3,1:T(4,128)(2,1)S(1)}, u32[]{:S(2)}, u32[]{:S(2)}) async-start(bf16[4,32,2,1,1408]{4,0,2,3,1:T(4,128)(2,1)} %bitcast.71), calls=%async_computation.3 | async-start | bytes 1441792 | tf_op jit(solution)/shard_map/all_to_all | solution.py:185
  331.0 19.5 %collective-permute-start.35 = (bf16[16,1408]{1,0:T(8,128)(2,1)S(1)}, bf16[16,1408]{1,0:T(8,128)(2,1)S(1)}, u32[]{:S(2)}, u32[]{:S(2)}) collective-permute-start(bf16[16,1408]{1,0:T(8,128)(2,1)S(1)} %get-tuple-element.214), channel_id=1, source_target_pairs={{24,0},{32,8},{40,16},{48,24},{56,32},{64,40},{72,48},{80,56},{88,... | collective-permute-start | bytes 135176 | tf_op jit(solution)/shard_map/ppermute | solution.py:14
  332.3 20.1 %collective-permute-start.34 = (bf16[16,1408]{1,0:T(8,128)(2,1)S(1)}, bf16[16,1408]{1,0:T(8,128)(2,1)S(1)}, u32[]{:S(2)}, u32[]{:S(2)}) collective-permute-start(bf16[16,1408]{1,0:T(8,128)(2,1)S(1)} %get-tuple-element.215), channel_id=1, source_target_pairs={{16,0},{24,8},{32,16},{40,24},{48,32},{56,40},{64,48},{72,56},{80,... | collective-permute-start | bytes 135176 | tf_op jit(solution)/shard_map/ppermute | solution.py:14
  333.6 18.8 %collective-permute-start.33 = (bf16[16,1408]{1,0:T(8,128)(2,1)S(1)}, bf16[16,1408]{1,0:T(8,128)(2,1)S(1)}, u32[]{:S(2)}, u32[]{:S(2)}) collective-permute-start(bf16[16,1408]{1,0:T(8,128)(2,1)S(1)} %get-tuple-element.216), channel_id=1, source_target_pairs={{8,0},{16,8},{24,16},{32,24},{40,32},{48,40},{56,48},{64,56},{72,6... | collective-permute-start | bytes 135176 | tf_op jit(solution)/shard_map/ppermute | solution.py:14
  339.4 16.9 %collective-permute-start.38 = (bf16[16,1408]{1,0:T(8,128)(2,1)S(1)}, bf16[16,1408]{1,0:T(8,128)(2,1)S(1)}, u32[]{:S(2)}, u32[]{:S(2)}) collective-permute-start(bf16[16,1408]{1,0:T(8,128)(2,1)S(1)} %get-tuple-element.210), channel_id=1, source_target_pairs={{0,24},{8,32},{16,40},{24,48},{32,56},{40,64},{48,72},{56,80},{64,... | collective-permute-start | bytes 135176 | tf_op jit(solution)/shard_map/ppermute | solution.py:14
  345.4 10.9 %collective-permute-start.37 = (bf16[16,1408]{1,0:T(8,128)(2,1)S(1)}, bf16[16,1408]{1,0:T(8,128)(2,1)S(1)}, u32[]{:S(2)}, u32[]{:S(2)}) collective-permute-start(bf16[16,1408]{1,0:T(8,128)(2,1)S(1)} %get-tuple-element.211), channel_id=1, source_target_pairs={{0,16},{8,24},{16,32},{24,40},{32,48},{40,56},{48,64},{56,72},{64,... | collective-permute-start | bytes 135176 | tf_op jit(solution)/shard_map/ppermute | solution.py:14
  350.4 5.9 %collective-permute-start.36 = (bf16[16,1408]{1,0:T(8,128)(2,1)S(1)}, bf16[16,1408]{1,0:T(8,128)(2,1)S(1)}, u32[]{:S(2)}, u32[]{:S(2)}) collective-permute-start(bf16[16,1408]{1,0:T(8,128)(2,1)S(1)} %get-tuple-element.212), channel_id=1, source_target_pairs={{0,8},{8,16},{16,24},{24,32},{32,40},{40,48},{48,56},{56,64},{64,7... | collective-permute-start | bytes 135176 | tf_op jit(solution)/shard_map/ppermute | solution.py:14
  (13 other events, 177.1 us)
Sparse Core Ops, SparseCore 0:
  18.9 94.1 all-gather.5
  125.0 82.0 all-gather.7

commit v5 on v4

--- a/solution.py
+++ b/solution.py
@@ -233,7 +233,7 @@
             before = incoming[lane]
             if results:
                 before, _ = lax.optimization_barrier((before, results[-1]))
-            if len(landing) > 2:
+            if len(landing) > 4:
                 arrived, before = lax.optimization_barrier((landing.pop(0), before))
                 landed.append(arrived)
             now = fresh[entered] if entered < micro_count else before

time: 368 us -> 369 us (level)
  waiting for transfers between devices: 108 us -> 98.2 us
  starting transfers between devices: 152 us -> 159 us
    ppermute x7, waiting for transfers between devices: 10.9 us -> 1.58 us  [on_device(): lax.ppermute(leaving, 'section', [(last, done), (0, done + 1)])]
    ppermute x7, starting transfers between devices: 46 us -> 52.8 us  [on_device(): lax.ppermute(leaving, 'section', [(last, done), (0, done + 1)])]
  transfers between devices with their start and end apart: 45 -> 45, of which waited for: 13 -> 12; matrix products, arithmetic and copies ran while one was open for 7% -> 8% of each run, Pallas kernels for 12% -> 12%
where the time goes in v5:
time: 369 us; the launch traced here: 364 us
  starting transfers between devices  159 us (43%)
  waiting for transfers between devices  98.2 us (27%)
  Pallas kernels  44.2 us (12%)
  local copies, waits for them, and re-layouts  27.9 us (8%)
  between operations  15.3 us (4%)
  other arithmetic  11.5 us (3%)
  matrix products  7.67 us (2%)
    ppermute x7, starting transfers between devices, on_device(): lax.ppermute(leaving, 'section', [(last, done), (0, done + 1)])  52.8 us
    pallas_call x22, Pallas kernels, block(): pl.pallas_call(functools.partial(block_kernel, 256), out_shape=(jax.Shape...  39.7 us
    ppermute x20, starting transfers between devices, on_device(): lax.ppermute(result, 'section', [(i, i + 1) for i in range(senders, last)])  39.4 us
    ppermute x3, waiting for transfers between devices, on_device(): held = jnp.concatenate([held, lax.ppermute(held, 'section', sent)], axis=0)  36.1 us
    all_gather x1, waiting for transfers between devices, gathered_columns(): lax.all_gather(rows, 'seq', axis_index_groups=same_core, axis=0, tiled=True)  32.1 us
    all_to_all x3, starting transfers between devices, to_slabs(): rows = lax.all_to_all(blocks, 'seq', at, at + 1, axis_index_groups=halves)  27.6 us
    ppermute x6, starting transfers between devices, from_behind(): return lax.ppermute(shard, axis, pairs)  16 us
    ppermute x2, starting transfers between devices, core_swap(): lax.ppermute(shard, 'seq', [(i, i ^ 1) for i in range(lax.axis_size('seq'...  11.7 us
  transfers between devices with their start and end apart: 45, of which 12 were waited for; matrix products, arithmetic and copies ran while one was open for 8% of the time, Pallas kernels for 12%

profile of v5, /device:TPU:1, one launch (start us, length us, event | category | flops | bytes accessed | tf_op | source)
XLA Modules:
  0.0 363.5 jit_solution(10041430883027213249)
XLA Ops:
  8.3 8.8 %collective-permute-start = (bf16[66,768]{1,0:T(8,128)(2,1)S(1)}, bf16[66,768]{1,0:T(8,128)(2,1)S(1)}, u32[]{:S(2)}, u32[]{:S(2)}) collective-permute-start(bf16[66,768]{1,0:T(8,128)(2,1)S(1)} %get-tuple-element.200), channel_id=1, source_target_pairs={{0,8},{8,0},{16,24},{24,16},{32,40},{40,32},{48,56},{56,48},{64,72... | collective-permute-start | bytes 304136 | tf_op jit(solution)/shard_map/ppermute | solution.py:22
  19.7 3.9 %all-to-all-start = ((bf16[1,2,32,1408]{3,1,0,2:T(2,128)(2,1)}), bf16[1,2,32,1408]{3,1,0,2:T(2,128)(2,1)S(1)}, u32[]{:S(2)}, u32[]{:S(2)}) async-start(bf16[1,2,32,1408]{3,1,0,2:T(2,128)(2,1)} %copy.23), calls=%async_computation | async-start | bytes 360448 | tf_op jit(solution)/shard_map/all_to_all | solution.py:178
  23.6 9.9 %all-to-all-done = bf16[1,2,32,1408]{3,1,0,2:T(2,128)(2,1)S(1)} async-done(((bf16[1,2,32,1408]{3,1,0,2:T(2,128)(2,1)}), bf16[1,2,32,1408]{3,1,0,2:T(2,128)(2,1)S(1)}, u32[]{:S(2)}, u32[]{:S(2)}) %all-to-all-start) | async-done | bytes 180256 | tf_op jit(solution)/shard_map/all_to_all | solution.py:178
  33.6 3.5 collective-permute-start.1
  37.2 2.4 collective-permute-done.1
  41.0 5.6 %collective-permute-done.2 = bf16[1,72,1408]{2,1,0:T(8,128)(2,1)S(1)} collective-permute-done((bf16[1,72,1408]{2,1,0:T(8,128)(2,1)S(1)}, bf16[1,72,1408]{2,1,0:T(8,128)(2,1)S(1)}, u32[]{:S(2)}, u32[]{:S(2)}) %collective-permute-start.2) | collective-permute-done | bytes 202784 | tf_op jit(solution)/shard_map/ppermute | solution.py:206
  47.9 8.7 %collective-permute-done.3 = bf16[2,72,1408]{2,1,0:T(8,128)(2,1)S(1)} collective-permute-done((bf16[2,72,1408]{2,1,0:T(8,128)(2,1)S(1)}, bf16[2,72,1408]{2,1,0:T(8,128)(2,1)S(1)}, u32[]{:S(2)}, u32[]{:S(2)}) %collective-permute-start.3) | collective-permute-done | bytes 405536 | tf_op jit(solution)/shard_map/ppermute | solution.py:206
  59.0 21.9 %collective-permute-done.4 = bf16[4,72,1408]{2,1,0:T(8,128)(2,1)S(1)} collective-permute-done((bf16[4,72,1408]{2,1,0:T(8,128)(2,1)}, bf16[4,72,1408]{2,1,0:T(8,128)(2,1)S(1)}, u32[]{:S(2)}, u32[]{:S(2)}) %collective-permute-start.4) | collective-permute-done | bytes 811040 | tf_op jit(solution)/shard_map/ppermute | solution.py:206
  81.0 32.1 %all-gather.6.cloned.1.call-done = bf16[32,132,768]{2,1,0:T(8,128)(2,1)} async-done(((bf16[1,132,768]{2,1,0:T(8,128)(2,1)}), bf16[32,132,768]{2,1,0:T(8,128)(2,1)}) %all-gather.6.cloned.1.call-update) | async-done | bytes 6488080 | tf_op jit(solution)/shard_map/all_gather | solution.py:41
  113.1 8.3 %reshape.137.mine_ref = bf16[4224,768]{1,0:T(8,128)(2,1)} reshape(bf16[32,132,768]{2,1,0:T(8,128)(2,1)} %all-gather.6.cloned.1.call-done) | data formatting | bytes 12976128 | tf_op jit(solution)/shard_map/optimization_barrier | solution.py:209
  121.4 2.9 collective-permute-start.5
  124.8 9.9 %collective-permute-done.5.other_ref = bf16[4224,768]{1,0:T(8,128)(2,1)} collective-permute-done((bf16[4224,768]{1,0:T(8,128)(2,1)}, bf16[4224,768]{1,0:T(8,128)(2,1)}, u32[]{:S(2)}, u32[]{:S(2)}) %collective-permute-start.5) | collective-permute-done | bytes 6488096 | tf_op jit(solution)/shard_map/ppermute | solution.py:22
  134.7 4.5 %shard_map.104.weights_ref = bf16[4224,1408]{1,0:T(8,128)(2,1)S(1)} custom-call(s32[1]{0:T(128)} %bitcast.3.core_ref, bf16[4224,768]{1,0:T(8,128)(2,1)} %reshape.137.mine_ref, bf16[4224,768]{1,0:T(8,128)(2,1)} %collective-permute-done.5.other_ref), custom_call_target="tpu_custom_call" | custom-call | bytes 23789568 | tf_op jit(solution)/shard_map/pallas_call | solution.py:69
  139.3 3.9 %shard_map.105 = (bf16[72,1408]{1,0:T(8,128)(2,1)S(1)}, bf16[64,1408]{1,0:T(8,128)(2,1)S(1)}) custom-call(s32[3]{0:T(128)S(1)} %get-tuple-element.218.flags_ref, bf16[4224,1408]{1,0:T(8,128)(2,1)S(1)} %shard_map.104.weights_ref, f32[1,1408]{1,0:T(1,128)S(1)} %copy-done.4, bf16[72,1408]{1,0:T(8,128)(2,1)S(1)} %broadcast_in_dim.37.incoming_ref, ...), custom_call_target="tpu_custom_call" | custom-call | flops 856424448 | bytes 811008 | tf_op jit(solution)/shard_map/pallas_call | solution.py:131
  144.5 3.9 %shard_map.106 = (bf16[72,1408]{1,0:T(8,128)(2,1)S(1)}, bf16[64,1408]{1,0:T(8,128)(2,1)S(1)}) custom-call(s32[3]{0:T(128)S(1)} %get-tuple-element.218.flags_ref, bf16[4224,1408]{1,0:T(8,128)(2,1)S(1)} %shard_map.104.weights_ref, f32[1,1408]{1,0:T(1,128)S(1)} %copy-done.4, bf16[72,1408]{1,0:T(8,128)(2,1)S(1)} %broadcast_in_dim.37.incoming_ref, ...), custom_call_target="tpu_custom_call" | custom-call | flops 856424448 | bytes 811008 | tf_op jit(solution)/shard_map/pallas_call | solution.py:131
  149.8 3.9 %shard_map.107 = (bf16[72,1408]{1,0:T(8,128)(2,1)S(1)}, bf16[64,1408]{1,0:T(8,128)(2,1)S(1)}) custom-call(s32[3]{0:T(128)S(1)} %get-tuple-element.211.flags_ref, bf16[4224,1408]{1,0:T(8,128)(2,1)S(1)} %shard_map.104.weights_ref, f32[1,1408]{1,0:T(1,128)S(1)} %copy-done.4, bf16[72,1408]{1,0:T(8,128)(2,1)S(1)} %collective-permute-done.6.incoming_ref, ...), custom_call_target="tpu_custom_call" | custom-call | flops 856424448 | bytes 811008 | tf_op jit(solution)/shard_map/pallas_call | solution.py:131
  153.8 3.3 collective-permute-start.7
  157.1 3.9 %shard_map.108 = (bf16[72,1408]{1,0:T(8,128)(2,1)S(1)}, bf16[64,1408]{1,0:T(8,128)(2,1)S(1)}) custom-call(s32[3]{0:T(128)S(1)} %get-tuple-element.211.flags_ref, bf16[4224,1408]{1,0:T(8,128)(2,1)S(1)} %shard_map.104.weights_ref, f32[1,1408]{1,0:T(1,128)S(1)} %copy-done.4, bf16[72,1408]{1,0:T(8,128)(2,1)S(1)} %collective-permute-done.8.incoming_ref, ...), custom_call_target="tpu_custom_call" | custom-call | flops 856424448 | bytes 811008 | tf_op jit(solution)/shard_map/pallas_call | solution.py:131
  161.0 1.9 collective-permute-start.10
  163.0 3.9 %shard_map.109 = (bf16[72,1408]{1,0:T(8,128)(2,1)S(1)}, bf16[64,1408]{1,0:T(8,128)(2,1)S(1)}) custom-call(s32[3]{0:T(128)S(1)} %get-tuple-element.212.flags_ref, bf16[4224,1408]{1,0:T(8,128)(2,1)S(1)} %shard_map.104.weights_ref, f32[1,1408]{1,0:T(1,128)S(1)} %copy-done.4, bf16[72,1408]{1,0:T(8,128)(2,1)S(1)} %collective-permute-done.7.incoming_ref, ...), custom_call_target="tpu_custom_call" | custom-call | flops 856424448 | bytes 811008 | tf_op jit(solution)/shard_map/pallas_call | solution.py:131
  167.0 1.9 collective-permute-start.9
  168.9 3.9 %shard_map.110 = (bf16[72,1408]{1,0:T(8,128)(2,1)S(1)}, bf16[64,1408]{1,0:T(8,128)(2,1)S(1)}) custom-call(s32[3]{0:T(128)S(1)} %get-tuple-element.212.flags_ref, bf16[4224,1408]{1,0:T(8,128)(2,1)S(1)} %shard_map.104.weights_ref, f32[1,1408]{1,0:T(1,128)S(1)} %copy-done.4, bf16[72,1408]{1,0:T(8,128)(2,1)S(1)} %collective-permute-done.10.incoming_ref, ...), custom_call_target="tpu_custom_call" | custom-call | flops 856424448 | bytes 811008 | tf_op jit(solution)/shard_map/pallas_call | solution.py:131
  172.8 2.2 collective-permute-start.12
  175.1 3.9 %shard_map.111 = (bf16[72,1408]{1,0:T(8,128)(2,1)S(1)}, bf16[64,1408]{1,0:T(8,128)(2,1)S(1)}) custom-call(s32[3]{0:T(128)S(1)} %get-tuple-element.213.flags_ref, bf16[4224,1408]{1,0:T(8,128)(2,1)S(1)} %shard_map.104.weights_ref, f32[1,1408]{1,0:T(1,128)S(1)} %copy-done.4, bf16[72,1408]{1,0:T(8,128)(2,1)S(1)} %collective-permute-done.9.incoming_ref, ...), custom_call_target="tpu_custom_call" | custom-call | flops 856424448 | bytes 811008 | tf_op jit(solution)/shard_map/pallas_call | solution.py:131
  179.1 1.9 collective-permute-start.11
  181.0 3.9 %shard_map.112 = (bf16[72,1408]{1,0:T(8,128)(2,1)S(1)}, bf16[64,1408]{1,0:T(8,128)(2,1)S(1)}) custom-call(s32[3]{0:T(128)S(1)} %get-tuple-element.213.flags_ref, bf16[4224,1408]{1,0:T(8,128)(2,1)S(1)} %shard_map.104.weights_ref, f32[1,1408]{1,0:T(1,128)S(1)} %copy-done.4, bf16[72,1408]{1,0:T(8,128)(2,1)S(1)} %collective-permute-done.12.incoming_ref, ...), custom_call_target="tpu_custom_call" | custom-call | flops 856424448 | bytes 811008 | tf_op jit(solution)/shard_map/pallas_call | solution.py:131
  184.9 1.9 collective-permute-start.14
  187.7 5.3 %collective-permute-start.13 = (bf16[72,1408]{1,0:T(8,128)(2,1)S(1)}, bf16[72,1408]{1,0:T(8,128)(2,1)S(1)}, u32[]{:S(2)}, u32[]{:S(2)}) collective-permute-start(bf16[72,1408]{1,0:T(8,128)(2,1)S(1)} %get-tuple-element.114), channel_id=1, source_target_pairs={{0,1},{1,2},{2,3},{3,4},{4,5},{5,6},{6,7},{8,9},{9,10},{10,11},{11... | collective-permute-start | bytes 608264 | tf_op jit(solution)/shard_map/ppermute | solution.py:244
  193.6 5.3 %collective-permute-start.16 = (bf16[72,1408]{1,0:T(8,128)(2,1)S(1)}, bf16[72,1408]{1,0:T(8,128)(2,1)S(1)}, u32[]{:S(2)}, u32[]{:S(2)}) collective-permute-start(bf16[72,1408]{1,0:T(8,128)(2,1)S(1)} %get-tuple-element.116), channel_id=1, source_target_pairs={{0,1},{1,2},{2,3},{3,4},{4,5},{5,6},{6,7},{8,9},{9,10},{10,11},{11... | collective-permute-start | bytes 608264 | tf_op jit(solution)/shard_map/ppermute | solution.py:244
  199.6 1.9 collective-permute-start.15
  202.1 5.2 %collective-permute-start.18 = (bf16[72,1408]{1,0:T(8,128)(2,1)S(1)}, bf16[72,1408]{1,0:T(8,128)(2,1)S(1)}, u32[]{:S(2)}, u32[]{:S(2)}) collective-permute-start(bf16[72,1408]{1,0:T(8,128)(2,1)S(1)} %get-tuple-element.120), channel_id=1, source_target_pairs={{0,1},{1,2},{2,3},{3,4},{4,5},{5,6},{6,7},{8,9},{9,10},{10,11},{11... | collective-permute-start | bytes 608264 | tf_op jit(solution)/shard_map/ppermute | solution.py:244
  213.9 4.7 %collective-permute-start.19 = (bf16[72,1408]{1,0:T(8,128)(2,1)}, bf16[72,1408]{1,0:T(8,128)(2,1)}, u32[]{:S(2)}, u32[]{:S(2)}) collective-permute-start(bf16[72,1408]{1,0:T(8,128)(2,1)} %broadcast_select_fusion.6), channel_id=1, source_target_pairs={{7,0},{0,1},{15,8},{8,9},{23,16},{16,17},{31,24},{24,25},{39,32},{... | collective-permute-start | bytes 608264 | tf_op jit(solution)/shard_map/ppermute | solution.py:250
  220.6 3.6 collective-permute-start.25
  226.3 18.3 %collective-permute-start.27 = (bf16[72,1408]{1,0:T(8,128)(2,1)}, bf16[72,1408]{1,0:T(8,128)(2,1)}, u32[]{:S(2)}, u32[]{:S(2)}) collective-permute-start(bf16[72,1408]{1,0:T(8,128)(2,1)} %broadcast_select_fusion.4), channel_id=1, source_target_pairs={{7,2},{0,3},{15,10},{8,11},{23,18},{16,19},{31,26},{24,27},{39,34}... | collective-permute-start | bytes 608264 | tf_op jit(solution)/shard_map/ppermute | solution.py:250
  249.7 10.8 %all-to-all-start.1 = ((bf16[4,32,2,1,1408]{4,2,0,3,1:T(2,128)(2,1)}), bf16[4,32,2,1,1408]{4,2,0,3,1:T(2,128)(2,1)S(1)}, u32[]{:S(2)}, u32[]{:S(2)}) async-start(bf16[4,32,2,1,1408]{4,2,0,3,1:T(2,128)(2,1)} %copy.24), calls=%async_computation.1 | async-start | bytes 1441792 | tf_op jit(solution)/shard_map/all_to_all | solution.py:185
  260.4 6.2 %collective-permute-start.29 = (bf16[72,1408]{1,0:T(8,128)(2,1)}, bf16[72,1408]{1,0:T(8,128)(2,1)S(1)}, u32[]{:S(2)}, u32[]{:S(2)}) collective-permute-start(bf16[72,1408]{1,0:T(8,128)(2,1)} %broadcast_select_fusion.3), channel_id=1, source_target_pairs={{7,3},{0,4},{15,11},{8,12},{23,19},{16,20},{31,27},{24,28},{39,35}... | collective-permute-start | bytes 608264 | tf_op jit(solution)/shard_map/ppermute | solution.py:250
  266.7 4.4 %copy-done.3 = bf16[4224,1408]{1,0:T(8,128)(2,1)S(1)} copy-done((bf16[4224,1408]{1,0:T(8,128)(2,1)S(1)}, bf16[4224,1408]{1,0:T(8,128)(2,1)}, u32[]{:S(2)}) %copy-start.3) | copy-done | bytes 11894808
  274.0 11.9 %collective-permute-start.31 = (bf16[72,1408]{1,0:T(8,128)(2,1)S(1)}, bf16[72,1408]{1,0:T(8,128)(2,1)S(1)}, u32[]{:S(2)}, u32[]{:S(2)}) collective-permute-start(bf16[72,1408]{1,0:T(8,128)(2,1)S(1)} %broadcast_select_fusion.1), channel_id=1, source_target_pairs={{7,5},{0,6},{15,13},{8,14},{23,21},{16,22},{31,29},{24,30},{39,37}... | collective-permute-start | bytes 608264 | tf_op jit(solution)/shard_map/ppermute | solution.py:250
  285.9 2.5 collective-permute-start.30
  289.0 5.6 %collective-permute-start.32 = (bf16[72,1408]{1,0:T(8,128)(2,1)S(1)}, bf16[72,1408]{1,0:T(8,128)(2,1)S(1)}, u32[]{:S(2)}, u32[]{:S(2)}) collective-permute-start(bf16[72,1408]{1,0:T(8,128)(2,1)S(1)} %broadcast_select_fusion), channel_id=1, source_target_pairs={{7,6},{0,7},{15,14},{8,15},{23,22},{16,23},{31,30},{24,31},{39,38}... | collective-permute-start | bytes 608264 | tf_op jit(solution)/shard_map/ppermute | solution.py:250
  300.1 10.2 %all-to-all-start.2 = ((bf16[32,2,1,1408]{3,1,2,0:T(2,128)(2,1)}), bf16[32,2,1,1408]{3,1,2,0:T(2,128)(2,1)S(1)}, u32[]{:S(2)}, u32[]{:S(2)}) async-start(bf16[32,2,1,1408]{3,1,2,0:T(2,128)(2,1)} %bitcast.59), calls=%async_computation.2 | async-start | bytes 360448 | tf_op jit(solution)/shard_map/all_to_all | solution.py:185
  312.3 6.2 %reshape.116 = bf16[1408,1408]{1,0:T(8,128)(2,1)} reshape(bf16[64,22,1408]{2,1,0:T(8,128)(2,1)} %all-gather.8.cloned.1.call-done) | data formatting | bytes 7929856 | tf_op jit(solution)/shard_map/reshape | solution.py:258
  321.6 6.6 %all-to-all-start.3 = ((bf16[4,32,2,1,1408]{4,0,2,3,1:T(4,128)(2,1)}), bf16[4,32,2,1,1408]{4,0,2,3,1:T(4,128)(2,1)S(1)}, u32[]{:S(2)}, u32[]{:S(2)}) async-start(bf16[4,32,2,1,1408]{4,0,2,3,1:T(4,128)(2,1)} %bitcast.71), calls=%async_computation.3 | async-start | bytes 1441792 | tf_op jit(solution)/shard_map/all_to_all | solution.py:185
  331.7 2.1 collective-permute-start.33
  333.8 2.8 convolution_convert_fusion
  337.6 6.0 %collective-permute-start.38 = (bf16[16,1408]{1,0:T(8,128)(2,1)S(1)}, bf16[16,1408]{1,0:T(8,128)(2,1)S(1)}, u32[]{:S(2)}, u32[]{:S(2)}) collective-permute-start(bf16[16,1408]{1,0:T(8,128)(2,1)S(1)} %get-tuple-element.202), channel_id=1, source_target_pairs={{0,24},{8,32},{16,40},{24,48},{32,56},{40,64},{48,72},{56,80},{64,... | collective-permute-start | bytes 135176 | tf_op jit(solution)/shard_map/ppermute | solution.py:14
  343.5 3.4 collective-permute-start.37
  350.9 3.5 fusion.46
  (164 shorter events, 54.7 us)
Async XLA Ops:
  7.2 105.9 %all-gather.6.cloned.1.call-start = ((), (), s32[]{:S(2)}) async-start(), calls=%async_computation.4 | async-start | bytes 6893568 | tf_op jit(solution)/shard_map/all_gather | solution.py:41
  8.3 9.7 %collective-permute-start = (bf16[66,768]{1,0:T(8,128)(2,1)S(1)}, bf16[66,768]{1,0:T(8,128)(2,1)S(1)}, u32[]{:S(2)}, u32[]{:S(2)}) collective-permute-start(bf16[66,768]{1,0:T(8,128)(2,1)S(1)} %get-tuple-element.200), channel_id=1, source_target_pairs={{0,8},{8,0},{16,24},{24,16},{32,40},{40,32},{48,56},{56,48},{64,72... | collective-permute-start | bytes 304136 | tf_op jit(solution)/shard_map/ppermute | solution.py:22
  19.7 13.8 %all-to-all-start = ((bf16[1,2,32,1408]{3,1,0,2:T(2,128)(2,1)}), bf16[1,2,32,1408]{3,1,0,2:T(2,128)(2,1)S(1)}, u32[]{:S(2)}, u32[]{:S(2)}) async-start(bf16[1,2,32,1408]{3,1,0,2:T(2,128)(2,1)} %copy.23), calls=%async_computation | async-start | bytes 360448 | tf_op jit(solution)/shard_map/all_to_all | solution.py:178
  23.6 275.8 %all-gather.8.cloned.1.call-start = ((), (), s32[]{:S(2)}) async-start(), calls=%async_computation.5 | async-start | bytes 4392960 | tf_op jit(solution)/shard_map/all_gather | solution.py:213
  33.6 6.1 %collective-permute-start.1 = (bf16[8,1408]{1,0:T(8,128)(2,1)S(1)}, bf16[8,1408]{1,0:T(8,128)(2,1)S(1)}, u32[]{:S(2)}, u32[]{:S(2)}) collective-permute-start(bf16[8,1408]{1,0:T(8,128)(2,1)S(1)} %select_n.154), channel_id=1, source_target_pairs={{0,256},{8,264},{16,272},{24,280},{32,288},{40,296},{48,304},{56,3... | collective-permute-start | bytes 67592 | tf_op jit(solution)/shard_map/ppermute | solution.py:193
  39.7 6.9 %collective-permute-start.2 = (bf16[1,72,1408]{2,1,0:T(8,128)(2,1)S(1)}, bf16[1,72,1408]{2,1,0:T(8,128)(2,1)S(1)}, u32[]{:S(2)}, u32[]{:S(2)}) collective-permute-start(bf16[1,72,1408]{2,1,0:T(8,128)(2,1)S(1)} %maximum_select_fusion.2), channel_id=1, source_target_pairs={{1,0},{3,2},{5,4},{7,6},{9,8},{11,10},{13,12},{15,14},{17,16},{19,... | collective-permute-start | bytes 608264 | tf_op jit(solution)/shard_map/ppermute | solution.py:206
  46.6 10.0 %collective-permute-start.3 = (bf16[2,72,1408]{2,1,0:T(8,128)(2,1)S(1)}, bf16[2,72,1408]{2,1,0:T(8,128)(2,1)S(1)}, u32[]{:S(2)}, u32[]{:S(2)}) collective-permute-start(bf16[2,72,1408]{2,1,0:T(8,128)(2,1)S(1)} %pad_maximum_fusion.1), channel_id=1, source_target_pairs={{2,0},{6,4},{10,8},{14,12},{18,16},{22,20},{26,24},{30,28},{34,32}... | collective-permute-start | bytes 1216520 | tf_op jit(solution)/shard_map/ppermute | solution.py:206
  57.6 23.3 %collective-permute-start.4 = (bf16[4,72,1408]{2,1,0:T(8,128)(2,1)}, bf16[4,72,1408]{2,1,0:T(8,128)(2,1)S(1)}, u32[]{:S(2)}, u32[]{:S(2)}) collective-permute-start(bf16[4,72,1408]{2,1,0:T(8,128)(2,1)} %pad_maximum_fusion), channel_id=1, source_target_pairs={{4,0},{12,8},{20,16},{28,24},{36,32},{44,40},{52,48},{60,56},{68,6... | collective-permute-start | bytes 2433032 | tf_op jit(solution)/shard_map/ppermute | solution.py:206
  81.0 43.7 %copy-start.7 = (s32[1,1,64]{2,1,0:T(1,128)S(1)}, s32[1,1,64]{2,1,0:T(1,128)}, u32[]{:S(2)}) copy-start(s32[1,1,64]{2,1,0:T(1,128)} %param.17) | copy-start | bytes 772
  81.0 43.7 %copy-start.10 = (f32[1,1,64]{2,1,0:T(1,128)S(1)}, f32[1,1,64]{2,1,0:T(1,128)}, u32[]{:S(2)}) copy-start(f32[1,1,64]{2,1,0:T(1,128)} %param.19) | copy-start | bytes 772
  121.4 13.3 %collective-permute-start.5 = (bf16[4224,768]{1,0:T(8,128)(2,1)}, bf16[4224,768]{1,0:T(8,128)(2,1)}, u32[]{:S(2)}, u32[]{:S(2)}) collective-permute-start(bf16[4224,768]{1,0:T(8,128)(2,1)} %reshape.137.mine_ref), channel_id=1, source_target_pairs={{0,8},{8,0},{16,24},{24,16},{32,40},{40,32},{48,56},{56,48},{64,72... | collective-permute-start | bytes 19464200 | tf_op jit(solution)/shard_map/ppermute | solution.py:22
  139.3 105.3 %copy-start.2 = (bf16[4224,1408]{1,0:T(8,128)(2,1)}, bf16[4224,1408]{1,0:T(8,128)(2,1)S(1)}, u32[]{:S(2)}) copy-start(bf16[4224,1408]{1,0:T(8,128)(2,1)S(1)} %shard_map.104.weights_ref) | copy-start | bytes 35684356
  143.2 6.6 %collective-permute-start.6 = (bf16[72,1408]{1,0:T(8,128)(2,1)S(1)}, bf16[72,1408]{1,0:T(8,128)(2,1)S(1)}, u32[]{:S(2)}, u32[]{:S(2)}) collective-permute-start(bf16[72,1408]{1,0:T(8,128)(2,1)S(1)} %get-tuple-element.91), channel_id=1, source_target_pairs={{0,1},{1,2},{2,3},{3,4},{4,5},{5,6},{6,7},{8,9},{9,10},{10,11},{11... | collective-permute-start | bytes 608264 | tf_op jit(solution)/shard_map/ppermute | solution.py:244
  148.5 8.6 %collective-permute-start.8 = (bf16[72,1408]{1,0:T(8,128)(2,1)S(1)}, bf16[72,1408]{1,0:T(8,128)(2,1)S(1)}, u32[]{:S(2)}, u32[]{:S(2)}) collective-permute-start(bf16[72,1408]{1,0:T(8,128)(2,1)S(1)} %get-tuple-element.94), channel_id=1, source_target_pairs={{0,1},{1,2},{2,3},{3,4},{4,5},{5,6},{6,7},{8,9},{9,10},{10,11},{11... | collective-permute-start | bytes 608264 | tf_op jit(solution)/shard_map/ppermute | solution.py:244
  153.8 9.2 %collective-permute-start.7 = (bf16[72,1408]{1,0:T(8,128)(2,1)S(1)}, bf16[72,1408]{1,0:T(8,128)(2,1)S(1)}, u32[]{:S(2)}, u32[]{:S(2)}) collective-permute-start(bf16[72,1408]{1,0:T(8,128)(2,1)S(1)} %get-tuple-element.97), channel_id=1, source_target_pairs={{0,1},{1,2},{2,3},{3,4},{4,5},{5,6},{6,7},{8,9},{9,10},{10,11},{11... | collective-permute-start | bytes 608264 | tf_op jit(solution)/shard_map/ppermute | solution.py:244
  161.0 7.9 %collective-permute-start.10 = (bf16[72,1408]{1,0:T(8,128)(2,1)S(1)}, bf16[72,1408]{1,0:T(8,128)(2,1)S(1)}, u32[]{:S(2)}, u32[]{:S(2)}) collective-permute-start(bf16[72,1408]{1,0:T(8,128)(2,1)S(1)} %get-tuple-element.100), channel_id=1, source_target_pairs={{0,1},{1,2},{2,3},{3,4},{4,5},{5,6},{6,7},{8,9},{9,10},{10,11},{11... | collective-permute-start | bytes 608264 | tf_op jit(solution)/shard_map/ppermute | solution.py:244
  167.0 8.2 %collective-permute-start.9 = (bf16[72,1408]{1,0:T(8,128)(2,1)S(1)}, bf16[72,1408]{1,0:T(8,128)(2,1)S(1)}, u32[]{:S(2)}, u32[]{:S(2)}) collective-permute-start(bf16[72,1408]{1,0:T(8,128)(2,1)S(1)} %get-tuple-element.103), channel_id=1, source_target_pairs={{0,1},{1,2},{2,3},{3,4},{4,5},{5,6},{6,7},{8,9},{9,10},{10,11},{11... | collective-permute-start | bytes 608264 | tf_op jit(solution)/shard_map/ppermute | solution.py:244
  172.8 8.2 %collective-permute-start.12 = (bf16[72,1408]{1,0:T(8,128)(2,1)S(1)}, bf16[72,1408]{1,0:T(8,128)(2,1)S(1)}, u32[]{:S(2)}, u32[]{:S(2)}) collective-permute-start(bf16[72,1408]{1,0:T(8,128)(2,1)S(1)} %get-tuple-element.106), channel_id=1, source_target_pairs={{0,1},{1,2},{2,3},{3,4},{4,5},{5,6},{6,7},{8,9},{9,10},{10,11},{11... | collective-permute-start | bytes 608264 | tf_op jit(solution)/shard_map/ppermute | solution.py:244
  179.1 7.9 %collective-permute-start.11 = (bf16[72,1408]{1,0:T(8,128)(2,1)S(1)}, bf16[72,1408]{1,0:T(8,128)(2,1)S(1)}, u32[]{:S(2)}, u32[]{:S(2)}) collective-permute-start(bf16[72,1408]{1,0:T(8,128)(2,1)S(1)} %get-tuple-element.109), channel_id=1, source_target_pairs={{0,1},{1,2},{2,3},{3,4},{4,5},{5,6},{6,7},{8,9},{9,10},{10,11},{11... | collective-permute-start | bytes 608264 | tf_op jit(solution)/shard_map/ppermute | solution.py:244
  184.9 8.1 %collective-permute-start.14 = (bf16[72,1408]{1,0:T(8,128)(2,1)S(1)}, bf16[72,1408]{1,0:T(8,128)(2,1)S(1)}, u32[]{:S(2)}, u32[]{:S(2)}) collective-permute-start(bf16[72,1408]{1,0:T(8,128)(2,1)S(1)} %get-tuple-element.112), channel_id=1, source_target_pairs={{0,1},{1,2},{2,3},{3,4},{4,5},{5,6},{6,7},{8,9},{9,10},{10,11},{11... | collective-permute-start | bytes 608264 | tf_op jit(solution)/shard_map/ppermute | solution.py:244
  187.7 11.2 %collective-permute-start.13 = (bf16[72,1408]{1,0:T(8,128)(2,1)S(1)}, bf16[72,1408]{1,0:T(8,128)(2,1)S(1)}, u32[]{:S(2)}, u32[]{:S(2)}) collective-permute-start(bf16[72,1408]{1,0:T(8,128)(2,1)S(1)} %get-tuple-element.114), channel_id=1, source_target_pairs={{0,1},{1,2},{2,3},{3,4},{4,5},{5,6},{6,7},{8,9},{9,10},{10,11},{11... | collective-permute-start | bytes 608264 | tf_op jit(solution)/shard_map/ppermute | solution.py:244
  193.6 7.9 %collective-permute-start.16 = (bf16[72,1408]{1,0:T(8,128)(2,1)S(1)}, bf16[72,1408]{1,0:T(8,128)(2,1)S(1)}, u32[]{:S(2)}, u32[]{:S(2)}) collective-permute-start(bf16[72,1408]{1,0:T(8,128)(2,1)S(1)} %get-tuple-element.116), channel_id=1, source_target_pairs={{0,1},{1,2},{2,3},{3,4},{4,5},{5,6},{6,7},{8,9},{9,10},{10,11},{11... | collective-permute-start | bytes 608264 | tf_op jit(solution)/shard_map/ppermute | solution.py:244
  199.6 7.9 %collective-permute-start.15 = (bf16[72,1408]{1,0:T(8,128)(2,1)S(1)}, bf16[72,1408]{1,0:T(8,128)(2,1)S(1)}, u32[]{:S(2)}, u32[]{:S(2)}) collective-permute-start(bf16[72,1408]{1,0:T(8,128)(2,1)S(1)} %get-tuple-element.118), channel_id=1, source_target_pairs={{0,1},{1,2},{2,3},{3,4},{4,5},{5,6},{6,7},{8,9},{9,10},{10,11},{11... | collective-permute-start | bytes 608264 | tf_op jit(solution)/shard_map/ppermute | solution.py:244
  202.1 8.4 %collective-permute-start.18 = (bf16[72,1408]{1,0:T(8,128)(2,1)S(1)}, bf16[72,1408]{1,0:T(8,128)(2,1)S(1)}, u32[]{:S(2)}, u32[]{:S(2)}) collective-permute-start(bf16[72,1408]{1,0:T(8,128)(2,1)S(1)} %get-tuple-element.120), channel_id=1, source_target_pairs={{0,1},{1,2},{2,3},{3,4},{4,5},{5,6},{6,7},{8,9},{9,10},{10,11},{11... | collective-permute-start | bytes 608264 | tf_op jit(solution)/shard_map/ppermute | solution.py:244
  208.1 3.8 %collective-permute-start.17 = (bf16[72,1408]{1,0:T(8,128)(2,1)S(1)}, bf16[72,1408]{1,0:T(8,128)(2,1)S(1)}, u32[]{:S(2)}, u32[]{:S(2)}) collective-permute-start(bf16[72,1408]{1,0:T(8,128)(2,1)S(1)} %get-tuple-element.122), channel_id=1, source_target_pairs={{3,4},{4,5},{5,6},{6,7},{11,12},{12,13},{13,14},{14,15},{19,20},{2... | collective-permute-start | bytes 608264 | tf_op jit(solution)/shard_map/ppermute | solution.py:244
  211.1 2.1 collective-permute-start.20
  212.5 11.9 %collective-permute-start.22 = (bf16[72,1408]{1,0:T(8,128)(2,1)S(1)}, bf16[72,1408]{1,0:T(8,128)(2,1)S(1)}, u32[]{:S(2)}, u32[]{:S(2)}) collective-permute-start(bf16[72,1408]{1,0:T(8,128)(2,1)S(1)} %get-tuple-element.126), channel_id=1, source_target_pairs={{3,4},{4,5},{5,6},{6,7},{11,12},{12,13},{13,14},{14,15},{19,20},{2... | collective-permute-start | bytes 608264 | tf_op jit(solution)/shard_map/ppermute | solution.py:244
  213.9 58.6 %collective-permute-start.19 = (bf16[72,1408]{1,0:T(8,128)(2,1)}, bf16[72,1408]{1,0:T(8,128)(2,1)}, u32[]{:S(2)}, u32[]{:S(2)}) collective-permute-start(bf16[72,1408]{1,0:T(8,128)(2,1)} %broadcast_select_fusion.6), channel_id=1, source_target_pairs={{7,0},{0,1},{15,8},{8,9},{23,16},{16,17},{31,24},{24,25},{39,32},{... | collective-permute-start | bytes 608264 | tf_op jit(solution)/shard_map/ppermute | solution.py:250
  219.3 25.3 %collective-permute-start.21 = (bf16[72,1408]{1,0:T(8,128)(2,1)S(1)}, bf16[72,1408]{1,0:T(8,128)(2,1)S(1)}, u32[]{:S(2)}, u32[]{:S(2)}) collective-permute-start(bf16[72,1408]{1,0:T(8,128)(2,1)S(1)} %get-tuple-element.128), channel_id=1, source_target_pairs={{3,4},{4,5},{5,6},{6,7},{11,12},{12,13},{13,14},{14,15},{19,20},{2... | collective-permute-start | bytes 608264 | tf_op jit(solution)/shard_map/ppermute | solution.py:244
  220.6 65.2 %collective-permute-start.25 = (bf16[72,1408]{1,0:T(8,128)(2,1)}, bf16[72,1408]{1,0:T(8,128)(2,1)}, u32[]{:S(2)}, u32[]{:S(2)}) collective-permute-start(bf16[72,1408]{1,0:T(8,128)(2,1)} %broadcast_select_fusion.5), channel_id=1, source_target_pairs={{7,1},{0,2},{15,9},{8,10},{23,17},{16,18},{31,25},{24,26},{39,33},... | collective-permute-start | bytes 608264 | tf_op jit(solution)/shard_map/ppermute | solution.py:250
  225.7 34.8 %collective-permute-start.24 = (bf16[72,1408]{1,0:T(8,128)(2,1)S(1)}, bf16[72,1408]{1,0:T(8,128)(2,1)S(1)}, u32[]{:S(2)}, u32[]{:S(2)}) collective-permute-start(bf16[72,1408]{1,0:T(8,128)(2,1)S(1)} %get-tuple-element.130), channel_id=1, source_target_pairs={{3,4},{4,5},{5,6},{6,7},{11,12},{12,13},{13,14},{14,15},{19,20},{2... | collective-permute-start | bytes 608264 | tf_op jit(solution)/shard_map/ppermute | solution.py:244
  226.3 69.0 %collective-permute-start.27 = (bf16[72,1408]{1,0:T(8,128)(2,1)}, bf16[72,1408]{1,0:T(8,128)(2,1)}, u32[]{:S(2)}, u32[]{:S(2)}) collective-permute-start(bf16[72,1408]{1,0:T(8,128)(2,1)} %broadcast_select_fusion.4), channel_id=1, source_target_pairs={{7,2},{0,3},{15,10},{8,11},{23,18},{16,19},{31,26},{24,27},{39,34}... | collective-permute-start | bytes 608264 | tf_op jit(solution)/shard_map/ppermute | solution.py:250
  245.2 26.5 %collective-permute-start.23 = (bf16[72,1408]{1,0:T(8,128)(2,1)S(1)}, bf16[72,1408]{1,0:T(8,128)(2,1)S(1)}, u32[]{:S(2)}, u32[]{:S(2)}) collective-permute-start(bf16[72,1408]{1,0:T(8,128)(2,1)S(1)} %get-tuple-element.132), channel_id=1, source_target_pairs={{3,4},{4,5},{5,6},{6,7},{11,12},{12,13},{13,14},{14,15},{19,20},{2... | collective-permute-start | bytes 608264 | tf_op jit(solution)/shard_map/ppermute | solution.py:244
  249.7 49.6 %all-to-all-start.1 = ((bf16[4,32,2,1,1408]{4,2,0,3,1:T(2,128)(2,1)}), bf16[4,32,2,1,1408]{4,2,0,3,1:T(2,128)(2,1)S(1)}, u32[]{:S(2)}, u32[]{:S(2)}) async-start(bf16[4,32,2,1,1408]{4,2,0,3,1:T(2,128)(2,1)} %copy.24), calls=%async_computation.1 | async-start | bytes 1441792 | tf_op jit(solution)/shard_map/all_to_all | solution.py:185
  260.4 35.5 %collective-permute-start.29 = (bf16[72,1408]{1,0:T(8,128)(2,1)}, bf16[72,1408]{1,0:T(8,128)(2,1)S(1)}, u32[]{:S(2)}, u32[]{:S(2)}) collective-permute-start(bf16[72,1408]{1,0:T(8,128)(2,1)} %broadcast_select_fusion.3), channel_id=1, source_target_pairs={{7,3},{0,4},{15,11},{8,12},{23,19},{16,20},{31,27},{24,28},{39,35}... | collective-permute-start | bytes 608264 | tf_op jit(solution)/shard_map/ppermute | solution.py:250
  271.7 2.3 collective-permute-start.26
  273.1 15.9 %collective-permute-start.28 = (bf16[72,1408]{1,0:T(8,128)(2,1)S(1)}, bf16[72,1408]{1,0:T(8,128)(2,1)S(1)}, u32[]{:S(2)}, u32[]{:S(2)}) collective-permute-start(bf16[72,1408]{1,0:T(8,128)(2,1)S(1)} %get-tuple-element.138), channel_id=1, source_target_pairs={{3,4},{4,5},{5,6},{6,7},{11,12},{12,13},{13,14},{14,15},{19,20},{2... | collective-permute-start | bytes 608264 | tf_op jit(solution)/shard_map/ppermute | solution.py:244
  274.0 22.0 %collective-permute-start.31 = (bf16[72,1408]{1,0:T(8,128)(2,1)S(1)}, bf16[72,1408]{1,0:T(8,128)(2,1)S(1)}, u32[]{:S(2)}, u32[]{:S(2)}) collective-permute-start(bf16[72,1408]{1,0:T(8,128)(2,1)S(1)} %broadcast_select_fusion.1), channel_id=1, source_target_pairs={{7,5},{0,6},{15,13},{8,14},{23,21},{16,22},{31,29},{24,30},{39,37}... | collective-permute-start | bytes 608264 | tf_op jit(solution)/shard_map/ppermute | solution.py:250
  285.9 10.1 %collective-permute-start.30 = (bf16[72,1408]{1,0:T(8,128)(2,1)S(1)}, bf16[72,1408]{1,0:T(8,128)(2,1)S(1)}, u32[]{:S(2)}, u32[]{:S(2)}) collective-permute-start(bf16[72,1408]{1,0:T(8,128)(2,1)S(1)} %broadcast_select_fusion.2), channel_id=1, source_target_pairs={{7,4},{0,5},{15,12},{8,13},{23,20},{16,21},{31,28},{24,29},{39,36}... | collective-permute-start | bytes 608264 | tf_op jit(solution)/shard_map/ppermute | solution.py:250
  289.0 8.5 %collective-permute-start.32 = (bf16[72,1408]{1,0:T(8,128)(2,1)S(1)}, bf16[72,1408]{1,0:T(8,128)(2,1)S(1)}, u32[]{:S(2)}, u32[]{:S(2)}) collective-permute-start(bf16[72,1408]{1,0:T(8,128)(2,1)S(1)} %broadcast_select_fusion), channel_id=1, source_target_pairs={{7,6},{0,7},{15,14},{8,15},{23,22},{16,23},{31,30},{24,31},{39,38}... | collective-permute-start | bytes 608264 | tf_op jit(solution)/shard_map/ppermute | solution.py:250
  300.1 20.1 %all-to-all-start.2 = ((bf16[32,2,1,1408]{3,1,2,0:T(2,128)(2,1)}), bf16[32,2,1,1408]{3,1,2,0:T(2,128)(2,1)S(1)}, u32[]{:S(2)}, u32[]{:S(2)}) async-start(bf16[32,2,1,1408]{3,1,2,0:T(2,128)(2,1)} %bitcast.59), calls=%async_computation.2 | async-start | bytes 360448 | tf_op jit(solution)/shard_map/all_to_all | solution.py:185
  321.6 33.8 %all-to-all-start.3 = ((bf16[4,32,2,1,1408]{4,0,2,3,1:T(4,128)(2,1)}), bf16[4,32,2,1,1408]{4,0,2,3,1:T(4,128)(2,1)S(1)}, u32[]{:S(2)}, u32[]{:S(2)}) async-start(bf16[4,32,2,1,1408]{4,0,2,3,1:T(4,128)(2,1)} %bitcast.71), calls=%async_computation.3 | async-start | bytes 1441792 | tf_op jit(solution)/shard_map/all_to_all | solution.py:185
  329.1 19.5 %collective-permute-start.35 = (bf16[16,1408]{1,0:T(8,128)(2,1)S(1)}, bf16[16,1408]{1,0:T(8,128)(2,1)S(1)}, u32[]{:S(2)}, u32[]{:S(2)}) collective-permute-start(bf16[16,1408]{1,0:T(8,128)(2,1)S(1)} %get-tuple-element.206), channel_id=1, source_target_pairs={{24,0},{32,8},{40,16},{48,24},{56,32},{64,40},{72,48},{80,56},{88,... | collective-permute-start | bytes 135176 | tf_op jit(solution)/shard_map/ppermute | solution.py:14
  330.4 20.1 %collective-permute-start.34 = (bf16[16,1408]{1,0:T(8,128)(2,1)S(1)}, bf16[16,1408]{1,0:T(8,128)(2,1)S(1)}, u32[]{:S(2)}, u32[]{:S(2)}) collective-permute-start(bf16[16,1408]{1,0:T(8,128)(2,1)S(1)} %get-tuple-element.207), channel_id=1, source_target_pairs={{16,0},{24,8},{32,16},{40,24},{48,32},{56,40},{64,48},{72,56},{80,... | collective-permute-start | bytes 135176 | tf_op jit(solution)/shard_map/ppermute | solution.py:14
  331.7 18.8 %collective-permute-start.33 = (bf16[16,1408]{1,0:T(8,128)(2,1)S(1)}, bf16[16,1408]{1,0:T(8,128)(2,1)S(1)}, u32[]{:S(2)}, u32[]{:S(2)}) collective-permute-start(bf16[16,1408]{1,0:T(8,128)(2,1)S(1)} %get-tuple-element.208), channel_id=1, source_target_pairs={{8,0},{16,8},{24,16},{32,24},{40,32},{48,40},{56,48},{64,56},{72,6... | collective-permute-start | bytes 135176 | tf_op jit(solution)/shard_map/ppermute | solution.py:14
  337.6 16.9 %collective-permute-start.38 = (bf16[16,1408]{1,0:T(8,128)(2,1)S(1)}, bf16[16,1408]{1,0:T(8,128)(2,1)S(1)}, u32[]{:S(2)}, u32[]{:S(2)}) collective-permute-start(bf16[16,1408]{1,0:T(8,128)(2,1)S(1)} %get-tuple-element.202), channel_id=1, source_target_pairs={{0,24},{8,32},{16,40},{24,48},{32,56},{40,64},{48,72},{56,80},{64,... | collective-permute-start | bytes 135176 | tf_op jit(solution)/shard_map/ppermute | solution.py:14
  343.5 10.9 %collective-permute-start.37 = (bf16[16,1408]{1,0:T(8,128)(2,1)S(1)}, bf16[16,1408]{1,0:T(8,128)(2,1)S(1)}, u32[]{:S(2)}, u32[]{:S(2)}) collective-permute-start(bf16[16,1408]{1,0:T(8,128)(2,1)S(1)} %get-tuple-element.203), channel_id=1, source_target_pairs={{0,16},{8,24},{16,32},{24,40},{32,48},{40,56},{48,64},{56,72},{64,... | collective-permute-start | bytes 135176 | tf_op jit(solution)/shard_map/ppermute | solution.py:14
  348.5 5.9 %collective-permute-start.36 = (bf16[16,1408]{1,0:T(8,128)(2,1)S(1)}, bf16[16,1408]{1,0:T(8,128)(2,1)S(1)}, u32[]{:S(2)}, u32[]{:S(2)}) collective-permute-start(bf16[16,1408]{1,0:T(8,128)(2,1)S(1)} %get-tuple-element.204), channel_id=1, source_target_pairs={{0,8},{8,16},{16,24},{24,32},{32,40},{40,48},{48,56},{56,64},{64,7... | collective-permute-start | bytes 135176 | tf_op jit(solution)/shard_map/ppermute | solution.py:14
  (11 other events, 170.3 us)
Sparse Core Ops, SparseCore 0:
  18.9 94.1 all-gather.5
  125.0 82.0 all-gather.7
